TPU v7x, 1024 devices: a whole 8x8x8 slice. The times are simulated.
1024 devices in a mesh: ctx: 64 (over x, z), exp: 16 (over y, core).
Axes of the slice: x: 8, y: 8, z: 8, core: 2. Of those that a mesh axis runs over, the one named last changes fastest.
Arguments:
- layer_input: bfloat16 [16, 8192, 3072], P('exp', 'ctx'), may hold values from -6 to 6
- expert_ids: int32 [16, 8192, 2], P('exp', 'ctx'), may hold values from 0 to 15, as said below
- router_probs: float32 [16, 8192, 16], P('exp', 'ctx'), may hold values from 0 to 1, as said below
- router_weight: bfloat16 [16, 3072], replicated, may hold values from -1.5 to 1.5
- expert_grads: bfloat16 [64, 16, 320, 3072], P('ctx', 'exp'), may hold values from -6 to 6
- gate_dots: bfloat16 [64, 16, 320], P('ctx', 'exp'), may hold values from -12 to 12
Outputs:
- moe_input_grad: bfloat16 [16, 8192, 3072], P('exp', 'ctx')
- router_weight_grad: float32 [16, 3072], P('exp')
Inputs may be any that keep to these rules, and one draw needn't show every extreme that they name: `expert_ids`: in each aligned block of 128 rows of a window (the rows of one device) every expert is named at least once and at most 20 times, and some expert exactly 20 times; a row names 2 different experts. `router_probs`: each row is positive and sums to one; the experts that expert_ids names in a row hold that row's largest probabilities.
All inputs are finite; a program needn't handle non-finite values.
Results may differ from a plain program's by a relative error of at most 0.0033.
Values may be sent and summed in bfloat16 or wider, within the bound.
No kernel may reach another device: no remote copies, remote signals or barrier semaphores. Data moves between devices by JAX's collectives and lax.ppermute only.
A program may use at most 32 MiB of HBM per device.

v0:
```python
import jax
import jax.numpy as jnp
from jax import lax
from jax.sharding import PartitionSpec as P


def shards(layer_input, expert_ids, router_probs, router_weight, expert_grads, gate_dots):
    returned, dot_values = (
        lax.all_to_all(expert_grads, "exp", split_axis=2, concat_axis=1, tiled=True),
        lax.all_to_all(gate_dots, "exp", split_axis=2, concat_axis=1, tiled=True),
    )
    slot_cap = returned.shape[2]
    experts = returned.shape[1]
    width = returned.shape[3]
    copy_table = returned.reshape(experts * slot_cap, width)
    dot_column = dot_values.reshape(experts * slot_cap)
    choice_ids = expert_ids[0]
    row_count = choice_ids.shape[0]
    top_count = choice_ids.shape[1]
    flat_choice = choice_ids.reshape(row_count * top_count)
    onehot = (flat_choice[:, None] == jnp.arange(experts, dtype=jnp.int32)[None, :]).astype(
        jnp.int32
    )
    prior_count = jnp.cumsum(onehot, axis=0) - onehot
    slot_number = jnp.sum(prior_count * onehot, axis=1)
    slot_index = flat_choice * slot_cap + slot_number
    copy_rows = (
        jnp.take(copy_table, slot_index, axis=0)
        .astype(jnp.float32)
        .reshape(row_count, top_count, width)
    )
    gate_grad = jnp.take(dot_column.astype(jnp.float32), slot_index, axis=0).reshape(
        row_count, top_count
    )
    prob_rows = router_probs[0]
    choice_mask = (choice_ids[..., None] == jnp.arange(experts, dtype=jnp.int32)).astype(
        jnp.float32
    )
    picked = jnp.sum(choice_mask * prob_rows[:, None, :], axis=-1)
    exp_total = jnp.sum(picked, axis=1, keepdims=True)
    gate_value = picked / exp_total
    pick_grad = gate_grad / exp_total - jnp.sum(gate_grad * picked, axis=1, keepdims=True) / (
        exp_total * exp_total
    )
    router_grad = jnp.sum(choice_mask * pick_grad[..., None], axis=1)
    logit_grad = (
        prob_rows * (router_grad - jnp.sum(prob_rows * router_grad, axis=1, keepdims=True))
    ).astype(jnp.bfloat16)
    router_term = jnp.dot(logit_grad, router_weight, preferred_element_type=jnp.float32)
    combined = jnp.sum(gate_value[..., None] * copy_rows, axis=1) + router_term
    moe_input_grad = combined.astype(jnp.bfloat16).reshape(1, row_count, width)
    weight_term = lax.dot_general(
        logit_grad, layer_input[0], (((0,), (0,)), ((), ())), preferred_element_type=jnp.float32
    )
    owned = experts // lax.axis_size("exp")
    summed = lax.psum(weight_term, ("ctx", "exp"))
    router_weight_grad = lax.dynamic_slice_in_dim(summed, lax.axis_index("exp") * owned, owned, 0)
    return (moe_input_grad, router_weight_grad)


def solution(mesh):
    in_specs = (
        P("exp", "ctx", None),
        P("exp", "ctx", None),
        P("exp", "ctx", None),
        P(),
        P("ctx", "exp", None, None),
        P("ctx", "exp", None),
    )
    out_specs = (P("exp", "ctx", None), P("exp", None))
    return jax.shard_map(shards, mesh=mesh, in_specs=in_specs, out_specs=out_specs, check_vma=False)
```

profile of v0, /device:TPU:1, one launch (start us, length us, event | category | flops | bytes accessed | tf_op | source)
XLA Modules:
  0.0 385.8 jit_solution(6001172415876137938)
XLA Ops:
  7.2 1.6 copy.43
  8.8 17.5 %all-to-all-start.1 = ((bf16[1,1,320]{1,0,2:T(2,128)(2,1)}), bf16[1,1,320]{1,0,2:T(2,128)(2,1)S(1)}, u32[]{:S(2)}, u32[]{:S(2)}) async-start(bf16[1,1,320]{1,0,2:T(2,128)(2,1)} %copy.43), calls=%async_computation.1 | async-start | bytes 327680 | tf_op jit(solution)/shard_map/all_to_all | solution.py:10
  26.2 6.5 %copy.51 = bf16[1,1,320,3072]{3,1,0,2:T(2,128)(2,1)} copy(bf16[1,1,320,3072]{3,2,1,0:T(8,128)(2,1)} %param.10) | data formatting | bytes 3932160 | tf_op args[4]
  32.7 0.5 broadcast.159
  33.2 12.9 %reduce.5 = bf16[320,3072]{1,0:T(8,128)(2,1)S(1)} reduce(bf16[320,1,1,3072]{3,2,1,0:T(2,128)(2,1)} %bitcast.56, bf16[]{:T(256)} %broadcast.159), dimensions={1,2}, to_apply=%bitcast.54.reduce_sub_computation | reduce | bytes 3932162
  46.1 2.3 reshape.210
  48.3 7.4 %all-to-all-start = ((bf16[16,2,30720]{2,1,0:T(2,128)(2,1)}), bf16[16,2,30720]{2,1,0:T(2,128)(2,1)S(1)}, u32[]{:S(2)}, u32[]{:S(2)}) async-start(bf16[16,2,30720]{2,1,0:T(2,128)(2,1)} %reshape.210), calls=%async_computation | async-start | bytes 3932160 | tf_op jit(solution)/shard_map/all_to_all | solution.py:9
  55.7 0.2 all-reduce.2.cloned.1.call-start
  56.2 0.1 eq.45
  56.6 0.6 reduce-window.6
  57.2 0.2 slice_reduce_fusion
  57.6 0.1 reduce_sum.72
  57.8 1.1 convert_reduce_fusion
  58.9 1.9 gather_fusion.1
  61.2 0.9 fusion.2
  62.1 0.1 copy.40
  62.4 291.3 %all-reduce.2.cloned.1.call-done = f32[16,3072]{1,0:T(8,128)} async-done(((f32[16,3072]{1,0:T(8,128)}), f32[16,3072]{1,0:T(8,128)}) %all-reduce.2.cloned.1.call-update) | async-done | bytes 196624 | tf_op jit(solution)/shard_map/psum | solution.py:56
  353.7 1.5 constant_dynamic-slice_fusion
  355.2 6.6 %reshape.211 = bf16[320,1,1,3072]{3,2,1,0:T(2,128)(2,1)} reshape(bf16[16,2,30720]{2,1,0:T(2,128)(2,1)S(1)} %all-to-all-done) | data formatting | bytes 3932160
  361.8 2.7 copy.50
  364.5 2.7 gather_fusion
  367.2 3.7 gather.13
  371.0 6.7 %multiply_reduce_fusion = f32[128,3072]{1,0:T(8,128)S(1)} fusion(bf16[128,2,3072]{2,1,0:T(2,128)(2,1)S(1)} %gather.13, pred[128,2]{1,0:T(8,128)(4,1)S(1)} %copy.40, f32[128,2]{1,0:T(8,128)S(1)} %copy.35), kind=kLoop, calls=%fused_computation.5 | loop fusion | flops 2752512 | bytes 3147008 | tf_op jit(solution)/shard_map/reduce_sum | solution.py:50
  377.7 1.3 fusion.1
  (32 shorter events, 1.2 us)
Async XLA Ops:
  7.2 54.0 %copy-start = (bf16[1,128,3072]{2,1,0:T(8,128)(2,1)S(1)}, bf16[1,128,3072]{2,1,0:T(8,128)(2,1)}, u32[]{:S(2)}) copy-start(bf16[1,128,3072]{2,1,0:T(8,128)(2,1)} %param.6) | copy-start | bytes 2359300
  8.8 39.6 %all-to-all-start.1 = ((bf16[1,1,320]{1,0,2:T(2,128)(2,1)}), bf16[1,1,320]{1,0,2:T(2,128)(2,1)S(1)}, u32[]{:S(2)}, u32[]{:S(2)}) async-start(bf16[1,1,320]{1,0,2:T(2,128)(2,1)} %copy.43), calls=%async_computation.1 | async-start | bytes 327680 | tf_op jit(solution)/shard_map/all_to_all | solution.py:10
  48.3 7.6 %copy-start.3 = (s32[1,128,2]{1,2,0:T(2,128)S(1)}, s32[1,128,2]{1,2,0:T(2,128)}, u32[]{:S(2)}) copy-start(s32[1,128,2]{1,2,0:T(2,128)} %param.7) | copy-start | bytes 3076
  48.3 9.5 %copy-start.1 = (f32[1,128,16]{1,2,0:T(8,128)S(1)}, f32[1,128,16]{1,2,0:T(8,128)}, u32[]{:S(2)}) copy-start(f32[1,128,16]{1,2,0:T(8,128)} %param.8) | copy-start | bytes 24580
  48.3 306.9 %all-to-all-start = ((bf16[16,2,30720]{2,1,0:T(2,128)(2,1)}), bf16[16,2,30720]{2,1,0:T(2,128)(2,1)S(1)}, u32[]{:S(2)}, u32[]{:S(2)}) async-start(bf16[16,2,30720]{2,1,0:T(2,128)(2,1)} %reshape.210), calls=%async_computation | async-start | bytes 3932160 | tf_op jit(solution)/shard_map/all_to_all | solution.py:9
  55.7 298.0 %all-reduce.2.cloned.1.call-start = ((), (), s32[]{:S(2)}) async-start(), calls=%async_computation.2 | async-start | bytes 393216 | tf_op jit(solution)/shard_map/psum | solution.py:56
  371.0 6.7 %copy-start.2 = (bf16[16,3072]{1,0:T(8,128)(2,1)S(1)}, bf16[16,3072]{1,0:T(8,128)(2,1)}, u32[]{:S(2)}) copy-start(bf16[16,3072]{1,0:T(8,128)(2,1)} %param.9) | copy-start | bytes 294916
Sparse Core Ops, SparseCore 0:
  62.2 291.4 all-reduce.1
where the time goes:
time: 386 us
  waiting for transfers between devices  291 us (75%)
  local copies, waits for them, and re-layouts  31.5 us (8%)
  starting transfers between devices  25.1 us (7%)
  other arithmetic  21.5 us (6%)
  between operations  14.2 us (4%)
    psum x1, waiting for transfers between devices, shards(): summed = lax.psum(weight_term, ('ctx', 'exp'))  291 us
    unnamed x15, local copies, waits for them, and re-layouts  20.3 us
    all_to_all x1, starting transfers between devices, shards(): lax.all_to_all(gate_dots, 'exp', split_axis=2, concat_axis=1, tiled=True)  17.5 us
    unnamed x1, other arithmetic  12.9 us
  transfers between devices with their start and end apart: 3, of which 1 were waited for; matrix products, arithmetic and copies ran while one was open for 8% of the time, Pallas kernels for 0%

commit v1 on v0

v1 whole, which is shorter than its diff:
```python
import jax
import jax.numpy as jnp
from jax import lax
from jax.experimental import pallas as pl
from jax.experimental.pallas import tpu as pltpu
from jax.sharding import PartitionSpec as P

QUARTERS = 4
LANES = 128
VMEM = 48 * 1024 * 1024


def dot_rows(left, right):
    return lax.dot_general(
        left, right, (((0,), (0,)), ((), ())), preferred_element_type=jnp.float32
    )


def gate_pack_kernel(cap, dots_ref, out_ref):
    windows, lanes = out_ref.shape[0], out_ref.shape[2]
    count = dots_ref.shape[1]
    column = lax.broadcasted_iota(jnp.int32, (windows, count), 1)
    first = lax.broadcasted_iota(jnp.int32, (windows, count), 0) * cap
    dots = jnp.broadcast_to(dots_ref[...].astype(jnp.float32), (windows, count))
    own = jnp.where((column >= first) & (column < first + cap), dots, 0.0)
    slot = lax.broadcasted_iota(jnp.int32, (count, lanes), 0) % cap
    lane = lax.broadcasted_iota(jnp.int32, (count, lanes), 1)
    place = jnp.where(slot == lane, 1.0, 0.0)
    laid = jnp.dot(
        own.astype(jnp.bfloat16), place.astype(jnp.bfloat16), preferred_element_type=jnp.float32
    )
    out_ref[...] = laid[:, None, :]


def pack_kernel(cap, rows_ref, out_ref):
    part = out_ref.shape[2]
    rows = rows_ref[...].astype(jnp.float32)
    for w in range(out_ref.shape[0]):
        window = rows[w * cap : (w + 1) * cap]
        stacked = jnp.concatenate(
            [window[:, q * part : (q + 1) * part] for q in range(QUARTERS)], axis=0
        )
        out_ref[w] = stacked.astype(jnp.bfloat16)


def router_kernel(ids_ref, probs_ref, dots_ref, input_ref, logit_ref, place_ref, term_ref):
    experts, tokens = probs_ref.shape
    probs = probs_ref[...]
    expert = lax.broadcasted_iota(jnp.int32, (experts, tokens), 0)
    chosen = [expert == ids_ref[k : k + 1, :] for k in range(2)]
    mask = jnp.where(chosen[0] | chosen[1], 1.0, 0.0)
    earlier = lax.broadcasted_iota(jnp.int32, (tokens, tokens), 0) < lax.broadcasted_iota(
        jnp.int32, (tokens, tokens), 1
    )
    prior = jnp.dot(
        mask.astype(jnp.bfloat16),
        jnp.where(earlier, 1.0, 0.0).astype(jnp.bfloat16),
        preferred_element_type=jnp.float32,
    )
    dots = dots_ref[...][:, 0, :].astype(jnp.bfloat16)
    lane_count = dots.shape[1]
    slot_row = lax.broadcasted_iota(jnp.int32, (lane_count, tokens), 0)
    picked, gate_grad, slots = [], [], []
    for k in range(2):
        onehot = jnp.where(chosen[k], 1.0, 0.0)
        picked.append(jnp.sum(jnp.where(chosen[k], probs, 0.0), axis=0, keepdims=True))
        slot = jnp.sum(onehot * prior, axis=0, keepdims=True).astype(jnp.int32)
        slots.append(slot)
        values = dot_rows(dots, onehot.astype(jnp.bfloat16))
        gate_grad.append(jnp.sum(jnp.where(slot_row == slot, values, 0.0), axis=0, keepdims=True))
    total = picked[0] + picked[1]
    shared = (gate_grad[0] * picked[0] + gate_grad[1] * picked[1]) / (total * total)
    router_grad = sum(
        jnp.where(chosen[k], gate_grad[k] / total - shared, 0.0) for k in range(2)
    )
    logit = probs * (router_grad - jnp.sum(probs * router_grad, axis=0, keepdims=True))
    logit = logit.astype(jnp.bfloat16)
    logit_ref[...] = logit
    place_ref[...] = jnp.concatenate(
        [picked[0] / total, picked[1] / total]
        + [s.astype(jnp.float32) for s in slots]
        + [jnp.zeros((4, tokens), jnp.float32)],
        axis=0,
    )
    term = jnp.dot(logit, input_ref[...], preferred_element_type=jnp.float32)
    term_ref[...] = term[:, None, :]


def combine_kernel(cap, ids_ref, place_ref, logit_ref, weight_ref, copies_ref, out_ref):
    experts, depth, part = copies_ref.shape
    tokens = ids_ref.shape[1]
    copies = copies_ref[...].reshape(experts * depth, part)
    row = lax.broadcasted_iota(jnp.int32, (experts * depth, tokens), 0)
    gates = [place_ref[k : k + 1, :] for k in range(2)]
    base = [
        ids_ref[k : k + 1, :] * depth + place_ref[2 + k : 3 + k, :].astype(jnp.int32)
        for k in range(2)
    ]
    for q in range(QUARTERS):
        spread = jnp.where(row == base[0] + q * cap, gates[0], 0.0) + jnp.where(
            row == base[1] + q * cap, gates[1], 0.0
        )
        high = spread.astype(jnp.bfloat16)
        low = (spread - high.astype(jnp.float32)).astype(jnp.bfloat16)
        columns = slice(q * part, (q + 1) * part)
        total = dot_rows(high, copies) + dot_rows(low, copies)
        total = total + dot_rows(logit_ref[...], weight_ref[:, columns])
        out_ref[:, columns] = total.astype(jnp.bfloat16)


def shards(side, layer_input, expert_ids, router_probs, router_weight, expert_grads, gate_dots):
    slots, width = expert_grads.shape[2:]
    tokens, experts = router_probs.shape[1:]
    windows = lax.axis_size("exp")
    cap = slots // windows
    part = width // QUARTERS
    depth = cap * QUARTERS
    params = pltpu.CompilerParams(vmem_limit_bytes=VMEM)

    laid = pl.pallas_call(
        lambda *refs: gate_pack_kernel(cap, *refs),
        out_shape=jax.ShapeDtypeStruct((windows, 1, LANES), jnp.float32),
        compiler_params=params,
    )(gate_dots[0])
    dots = lax.all_to_all(laid, "exp", 0, 0, tiled=True)

    packed = pl.pallas_call(
        lambda *refs: pack_kernel(cap, *refs),
        out_shape=jax.ShapeDtypeStruct((windows, depth, part), jnp.bfloat16),
        grid=(windows // 4,),
        in_specs=[pl.BlockSpec((4 * cap, width), lambda g: (g, 0))],
        out_specs=pl.BlockSpec((4, depth, part), lambda g: (g, 0, 0)),
        compiler_params=params,
    )(expert_grads[0, 0])
    copies = lax.all_to_all(packed, "exp", 0, 0, tiled=True)

    ids = jnp.swapaxes(expert_ids, 1, 2)[0]
    probs = jnp.swapaxes(router_probs, 1, 2)[0]
    logit, place, term = pl.pallas_call(
        router_kernel,
        out_shape=(
            jax.ShapeDtypeStruct((experts, tokens), jnp.bfloat16),
            jax.ShapeDtypeStruct((8, tokens), jnp.float32),
            jax.ShapeDtypeStruct((experts, 1, width), jnp.float32),
        ),
        compiler_params=params,
    )(ids, probs, dots, layer_input[0])

    own = jnp.sum(lax.all_to_all(term, "exp", 0, 0, tiled=True), axis=0)
    across = [[x * side + z for x in range(side)] for z in range(side)]
    along = [[x * side + z for z in range(side)] for x in range(side)]
    for groups in (across, along):
        copied = jnp.broadcast_to(own[None], (side,) + own.shape)
        own = jnp.sum(
            lax.all_to_all(copied, "ctx", 0, 0, axis_index_groups=groups, tiled=True), axis=0
        )

    combined = pl.pallas_call(
        lambda *refs: combine_kernel(cap, *refs),
        out_shape=jax.ShapeDtypeStruct((tokens, width), jnp.bfloat16),
        compiler_params=params,
    )(ids, place, logit, router_weight, copies)
    return combined[None], own


def solution(mesh):
    in_specs = (
        P("exp", "ctx", None),
        P("exp", "ctx", None),
        P("exp", "ctx", None),
        P(),
        P("ctx", "exp", None, None),
        P("ctx", "exp", None),
    )
    out_specs = (P("exp", "ctx", None), P("exp", None))
    side = round(mesh.shape["ctx"] ** 0.5)

    def step(*arrays):
        return shards(side, *arrays)

    return jax.shard_map(step, mesh=mesh, in_specs=in_specs, out_specs=out_specs, check_vma=False)
```

time: 386 us -> 130 us (0.34)
  waiting for transfers between devices: 291 us -> 51.7 us
  blocking collectives: 0 us -> 48.3 us
  local copies, waits for them, and re-layouts: 31.5 us -> 5.36 us
  other arithmetic: 21.5 us -> 0.88 us
  between operations: 14.2 us -> 0.7 us
  starting transfers between devices: 25.1 us -> 17.9 us
  Pallas kernels: 0 us -> 4.71 us
    psum x1 -> x0, waiting for transfers between devices: 291 us -> none  [shards(): summed = lax.psum(weight_term, ('ctx', 'exp'))]
    all_to_all x2, waiting for transfers between devices: 0.01 us -> 51.7 us  [the longest x1 45.7 us: shards(): copies = lax.all_to_all(packed, 'exp', 0, 0, tiled=True)]
    all_to_all x0 -> x3, blocking collectives: none -> 48.3 us  [the longest x1 23.6 us: shards(): dots = lax.all_to_all(laid, 'exp', 0, 0, tiled=True)]
    unnamed x15 -> x16, local copies, waits for them, and re-layouts: 20.3 us -> 4.62 us
    unnamed x1 -> x0, other arithmetic: 12.9 us -> none
    gather x5 -> x0, local copies, waits for them, and re-layouts: 8.57 us -> none  [the longest x2 6.44 us: shards(): jnp.take(copy_table, slot_index, axis=0).astype(jnp.float32)]
    all_to_all x2, starting transfers between devices: 24.9 us -> 17.9 us  [the longest x1 12.2 us: shards(): lax.all_to_all(copied, 'ctx', 0, 0, axis_index_groups=groups, tiled=True)]
    reduce_sum x6 -> x3, other arithmetic: 6.85 us -> 0.88 us  [the longest x2 0.75 us: shards(): jnp.sum(lax.all_to_all(copied, 'ctx', 0, 0, axis_index_groups=groups, til...]
  transfers between devices with their start and end apart: 3 -> 2, of which waited for: 1 -> 2; matrix products, arithmetic and copies ran while one was open for 8% -> 1% of each run, Pallas kernels for 0% -> 0%
where the time goes in v1:
time: 130 us; the launch traced here: 129 us
  waiting for transfers between devices  51.7 us (40%)
  blocking collectives  48.3 us (37%)
  starting transfers between devices  17.9 us (14%)
  local copies, waits for them, and re-layouts  5.36 us (4%)
  Pallas kernels  4.71 us (4%)
    all_to_all x1, waiting for transfers between devices, shards(): copies = lax.all_to_all(packed, 'exp', 0, 0, tiled=True)  45.7 us
    all_to_all x1, blocking collectives, shards(): dots = lax.all_to_all(laid, 'exp', 0, 0, tiled=True)  23.6 us
    all_to_all x1, blocking collectives, shards(): own = jnp.sum(lax.all_to_all(term, 'exp', 0, 0, tiled=True), axis=0)  13.5 us
    all_to_all x1, starting transfers between devices, shards(): lax.all_to_all(copied, 'ctx', 0, 0, axis_index_groups=groups, tiled=True)  12.2 us
    all_to_all x1, blocking collectives, shards(): lax.all_to_all(copied, 'ctx', 0, 0, axis_index_groups=groups, tiled=True)  11.2 us
    all_to_all x1, waiting for transfers between devices, shards(): lax.all_to_all(copied, 'ctx', 0, 0, axis_index_groups=groups, tiled=True)  6.02 us
    all_to_all x1, starting transfers between devices, shards(): copies = lax.all_to_all(packed, 'exp', 0, 0, tiled=True)  5.7 us
    unnamed x16, local copies, waits for them, and re-layouts  4.62 us
  transfers between devices with their start and end apart: 2, of which 2 were waited for; matrix products, arithmetic and copies ran while one was open for 1% of the time, Pallas kernels for 0%

profile of v1, /device:TPU:1, one launch (start us, length us, event | category | flops | bytes accessed | tf_op | source)
XLA Modules:
  0.0 129.5 jit_solution(10935504752990731306)
XLA Ops:
  0.6 0.0 copy-start.1
  0.6 0.0 copy-start.7
  0.6 0.8 copy-done.7
  1.5 0.2 shard_map.77
  1.7 23.6 %all_to_all.25.dots_ref = f32[16,1,128]{2,1,0:T(1,128)S(1)} all-to-all(f32[16,1,128]{2,1,0:T(1,128)S(1)} %shard_map.77), channel_id=1, replica_groups=mesh['ctx'=64,'exp'=16] {'exp'}, dimensions={0} | all-to-all | bytes 16384 | tf_op jit(solution)/shard_map/all_to_all | solution.py:125
  25.3 1.1 copy-done.2
  26.4 0.7 copy-done.4
  27.1 0.7 copy-done.5
  27.8 0.4 shard_map.78
  28.2 13.5 %all_to_all.26 = f32[16,1,3072]{2,1,0:T(1,128)S(1)} all-to-all(f32[16,1,3072]{2,1,0:T(1,128)S(1)} %get-tuple-element.7), channel_id=1, replica_groups=mesh['ctx'=64,'exp'=16] {'exp'}, dimensions={0} | all-to-all | bytes 393216 | tf_op jit(solution)/shard_map/all_to_all | solution.py:149
  41.7 0.1 reduce_sum.29
  41.8 0.1 broadcast_in_dim.7
  41.9 11.2 %all_to_all.27 = f32[8,1,3072]{2,1,0:T(1,128)S(1)} all-to-all(f32[8,1,3072]{2,1,0:T(1,128)S(1)} %broadcast_in_dim.7), channel_id=1, replica_groups={{0,128,256,384,512,640,768,896},{16,144,272,400,528,656,784,912},{32,16..., dimensions={0} | all-to-all | bytes 196608 | tf_op jit(solution)/shard_map/all_to_all | solution.py:155
  53.1 0.1 reduce_sum.30
  53.1 0.7 broadcast_in_dim.8
  53.8 12.2 %all-to-all-start.4 = ((f32[8,1,3072]{2,1,0:T(1,128)}), f32[8,1,3072]{2,1,0:T(1,128)S(1)}, u32[]{:S(2)}, u32[]{:S(2)}) async-start(f32[8,1,3072]{2,1,0:T(1,128)} %broadcast_in_dim.8), calls=%async_computation.4 | async-start | bytes 196608 | tf_op jit(solution)/shard_map/all_to_all | solution.py:155
  66.1 0.4 shard_map.79
  66.4 1.3 copy-done
  67.7 6.0 %all-to-all-done.4 = f32[8,1,3072]{2,1,0:T(1,128)S(1)} async-done(((f32[8,1,3072]{2,1,0:T(1,128)}), f32[8,1,3072]{2,1,0:T(1,128)S(1)}, u32[]{:S(2)}, u32[]{:S(2)}) %all-to-all-start.4) | async-done | bytes 98336 | tf_op jit(solution)/shard_map/all_to_all | solution.py:155
  73.7 5.7 %all-to-all-start.1 = ((bf16[16,80,768]{2,1,0:T(8,128)(2,1)}), bf16[16,80,768]{2,1,0:T(8,128)(2,1)S(1)}, u32[]{:S(2)}, u32[]{:S(2)}) async-start(bf16[16,80,768]{2,1,0:T(8,128)(2,1)} %copy-done), calls=%async_computation.1 | async-start | bytes 3932160 | tf_op jit(solution)/shard_map/all_to_all | solution.py:135
  79.4 0.7 reduce_sum.31
  80.1 45.7 %all-to-all-done.1.refs_4_ = bf16[16,80,768]{2,1,0:T(8,128)(2,1)S(1)} async-done(((bf16[16,80,768]{2,1,0:T(8,128)(2,1)}), bf16[16,80,768]{2,1,0:T(8,128)(2,1)S(1)}, u32[]{:S(2)}, u32[]{:S(2)}) %all-to-all-start.1) | async-done | bytes 1966112 | tf_op jit(solution)/shard_map/all_to_all | solution.py:135
  125.8 0.0 copy-done.3
  125.8 3.7 %shard_map.80 = bf16[128,3072]{1,0:T(8,128)(2,1)} custom-call(s32[2,128]{1,0:T(2,128)S(1)} %bitcast.15, f32[8,128]{1,0:T(8,128)S(1)} %get-tuple-element.5.refs_1_, bf16[16,128]{1,0:T(8,128)(2,1)S(1)} %get-tuple-element.6.refs_2_, bf16[16,3072]{1,0:T(8,128)(2,1)S(1)} %copy-done.3, bf16[16,80,768]{2,1,0:T(8,128)(2,1)S(1)} %all-to-all-done.1.refs_4_), custom_call_target="tpu_custom_call" | custom-call | tf_op jit(solution)/shard_map/pallas_call | solution.py:158
  (8 shorter events, 0.0 us)
Async XLA Ops:
  0.6 65.4 %copy-start.1 = (bf16[1,1,320,3072]{3,2,1,0:T(8,128)(2,1)S(1)}, bf16[1,1,320,3072]{3,2,1,0:T(8,128)(2,1)}, u32[]{:S(2)}) copy-start(bf16[1,1,320,3072]{3,2,1,0:T(8,128)(2,1)} %param.10) | copy-start | bytes 5898244
  0.6 0.8 copy-start.7
  25.3 1.1 copy-start.2
  26.4 0.7 copy-start.4
  27.1 0.7 copy-start.5
  53.8 19.9 %all-to-all-start.4 = ((f32[8,1,3072]{2,1,0:T(1,128)}), f32[8,1,3072]{2,1,0:T(1,128)S(1)}, u32[]{:S(2)}, u32[]{:S(2)}) async-start(f32[8,1,3072]{2,1,0:T(1,128)} %broadcast_in_dim.8), calls=%async_computation.4 | async-start | bytes 196608 | tf_op jit(solution)/shard_map/all_to_all | solution.py:155
  66.4 1.3 copy-start
  67.7 58.1 %copy-start.3 = (bf16[16,3072]{1,0:T(8,128)(2,1)S(1)}, bf16[16,3072]{1,0:T(8,128)(2,1)}, u32[]{:S(2)}) copy-start(bf16[16,3072]{1,0:T(8,128)(2,1)} %refs_3_.1) | copy-start | bytes 294916
  67.7 58.1 %copy-start.6 = (s32[1,128,2]{1,2,0:T(2,128)S(1)}, s32[1,128,2]{1,2,0:T(2,128)}, u32[]{:S(2)}) copy-start(s32[1,128,2]{1,2,0:T(2,128)} %param.7) | copy-start | bytes 3076
  73.7 52.0 %all-to-all-start.1 = ((bf16[16,80,768]{2,1,0:T(8,128)(2,1)}), bf16[16,80,768]{2,1,0:T(8,128)(2,1)S(1)}, u32[]{:S(2)}, u32[]{:S(2)}) async-start(bf16[16,80,768]{2,1,0:T(8,128)(2,1)} %copy-done), calls=%async_computation.1 | async-start | bytes 3932160 | tf_op jit(solution)/shard_map/all_to_all | solution.py:135

commit v2 on v1

--- a/solution.py
+++ b/solution.py
@@ -6,6 +6,7 @@
 from jax.sharding import PartitionSpec as P
 
 QUARTERS = 4
+STEPS = (0, 3, 5, 2, 6, 4, 1, 7)
 LANES = 128
 VMEM = 48 * 1024 * 1024
 
@@ -32,18 +33,32 @@
     out_ref[...] = laid[:, None, :]
 
 
-def pack_kernel(cap, rows_ref, out_ref):
-    part = out_ref.shape[2]
+def pack_kernel(cap, rows_ref, kept_ref, given_ref):
+    part = kept_ref.shape[2]
+    core = lax.axis_index("exp") % 2
     rows = rows_ref[...].astype(jnp.float32)
-    for w in range(out_ref.shape[0]):
-        window = rows[w * cap : (w + 1) * cap]
-        stacked = jnp.concatenate(
-            [window[:, q * part : (q + 1) * part] for q in range(QUARTERS)], axis=0
-        )
-        out_ref[w] = stacked.astype(jnp.bfloat16)
-
-
-def router_kernel(ids_ref, probs_ref, dots_ref, input_ref, logit_ref, place_ref, term_ref):
+    for pair in range(kept_ref.shape[0]):
+        stacks = []
+        for w in (2 * pair, 2 * pair + 1):
+            window = rows[w * cap : (w + 1) * cap]
+            stacked = jnp.concatenate(
+                [window[:, q * part : (q + 1) * part] for q in range(QUARTERS)], axis=0
+            )
+            stacks.append(stacked)
+        kept_ref[pair] = jnp.where(core == 0, stacks[0], stacks[1]).astype(jnp.bfloat16)
+        given_ref[pair] = jnp.where(core == 0, stacks[1], stacks[0]).astype(jnp.bfloat16)
+
+
+def deal_kernel(kept_ref, got_ref, *out_refs):
+    chips = kept_ref.shape[0]
+    chip = lax.axis_index("exp") // 2
+    for step, out_ref in zip(STEPS, out_refs):
+        target = (chip + step) % chips
+        out_ref[0] = kept_ref[target]
+        out_ref[1] = got_ref[target]
+
+
+def router_kernel(depth, ids_ref, probs_ref, dots_ref, input_ref, logit_ref, place_ref, term_ref):
     experts, tokens = probs_ref.shape
     probs = probs_ref[...]
     expert = lax.broadcasted_iota(jnp.int32, (experts, tokens), 0)
@@ -76,34 +91,41 @@
     logit = probs * (router_grad - jnp.sum(probs * router_grad, axis=0, keepdims=True))
     logit = logit.astype(jnp.bfloat16)
     logit_ref[...] = logit
-    place_ref[...] = jnp.concatenate(
-        [picked[0] / total, picked[1] / total]
-        + [s.astype(jnp.float32) for s in slots]
-        + [jnp.zeros((4, tokens), jnp.float32)],
+    chip, core = lax.axis_index("exp") // 2, lax.axis_index("exp") % 2
+    rows = []
+    for k in range(2):
+        ids = ids_ref[k : k + 1, :]
+        step = (chip - ids // 2 + experts // 2) % (experts // 2)
+        place = sum(jnp.where(step == STEPS[n], n, 0) for n in range(len(STEPS)))
+        block = place * 2 + (ids % 2 + core) % 2
+        rows.append((block * depth + slots[k]).astype(jnp.float32))
+    place = jnp.concatenate(
+        [picked[0] / total, picked[1] / total] + rows + [jnp.zeros((4, tokens), jnp.float32)],
         axis=0,
     )
+    place_ref[...] = place.T
     term = jnp.dot(logit, input_ref[...], preferred_element_type=jnp.float32)
     term_ref[...] = term[:, None, :]
 
 
-def combine_kernel(cap, ids_ref, place_ref, logit_ref, weight_ref, copies_ref, out_ref):
-    experts, depth, part = copies_ref.shape
-    tokens = ids_ref.shape[1]
-    copies = copies_ref[...].reshape(experts * depth, part)
-    row = lax.broadcasted_iota(jnp.int32, (experts * depth, tokens), 0)
-    gates = [place_ref[k : k + 1, :] for k in range(2)]
-    base = [
-        ids_ref[k : k + 1, :] * depth + place_ref[2 + k : 3 + k, :].astype(jnp.int32)
-        for k in range(2)
-    ]
+def combine_kernel(cap, place_ref, logit_ref, weight_ref, *refs):
+    out_ref = refs[-1]
+    depth, part = refs[0].shape[1:]
+    tokens = place_ref.shape[0]
+    copies = jnp.concatenate([ref[...].reshape(2 * depth, part) for ref in refs[:-1]], axis=0)
+    column = lax.broadcasted_iota(jnp.int32, (tokens, copies.shape[0]), 1)
+    gates = [place_ref[:, k : k + 1] for k in range(2)]
+    base = [place_ref[:, 2 + k : 3 + k].astype(jnp.int32) for k in range(2)]
     for q in range(QUARTERS):
-        spread = jnp.where(row == base[0] + q * cap, gates[0], 0.0) + jnp.where(
-            row == base[1] + q * cap, gates[1], 0.0
-        )
+        spread = jnp.where(column == base[0] + q * cap, gates[0], 0.0)
+        spread = jnp.where(column == base[1] + q * cap, gates[1], spread)
         high = spread.astype(jnp.bfloat16)
         low = (spread - high.astype(jnp.float32)).astype(jnp.bfloat16)
+        both = jnp.dot(
+            jnp.concatenate([high, low], axis=0), copies, preferred_element_type=jnp.float32
+        )
         columns = slice(q * part, (q + 1) * part)
-        total = dot_rows(high, copies) + dot_rows(low, copies)
+        total = both[:tokens] + both[tokens:]
         total = total + dot_rows(logit_ref[...], weight_ref[:, columns])
         out_ref[:, columns] = total.astype(jnp.bfloat16)
 
@@ -112,11 +134,23 @@
     slots, width = expert_grads.shape[2:]
     tokens, experts = router_probs.shape[1:]
     windows = lax.axis_size("exp")
+    chips = windows // 2
     cap = slots // windows
     part = width // QUARTERS
     depth = cap * QUARTERS
     params = pltpu.CompilerParams(vmem_limit_bytes=VMEM)
 
+    half = jax.ShapeDtypeStruct((chips, depth, part), jnp.bfloat16)
+    kept, given = pl.pallas_call(
+        lambda *refs: pack_kernel(cap, *refs),
+        out_shape=(half, half),
+        grid=(windows // 4,),
+        in_specs=[pl.BlockSpec((4 * cap, width), lambda g: (g, 0))],
+        out_specs=(pl.BlockSpec((2, depth, part), lambda g: (g, 0, 0)),) * 2,
+        compiler_params=params,
+    )(expert_grads[0, 0])
+    got = lax.ppermute(given, "exp", [(i, i ^ 1) for i in range(windows)])
+
     laid = pl.pallas_call(
         lambda *refs: gate_pack_kernel(cap, *refs),
         out_shape=jax.ShapeDtypeStruct((windows, 1, LANES), jnp.float32),
@@ -124,23 +158,24 @@
     )(gate_dots[0])
     dots = lax.all_to_all(laid, "exp", 0, 0, tiled=True)
 
-    packed = pl.pallas_call(
-        lambda *refs: pack_kernel(cap, *refs),
-        out_shape=jax.ShapeDtypeStruct((windows, depth, part), jnp.bfloat16),
-        grid=(windows // 4,),
-        in_specs=[pl.BlockSpec((4 * cap, width), lambda g: (g, 0))],
-        out_specs=pl.BlockSpec((4, depth, part), lambda g: (g, 0, 0)),
-        compiler_params=params,
-    )(expert_grads[0, 0])
-    copies = lax.all_to_all(packed, "exp", 0, 0, tiled=True)
+    dealt = pl.pallas_call(
+        deal_kernel,
+        out_shape=(jax.ShapeDtypeStruct((2, depth, part), jnp.bfloat16),) * chips,
+        compiler_params=params,
+    )(kept, got)
+    copies = [dealt[0]]
+    for step, block in zip(STEPS[1:], dealt[1:]):
+        moves = [(i, (i + 2 * step) % windows) for i in range(windows)]
+        copies.append(lax.ppermute(block, "exp", moves))
+    dots, _ = lax.optimization_barrier((dots, dealt))
 
     ids = jnp.swapaxes(expert_ids, 1, 2)[0]
     probs = jnp.swapaxes(router_probs, 1, 2)[0]
     logit, place, term = pl.pallas_call(
-        router_kernel,
+        lambda *refs: router_kernel(depth, *refs),
         out_shape=(
             jax.ShapeDtypeStruct((experts, tokens), jnp.bfloat16),
-            jax.ShapeDtypeStruct((8, tokens), jnp.float32),
+            jax.ShapeDtypeStruct((tokens, 8), jnp.float32),
             jax.ShapeDtypeStruct((experts, 1, width), jnp.float32),
         ),
         compiler_params=params,
@@ -159,7 +194,7 @@
         lambda *refs: combine_kernel(cap, *refs),
         out_shape=jax.ShapeDtypeStruct((tokens, width), jnp.bfloat16),
         compiler_params=params,
-    )(ids, place, logit, router_weight, copies)
+    )(place, logit, router_weight, *copies)
     return combined[None], own
 
 

time: 130 us -> 99.1 us (0.76)
  the two profiles are of different devices: /device:TPU:1 before, /device:TPU:46 now
where the time goes in v2:
time: 99.1 us; the launch traced here: 98.4 us
  starting transfers between devices  76.1 us (77%)
  Pallas kernels  7.31 us (7%)
  local copies, waits for them, and re-layouts  7.11 us (7%)
  waiting for transfers between devices  6.15 us (6%)
    all_to_all x2, starting transfers between devices, shards(): lax.all_to_all(copied, 'ctx', 0, 0, axis_index_groups=groups, tiled=True)  32.2 us
    ppermute x7, starting transfers between devices, shards(): copies.append(lax.ppermute(block, 'exp', moves))  27.9 us
    all_to_all x1, starting transfers between devices, shards(): dots = lax.all_to_all(laid, 'exp', 0, 0, tiled=True)  7.78 us
    all_to_all x1, starting transfers between devices, shards(): own = jnp.sum(lax.all_to_all(term, 'exp', 0, 0, tiled=True), axis=0)  6.33 us
    unnamed x24, local copies, waits for them, and re-layouts  5.72 us
    all_to_all x2, waiting for transfers between devices, shards(): lax.all_to_all(copied, 'ctx', 0, 0, axis_index_groups=groups, tiled=True)  5.22 us
    pallas_call x1, Pallas kernels, shards(): pl.pallas_call(lambda *refs: combine_kernel(cap, *refs), out_shape=jax.Sh...  3.45 us
  transfers between devices with their start and end apart: 12, of which 2 were waited for; matrix products, arithmetic and copies ran while one was open for 2% of the time, Pallas kernels for 4%

profile of v2, /device:TPU:46, one launch (start us, length us, event | category | flops | bytes accessed | tf_op | source)
XLA Modules:
  0.0 98.4 jit_solution(14772545528166025374)
XLA Ops:
  0.7 1.5 %copy-done = bf16[1,1,320,3072]{3,2,1,0:T(8,128)(2,1)S(1)} copy-done((bf16[1,1,320,3072]{3,2,1,0:T(8,128)(2,1)S(1)}, bf16[1,1,320,3072]{3,2,1,0:T(8,128)(2,1)}, u32[]{:S(2)}) %copy-start) | copy-done | bytes 1966104
  2.2 1.8 %shard_map.78 = (bf16[8,80,768]{2,1,0:T(8,128)(2,1)S(1)}, bf16[8,80,768]{2,1,0:T(8,128)(2,1)}) custom-call(bf16[320,3072]{1,0:T(8,128)(2,1)S(1)} %bitcast.11), custom_call_target="tpu_custom_call" | custom-call | tf_op jit(solution)/shard_map/pallas_call | solution.py:144
  4.0 1.9 %collective-permute-start = (bf16[8,80,768]{2,1,0:T(8,128)(2,1)}, bf16[8,80,768]{2,1,0:T(8,128)(2,1)S(1)}, u32[]{:S(2)}, u32[]{:S(2)}) collective-permute-start(bf16[8,80,768]{2,1,0:T(8,128)(2,1)} %get-tuple-element.17), channel_id=1, source_target_pairs={{0,1},{1,0},{2,3},{3,2},{4,5},{5,4},{6,7},{7,6},{8,9},{9,8},{10,11... | collective-permute-start | bytes 2949128 | tf_op jit(solution)/shard_map/ppermute | solution.py:152
  5.9 0.8 shard_map.77
  6.7 7.8 %all-to-all-start = ((f32[16,1,128]{2,1,0:T(1,128)}), f32[16,1,128]{2,1,0:T(1,128)S(1)}, u32[]{:S(2)}, u32[]{:S(2)}) async-start(f32[16,1,128]{2,1,0:T(1,128)} %shard_map.77), calls=%async_computation | async-start | bytes 16384 | tf_op jit(solution)/shard_map/all_to_all | solution.py:159
  16.0 0.7 copy-done.8
  16.7 0.7 copy-done.9
  17.4 0.7 copy-done.10
  18.1 0.7 copy-done.11
  18.8 0.9 all-to-all-done.refs_2_
  19.8 1.1 %shard_map.80 = (bf16[16,128]{1,0:T(8,128)(2,1)S(1)}, f32[128,8]{1,0:T(8,128)S(1)}, f32[16,1,3072]{2,1,0:T(1,128)}) custom-call(s32[2,128]{1,0:T(2,128)S(1)} %bitcast.15, f32[16,128]{1,0:T(8,128)S(1)} %bitcast.13, f32[16,1,128]{2,1,0:T(1,128)S(1)} %all-to-all-done.refs_2_, bf16[128,3072]{1,0:T(8,128)(2,1)S(1)} %bitcast.12), custom_call_target="tpu_custom_call" | custom-call | tf_op jit(solution)/shard_map/pallas_call | solution.py:174
  20.9 6.3 %all-to-all-start.1 = ((f32[16,1,3072]{2,1,0:T(1,128)}), f32[16,1,3072]{2,1,0:T(1,128)S(1)}, u32[]{:S(2)}, u32[]{:S(2)}) async-start(f32[16,1,3072]{2,1,0:T(1,128)} %get-tuple-element.29), calls=%async_computation.1 | async-start | bytes 393216 | tf_op jit(solution)/shard_map/all_to_all | solution.py:184
  27.2 5.5 %collective-permute-start.1 = (bf16[2,80,768]{2,1,0:T(8,128)(2,1)}, bf16[2,80,768]{2,1,0:T(8,128)(2,1)S(1)}, u32[]{:S(2)}, u32[]{:S(2)}) collective-permute-start(bf16[2,80,768]{2,1,0:T(8,128)(2,1)} %copy-done.11), channel_id=1, source_target_pairs={{0,6},{1,7},{2,8},{3,9},{4,10},{5,11},{6,12},{7,13},{8,14},{9,15},... | collective-permute-start | bytes 737288 | tf_op jit(solution)/shard_map/ppermute | solution.py:169
  32.7 3.4 %collective-permute-start.2 = (bf16[2,80,768]{2,1,0:T(8,128)(2,1)}, bf16[2,80,768]{2,1,0:T(8,128)(2,1)S(1)}, u32[]{:S(2)}, u32[]{:S(2)}) collective-permute-start(bf16[2,80,768]{2,1,0:T(8,128)(2,1)} %copy-done.10), channel_id=1, source_target_pairs={{0,10},{1,11},{2,12},{3,13},{4,14},{5,15},{6,0},{7,1},{8,2},{9,3},... | collective-permute-start | bytes 737288 | tf_op jit(solution)/shard_map/ppermute | solution.py:169
  36.9 12.0 %all-to-all-start.2 = ((f32[8,1,3072]{2,1,0:T(1,128)}), f32[8,1,3072]{2,1,0:T(1,128)S(1)}, u32[]{:S(2)}, u32[]{:S(2)}) async-start(f32[8,1,3072]{2,1,0:T(1,128)} %broadcast_in_dim.7), calls=%async_computation.2 | async-start | bytes 196608 | tf_op jit(solution)/shard_map/all_to_all | solution.py:190
  48.8 5.5 %collective-permute-start.3 = (bf16[2,80,768]{2,1,0:T(8,128)(2,1)}, bf16[2,80,768]{2,1,0:T(8,128)(2,1)S(1)}, u32[]{:S(2)}, u32[]{:S(2)}) collective-permute-start(bf16[2,80,768]{2,1,0:T(8,128)(2,1)} %copy-done.9), channel_id=1, source_target_pairs={{0,4},{1,5},{2,6},{3,7},{4,8},{5,9},{6,10},{7,11},{8,12},{9,13},{1... | collective-permute-start | bytes 737288 | tf_op jit(solution)/shard_map/ppermute | solution.py:169
  54.3 1.9 %collective-permute-start.4 = (bf16[2,80,768]{2,1,0:T(8,128)(2,1)}, bf16[2,80,768]{2,1,0:T(8,128)(2,1)S(1)}, u32[]{:S(2)}, u32[]{:S(2)}) collective-permute-start(bf16[2,80,768]{2,1,0:T(8,128)(2,1)} %copy-done.8), channel_id=1, source_target_pairs={{0,12},{1,13},{2,14},{3,15},{4,0},{5,1},{6,2},{7,3},{8,4},{9,5},{1... | collective-permute-start | bytes 737288 | tf_op jit(solution)/shard_map/ppermute | solution.py:169
  56.3 4.8 %collective-permute-start.5 = (bf16[2,80,768]{2,1,0:T(8,128)(2,1)}, bf16[2,80,768]{2,1,0:T(8,128)(2,1)S(1)}, u32[]{:S(2)}, u32[]{:S(2)}) collective-permute-start(bf16[2,80,768]{2,1,0:T(8,128)(2,1)} %copy-done.7), channel_id=1, source_target_pairs={{0,8},{1,9},{2,10},{3,11},{4,12},{5,13},{6,14},{7,15},{8,0},{9,1},... | collective-permute-start | bytes 737288 | tf_op jit(solution)/shard_map/ppermute | solution.py:169
  61.1 2.3 %collective-permute-start.6 = (bf16[2,80,768]{2,1,0:T(8,128)(2,1)}, bf16[2,80,768]{2,1,0:T(8,128)(2,1)S(1)}, u32[]{:S(2)}, u32[]{:S(2)}) collective-permute-start(bf16[2,80,768]{2,1,0:T(8,128)(2,1)} %copy-done.6), channel_id=1, source_target_pairs={{0,2},{1,3},{2,4},{3,5},{4,6},{5,7},{6,8},{7,9},{8,10},{9,11},{10,... | collective-permute-start | bytes 737288 | tf_op jit(solution)/shard_map/ppermute | solution.py:169
  63.4 4.6 %collective-permute-start.7 = (bf16[2,80,768]{2,1,0:T(8,128)(2,1)S(1)}, bf16[2,80,768]{2,1,0:T(8,128)(2,1)S(1)}, u32[]{:S(2)}, u32[]{:S(2)}) collective-permute-start(bf16[2,80,768]{2,1,0:T(8,128)(2,1)S(1)} %get-tuple-element.25), channel_id=1, source_target_pairs={{0,14},{1,15},{2,0},{3,1},{4,2},{5,3},{6,4},{7,5},{8,6},{9,7},{10,... | collective-permute-start | bytes 737288 | tf_op jit(solution)/shard_map/ppermute | solution.py:169
  68.1 0.7 broadcast_in_dim.8
  68.8 20.2 %all-to-all-start.3 = ((f32[8,1,3072]{2,1,0:T(1,128)}), f32[8,1,3072]{2,1,0:T(1,128)S(1)}, u32[]{:S(2)}, u32[]{:S(2)}) async-start(f32[8,1,3072]{2,1,0:T(1,128)} %broadcast_in_dim.8), calls=%async_computation.3 | async-start | bytes 196608 | tf_op jit(solution)/shard_map/all_to_all | solution.py:190
  89.1 3.5 %shard_map.81 = bf16[128,3072]{1,0:T(8,128)(2,1)} custom-call(f32[128,8]{1,0:T(8,128)S(1)} %get-tuple-element.27.refs_0_, bf16[16,128]{1,0:T(8,128)(2,1)S(1)} %get-tuple-element.28.refs_1_, bf16[16,3072]{1,0:T(8,128)(2,1)S(1)} %copy-done.2, bf16[2,80,768]{2,1,0:T(8,128)(2,1)S(1)} %get-tuple-element.18.refs_3_, ...), custom_call_target="tpu_custom_call" | custom-call | tf_op jit(solution)/shard_map/pallas_call | solution.py:193
  92.5 5.2 %all-to-all-done.3 = f32[8,1,3072]{2,1,0:T(1,128)S(1)} async-done(((f32[8,1,3072]{2,1,0:T(1,128)}), f32[8,1,3072]{2,1,0:T(1,128)S(1)}, u32[]{:S(2)}, u32[]{:S(2)}) %all-to-all-start.3) | async-done | bytes 98336 | tf_op jit(solution)/shard_map/all_to_all | solution.py:190
  (34 shorter events, 3.1 us)
Async XLA Ops:
  0.6 5.3 %copy-start.4 = (bf16[1,1,320]{2,1,0:T(2,128)(2,1)S(1)}, bf16[1,1,320]{2,1,0:T(2,128)(2,1)}, u32[]{:S(2)}) copy-start(bf16[1,1,320]{2,1,0:T(2,128)(2,1)} %param.11) | copy-start | bytes 1924
  0.6 1.6 %copy-start = (bf16[1,1,320,3072]{3,2,1,0:T(8,128)(2,1)S(1)}, bf16[1,1,320,3072]{3,2,1,0:T(8,128)(2,1)}, u32[]{:S(2)}) copy-start(bf16[1,1,320,3072]{3,2,1,0:T(8,128)(2,1)} %param.10) | copy-start | bytes 5898244
  2.2 17.6 %copy-start.1 = (bf16[1,128,3072]{2,1,0:T(8,128)(2,1)S(1)}, bf16[1,128,3072]{2,1,0:T(8,128)(2,1)}, u32[]{:S(2)}) copy-start(bf16[1,128,3072]{2,1,0:T(8,128)(2,1)} %param.6) | copy-start | bytes 2359300
  2.2 17.6 %copy-start.3 = (f32[1,128,16]{1,2,0:T(8,128)S(1)}, f32[1,128,16]{1,2,0:T(8,128)}, u32[]{:S(2)}) copy-start(f32[1,128,16]{1,2,0:T(8,128)} %param.8) | copy-start | bytes 24580
  2.2 17.6 %copy-start.5 = (s32[1,128,2]{1,2,0:T(2,128)S(1)}, s32[1,128,2]{1,2,0:T(2,128)}, u32[]{:S(2)}) copy-start(s32[1,128,2]{1,2,0:T(2,128)} %param.7) | copy-start | bytes 3076
  4.0 10.5 %collective-permute-start = (bf16[8,80,768]{2,1,0:T(8,128)(2,1)}, bf16[8,80,768]{2,1,0:T(8,128)(2,1)S(1)}, u32[]{:S(2)}, u32[]{:S(2)}) collective-permute-start(bf16[8,80,768]{2,1,0:T(8,128)(2,1)} %get-tuple-element.17), channel_id=1, source_target_pairs={{0,1},{1,0},{2,3},{3,2},{4,5},{5,4},{6,7},{7,6},{8,9},{9,8},{10,11... | collective-permute-start | bytes 2949128 | tf_op jit(solution)/shard_map/ppermute | solution.py:152
  6.7 13.0 %all-to-all-start = ((f32[16,1,128]{2,1,0:T(1,128)}), f32[16,1,128]{2,1,0:T(1,128)S(1)}, u32[]{:S(2)}, u32[]{:S(2)}) async-start(f32[16,1,128]{2,1,0:T(1,128)} %shard_map.77), calls=%async_computation | async-start | bytes 16384 | tf_op jit(solution)/shard_map/all_to_all | solution.py:159
  14.5 74.6 %copy-start.2 = (bf16[16,3072]{1,0:T(8,128)(2,1)S(1)}, bf16[16,3072]{1,0:T(8,128)(2,1)}, u32[]{:S(2)}) copy-start(bf16[16,3072]{1,0:T(8,128)(2,1)} %refs_2_.1) | copy-start | bytes 294916
  14.7 0.7 copy-start.6
  15.4 0.7 copy-start.7
  16.0 0.7 copy-start.8
  16.7 0.7 copy-start.9
  17.4 0.7 copy-start.10
  18.1 0.7 copy-start.11
  20.9 15.2 %all-to-all-start.1 = ((f32[16,1,3072]{2,1,0:T(1,128)}), f32[16,1,3072]{2,1,0:T(1,128)S(1)}, u32[]{:S(2)}, u32[]{:S(2)}) async-start(f32[16,1,3072]{2,1,0:T(1,128)} %get-tuple-element.29), calls=%async_computation.1 | async-start | bytes 393216 | tf_op jit(solution)/shard_map/all_to_all | solution.py:184
  27.2 33.9 %collective-permute-start.1 = (bf16[2,80,768]{2,1,0:T(8,128)(2,1)}, bf16[2,80,768]{2,1,0:T(8,128)(2,1)S(1)}, u32[]{:S(2)}, u32[]{:S(2)}) collective-permute-start(bf16[2,80,768]{2,1,0:T(8,128)(2,1)} %copy-done.11), channel_id=1, source_target_pairs={{0,6},{1,7},{2,8},{3,9},{4,10},{5,11},{6,12},{7,13},{8,14},{9,15},... | collective-permute-start | bytes 737288 | tf_op jit(solution)/shard_map/ppermute | solution.py:169
  32.7 30.7 %collective-permute-start.2 = (bf16[2,80,768]{2,1,0:T(8,128)(2,1)}, bf16[2,80,768]{2,1,0:T(8,128)(2,1)S(1)}, u32[]{:S(2)}, u32[]{:S(2)}) collective-permute-start(bf16[2,80,768]{2,1,0:T(8,128)(2,1)} %copy-done.10), channel_id=1, source_target_pairs={{0,10},{1,11},{2,12},{3,13},{4,14},{5,15},{6,0},{7,1},{8,2},{9,3},... | collective-permute-start | bytes 737288 | tf_op jit(solution)/shard_map/ppermute | solution.py:169
  36.9 31.1 %all-to-all-start.2 = ((f32[8,1,3072]{2,1,0:T(1,128)}), f32[8,1,3072]{2,1,0:T(1,128)S(1)}, u32[]{:S(2)}, u32[]{:S(2)}) async-start(f32[8,1,3072]{2,1,0:T(1,128)} %broadcast_in_dim.7), calls=%async_computation.2 | async-start | bytes 196608 | tf_op jit(solution)/shard_map/all_to_all | solution.py:190
  48.8 40.2 %collective-permute-start.3 = (bf16[2,80,768]{2,1,0:T(8,128)(2,1)}, bf16[2,80,768]{2,1,0:T(8,128)(2,1)S(1)}, u32[]{:S(2)}, u32[]{:S(2)}) collective-permute-start(bf16[2,80,768]{2,1,0:T(8,128)(2,1)} %copy-done.9), channel_id=1, source_target_pairs={{0,4},{1,5},{2,6},{3,7},{4,8},{5,9},{6,10},{7,11},{8,12},{9,13},{1... | collective-permute-start | bytes 737288 | tf_op jit(solution)/shard_map/ppermute | solution.py:169
  54.3 34.7 %collective-permute-start.4 = (bf16[2,80,768]{2,1,0:T(8,128)(2,1)}, bf16[2,80,768]{2,1,0:T(8,128)(2,1)S(1)}, u32[]{:S(2)}, u32[]{:S(2)}) collective-permute-start(bf16[2,80,768]{2,1,0:T(8,128)(2,1)} %copy-done.8), channel_id=1, source_target_pairs={{0,12},{1,13},{2,14},{3,15},{4,0},{5,1},{6,2},{7,3},{8,4},{9,5},{1... | collective-permute-start | bytes 737288 | tf_op jit(solution)/shard_map/ppermute | solution.py:169
  56.3 32.8 %collective-permute-start.5 = (bf16[2,80,768]{2,1,0:T(8,128)(2,1)}, bf16[2,80,768]{2,1,0:T(8,128)(2,1)S(1)}, u32[]{:S(2)}, u32[]{:S(2)}) collective-permute-start(bf16[2,80,768]{2,1,0:T(8,128)(2,1)} %copy-done.7), channel_id=1, source_target_pairs={{0,8},{1,9},{2,10},{3,11},{4,12},{5,13},{6,14},{7,15},{8,0},{9,1},... | collective-permute-start | bytes 737288 | tf_op jit(solution)/shard_map/ppermute | solution.py:169
  61.1 28.0 %collective-permute-start.6 = (bf16[2,80,768]{2,1,0:T(8,128)(2,1)}, bf16[2,80,768]{2,1,0:T(8,128)(2,1)S(1)}, u32[]{:S(2)}, u32[]{:S(2)}) collective-permute-start(bf16[2,80,768]{2,1,0:T(8,128)(2,1)} %copy-done.6), channel_id=1, source_target_pairs={{0,2},{1,3},{2,4},{3,5},{4,6},{5,7},{6,8},{7,9},{8,10},{9,11},{10,... | collective-permute-start | bytes 737288 | tf_op jit(solution)/shard_map/ppermute | solution.py:169
  63.4 25.7 %collective-permute-start.7 = (bf16[2,80,768]{2,1,0:T(8,128)(2,1)S(1)}, bf16[2,80,768]{2,1,0:T(8,128)(2,1)S(1)}, u32[]{:S(2)}, u32[]{:S(2)}) collective-permute-start(bf16[2,80,768]{2,1,0:T(8,128)(2,1)S(1)} %get-tuple-element.25), channel_id=1, source_target_pairs={{0,14},{1,15},{2,0},{3,1},{4,2},{5,3},{6,4},{7,5},{8,6},{9,7},{10,... | collective-permute-start | bytes 737288 | tf_op jit(solution)/shard_map/ppermute | solution.py:169
  68.8 29.0 %all-to-all-start.3 = ((f32[8,1,3072]{2,1,0:T(1,128)}), f32[8,1,3072]{2,1,0:T(1,128)S(1)}, u32[]{:S(2)}, u32[]{:S(2)}) async-start(f32[8,1,3072]{2,1,0:T(1,128)} %broadcast_in_dim.8), calls=%async_computation.3 | async-start | bytes 196608 | tf_op jit(solution)/shard_map/all_to_all | solution.py:190

commit v3 on v2

v3 whole, which is shorter than its diff:
```python
import jax
import jax.numpy as jnp
from jax import lax
from jax.experimental import pallas as pl
from jax.experimental.pallas import tpu as pltpu
from jax.sharding import PartitionSpec as P

QUARTERS = 4
LANES = 128
WHOLE = (0, 3, 5, 4)
SPLIT = (1, 2)
VMEM = 24 * 1024 * 1024


def dot_rows(left, right):
    return lax.dot_general(
        left, right, (((0,), (0,)), ((), ())), preferred_element_type=jnp.float32
    )


def gate_pack_kernel(cap, dots_ref, out_ref):
    windows, lanes = out_ref.shape[0], out_ref.shape[2]
    count = dots_ref.shape[1]
    column = lax.broadcasted_iota(jnp.int32, (windows, count), 1)
    first = lax.broadcasted_iota(jnp.int32, (windows, count), 0) * cap
    dots = jnp.broadcast_to(dots_ref[...].astype(jnp.float32), (windows, count))
    own = jnp.where((column >= first) & (column < first + cap), dots, 0.0)
    slot = lax.broadcasted_iota(jnp.int32, (count, lanes), 0) % cap
    lane = lax.broadcasted_iota(jnp.int32, (count, lanes), 1)
    place = jnp.where(slot == lane, 1.0, 0.0)
    laid = jnp.dot(
        own.astype(jnp.bfloat16), place.astype(jnp.bfloat16), preferred_element_type=jnp.float32
    )
    out_ref[...] = laid[:, None, :]


def split_target(chips, far):
    chip, core = lax.axis_index("exp") // 2, lax.axis_index("exp") % 2
    return (chip + jnp.where(core == 0, far, chips - far)) % chips


def pack_kernel(cap, rows_ref, packed_ref, given_ref):
    part = packed_ref.shape[2]
    chips = packed_ref.shape[0] // 2
    rows = rows_ref[...].astype(jnp.float32)
    for w in range(packed_ref.shape[0]):
        window = rows[w * cap : (w + 1) * cap]
        stacked = jnp.concatenate(
            [window[:, q * part : (q + 1) * part] for q in range(QUARTERS)], axis=0
        )
        packed_ref[w] = stacked.astype(jnp.bfloat16)
    chip, other = lax.axis_index("exp") // 2, 1 - lax.axis_index("exp") % 2
    for n, far in enumerate(WHOLE):
        given_ref[n] = packed_ref[(chip + far) % chips * 2 + other]
    for n, far in enumerate(SPLIT):
        target = (chip + jnp.where(other == 0, far, chips - far)) % chips
        given_ref[len(WHOLE) + 2 * n] = packed_ref[target * 2 + other]
        given_ref[len(WHOLE) + 2 * n + 1] = packed_ref[target * 2 + 1 - other]


def deal_kernel(packed_ref, got_ref, *out_refs):
    chips = packed_ref.shape[0] // 2
    chip, core = lax.axis_index("exp") // 2, lax.axis_index("exp") % 2
    for n, far in enumerate(WHOLE):
        out_refs[n][0] = packed_ref[(chip + far) % chips * 2 + core]
        out_refs[n][1] = got_ref[n]
    for n, far in enumerate(SPLIT):
        out_ref, target = out_refs[len(WHOLE) + n], split_target(chips, far)
        out_ref[0] = packed_ref[target * 2 + core]
        out_ref[1] = got_ref[len(WHOLE) + 2 * n]
        out_ref[2] = packed_ref[target * 2 + 1 - core]
        out_ref[3] = got_ref[len(WHOLE) + 2 * n + 1]


def sum_kernel(parts_ref, out_ref):
    total = parts_ref[0]
    for n in range(1, parts_ref.shape[0]):
        total = total + parts_ref[n]
    for n in range(out_ref.shape[0]):
        out_ref[n] = total


def router_kernel(depth, ids_ref, probs_ref, dots_ref, input_ref, logit_ref, place_ref, term_ref):
    experts, tokens = probs_ref.shape
    probs = probs_ref[...]
    expert = lax.broadcasted_iota(jnp.int32, (experts, tokens), 0)
    chosen = [expert == ids_ref[k : k + 1, :] for k in range(2)]
    mask = jnp.where(chosen[0] | chosen[1], 1.0, 0.0)
    earlier = lax.broadcasted_iota(jnp.int32, (tokens, tokens), 0) < lax.broadcasted_iota(
        jnp.int32, (tokens, tokens), 1
    )
    prior = jnp.dot(
        mask.astype(jnp.bfloat16),
        jnp.where(earlier, 1.0, 0.0).astype(jnp.bfloat16),
        preferred_element_type=jnp.float32,
    )
    dots = dots_ref[...][:, 0, :].astype(jnp.bfloat16)
    lane_count = dots.shape[1]
    slot_row = lax.broadcasted_iota(jnp.int32, (lane_count, tokens), 0)
    picked, gate_grad, slots = [], [], []
    for k in range(2):
        onehot = jnp.where(chosen[k], 1.0, 0.0)
        picked.append(jnp.sum(jnp.where(chosen[k], probs, 0.0), axis=0, keepdims=True))
        slot = jnp.sum(onehot * prior, axis=0, keepdims=True).astype(jnp.int32)
        slots.append(slot)
        values = dot_rows(dots, onehot.astype(jnp.bfloat16))
        gate_grad.append(jnp.sum(jnp.where(slot_row == slot, values, 0.0), axis=0, keepdims=True))
    total = picked[0] + picked[1]
    shared = (gate_grad[0] * picked[0] + gate_grad[1] * picked[1]) / (total * total)
    router_grad = sum(
        jnp.where(chosen[k], gate_grad[k] / total - shared, 0.0) for k in range(2)
    )
    logit = probs * (router_grad - jnp.sum(probs * router_grad, axis=0, keepdims=True))
    logit = logit.astype(jnp.bfloat16)
    logit_ref[...] = logit
    chip, core = lax.axis_index("exp") // 2, lax.axis_index("exp") % 2
    rows = []
    for k in range(2):
        ids = ids_ref[k : k + 1, :]
        step = (chip - ids // 2 + experts // 2) % (experts // 2)
        turned = jnp.where(core == 0, step, (experts // 2 - step) % (experts // 2))
        place = jnp.zeros_like(step)
        for n, far in enumerate(WHOLE):
            place = jnp.where(step == far, n, place)
        for n, far in enumerate(SPLIT):
            place = jnp.where(turned == far, len(WHOLE) + n, place)
            place = jnp.where(
                turned == experts // 2 - far, len(WHOLE) + len(SPLIT) + n, place
            )
        swapped = jnp.where(place >= len(WHOLE) + len(SPLIT), 1, 0)
        block = place * 2 + (ids % 2 + core + swapped) % 2
        rows.append((block * depth + slots[k]).astype(jnp.float32))
    place = jnp.concatenate(
        [picked[0] / total, picked[1] / total] + rows + [jnp.zeros((4, tokens), jnp.float32)],
        axis=0,
    )
    place_ref[...] = place.T
    term = jnp.dot(logit, input_ref[...], preferred_element_type=jnp.float32)
    term_ref[...] = term[:, None, :]


def weighted(cap, place_ref, blocks, first):
    tokens = place_ref.shape[0]
    depth, part = blocks[0].shape[1:]
    copies = jnp.concatenate([block.reshape(2 * depth, part) for block in blocks], axis=0)
    column = lax.broadcasted_iota(jnp.int32, (tokens, copies.shape[0]), 1) + first * depth
    gates = [place_ref[:, k : k + 1] for k in range(2)]
    base = [place_ref[:, 2 + k : 3 + k].astype(jnp.int32) for k in range(2)]
    quarters = []
    for q in range(QUARTERS):
        spread = jnp.where(column == base[0] + q * cap, gates[0], 0.0)
        spread = jnp.where(column == base[1] + q * cap, gates[1], spread)
        high = spread.astype(jnp.bfloat16)
        low = (spread - high.astype(jnp.float32)).astype(jnp.bfloat16)
        both = jnp.dot(
            jnp.concatenate([high, low], axis=0), copies, preferred_element_type=jnp.float32
        )
        quarters.append(both[:tokens] + both[tokens:])
    return quarters


def near_kernel(cap, place_ref, logit_ref, weight_ref, *refs):
    out_ref, near = refs[-1], refs[:-1]
    split = len(SPLIT)
    blocks = [ref[0:2] for ref in near[:split]] + [ref[2:4] for ref in near[split:]]
    part = out_ref.shape[1] // QUARTERS
    for q, total in enumerate(weighted(cap, place_ref, blocks, 2 * len(WHOLE))):
        columns = slice(q * part, (q + 1) * part)
        out_ref[:, columns] = total + dot_rows(logit_ref[...], weight_ref[:, columns])


def far_kernel(cap, place_ref, near_ref, *refs):
    out_ref = refs[-1]
    part = out_ref.shape[1] // QUARTERS
    for q, total in enumerate(weighted(cap, place_ref, [ref[...] for ref in refs[:-1]], 0)):
        columns = slice(q * part, (q + 1) * part)
        out_ref[:, columns] = (total + near_ref[:, columns]).astype(jnp.bfloat16)


def shards(side, layer_input, expert_ids, router_probs, router_weight, expert_grads, gate_dots):
    slots, width = expert_grads.shape[2:]
    tokens, experts = router_probs.shape[1:]
    windows = lax.axis_size("exp")
    chips = windows // 2
    cap = slots // windows
    part = width // QUARTERS
    depth = cap * QUARTERS
    params = pltpu.CompilerParams(vmem_limit_bytes=VMEM)

    def blocks_of(count):
        return jax.ShapeDtypeStruct((count, depth, part), jnp.bfloat16)

    def swap(block):
        return lax.ppermute(block, "exp", [(i, i ^ 1) for i in range(windows)])

    packed, given = pl.pallas_call(
        lambda *refs: pack_kernel(cap, *refs),
        out_shape=(blocks_of(windows), blocks_of(chips)),
        compiler_params=params,
    )(expert_grads[0, 0])
    got = swap(given)

    dealt = pl.pallas_call(
        deal_kernel,
        out_shape=(blocks_of(2),) * len(WHOLE) + (blocks_of(4),) * len(SPLIT),
        compiler_params=params,
    )(packed, got)
    far = [dealt[0]]
    for step, block in zip(WHOLE[1:], dealt[1:]):
        moves = [(i, (i + 2 * step) % windows) for i in range(windows)]
        far.append(lax.ppermute(block, "exp", moves))
    near = []
    for step, block in zip(SPLIT, dealt[len(WHOLE) :]):
        moves = [(i, (i + 2 * (step if i % 2 == 0 else -step)) % windows) for i in range(windows)]
        near.append(lax.ppermute(block, "exp", moves))

    laid = pl.pallas_call(
        lambda *refs: gate_pack_kernel(cap, *refs),
        out_shape=jax.ShapeDtypeStruct((windows, 1, LANES), jnp.float32),
        compiler_params=params,
    )(gate_dots[0])
    ids = jnp.swapaxes(expert_ids, 1, 2)[0]
    probs = jnp.swapaxes(router_probs, 1, 2)[0]

    def add(parts, count):
        return pl.pallas_call(
            sum_kernel,
            out_shape=jax.ShapeDtypeStruct((count, 1, width), jnp.float32),
            compiler_params=params,
        )(parts)

    router_out = (
        jax.ShapeDtypeStruct((experts, tokens), jnp.bfloat16),
        jax.ShapeDtypeStruct((tokens, 8), jnp.float32),
        jax.ShapeDtypeStruct((experts, 1, width), jnp.float32),
    )

    def over_exp(laid):
        dots = lax.all_to_all(laid, "exp", 0, 0, tiled=True)
        logit, place, term = pl.pallas_call(
            lambda *refs: router_kernel(depth, *refs),
            out_shape=router_out,
            compiler_params=params,
        )(ids, probs, dots, layer_input[0])
        return logit, place, add(lax.all_to_all(term, "exp", 0, 0, tiled=True), side)

    def over_ctx(operand):
        own, near = operand
        swapped = [swap(block) for block in near]
        across = [[x * side + z for x in range(side)] for z in range(side)]
        along = [[x * side + z for z in range(side)] for x in range(side)]
        for groups, count in ((across, side), (along, 1)):
            got = lax.all_to_all(own, "ctx", 0, 0, axis_index_groups=groups, tiled=True)
            own = add(got, count)
        return own, swapped

    runs = expert_ids[0, 0, 0] >= 0

    def unit(step, operand):
        out = jax.eval_shape(step, operand)
        empty = lambda _: jax.tree.map(lambda leaf: jnp.zeros(leaf.shape, leaf.dtype), out)
        return lax.cond(runs, step, empty, operand)

    laid, _ = lax.optimization_barrier((laid, dealt))
    logit, place, own = unit(over_exp, laid)
    own, swapped = unit(over_ctx, (own, near))
    near = near + swapped
    place, _ = lax.optimization_barrier((place, own))

    partial = pl.pallas_call(
        lambda *refs: near_kernel(cap, *refs),
        out_shape=jax.ShapeDtypeStruct((tokens, width), jnp.float32),
        compiler_params=params,
    )(place, logit, router_weight, *near)
    combined = pl.pallas_call(
        lambda *refs: far_kernel(cap, *refs),
        out_shape=jax.ShapeDtypeStruct((tokens, width), jnp.bfloat16),
        compiler_params=params,
    )(place, partial, *far)
    return combined[None], own[0]


def solution(mesh):
    in_specs = (
        P("exp", "ctx", None),
        P("exp", "ctx", None),
        P("exp", "ctx", None),
        P(),
        P("ctx", "exp", None, None),
        P("ctx", "exp", None),
    )
    out_specs = (P("exp", "ctx", None), P("exp", None))
    side = round(mesh.shape["ctx"] ** 0.5)

    def step(*arrays):
        return shards(side, *arrays)

    return jax.shard_map(step, mesh=mesh, in_specs=in_specs, out_specs=out_specs, check_vma=False)
```

time: 99.1 us -> 125 us (1.26)
  the two profiles are of different devices: /device:TPU:46 before, /device:TPU:1 now
where the time goes in v3:
time: 125 us; the launch traced here: 124 us
  blocking collectives  75.7 us (61%)
  starting transfers between devices  35.9 us (29%)
  Pallas kernels  6.77 us (5%)
  waiting for transfers between devices  2.19 us (2%)
  local copies, waits for them, and re-layouts  2.09 us (2%)
  between operations  1.49 us (1%)
    all_to_all x1, blocking collectives, over_exp(): dots = lax.all_to_all(laid, 'exp', 0, 0, tiled=True)  31.9 us
    all_to_all x2, blocking collectives, over_ctx(): got = lax.all_to_all(own, 'ctx', 0, 0, axis_index_groups=groups, tiled=True)  29.2 us
    ppermute x3, starting transfers between devices, swap(): return lax.ppermute(block, 'exp', [(i, i ^ 1) for i in range(windows)])  20.5 us
    all_to_all x1, blocking collectives, over_exp(): lax.all_to_all(term, 'exp', 0, 0, tiled=True)  14.5 us
    ppermute x3, starting transfers between devices, shards(): far.append(lax.ppermute(block, 'exp', moves))  11.4 us
    ppermute x2, starting transfers between devices, shards(): near.append(lax.ppermute(block, 'exp', moves))  3.97 us
    pallas_call x1, Pallas kernels, shards(): pl.pallas_call(lambda *refs: near_kernel(cap, *refs), out_shape=jax.Shape...  3.04 us
  transfers between devices with their start and end apart: 8, of which 1 were waited for; matrix products, arithmetic and copies ran while one was open for 0% of the time, Pallas kernels for 3%

profile of v3, /device:TPU:1, one launch (start us, length us, event | category | flops | bytes accessed | tf_op | source)
XLA Modules:
  0.0 124.2 jit_solution(4604799964357188294)
XLA Ops:
  0.6 1.5 %copy-done = bf16[1,1,320,3072]{3,2,1,0:T(8,128)(2,1)S(1)} copy-done((bf16[1,1,320,3072]{3,2,1,0:T(8,128)(2,1)S(1)}, bf16[1,1,320,3072]{3,2,1,0:T(8,128)(2,1)}, u32[]{:S(2)}) %copy-start) | copy-done | bytes 1966104
  2.2 0.5 shard_map.79
  2.7 0.0 copy-start.2
  2.7 16.2 %collective-permute-start.2 = (bf16[8,80,768]{2,1,0:T(8,128)(2,1)S(1)}, bf16[8,80,768]{2,1,0:T(8,128)(2,1)S(1)}, u32[]{:S(2)}, u32[]{:S(2)}) collective-permute-start(bf16[8,80,768]{2,1,0:T(8,128)(2,1)S(1)} %get-tuple-element.45), channel_id=1, source_target_pairs={{0,1},{1,0},{2,3},{3,2},{4,5},{5,4},{6,7},{7,6},{8,9},{9,8},{10,11... | collective-permute-start | bytes 2949128 | tf_op jit(solution)/shard_map/ppermute | solution.py:194
  18.9 2.2 %collective-permute-done.2.got_ref = bf16[8,80,768]{2,1,0:T(8,128)(2,1)S(1)} collective-permute-done((bf16[8,80,768]{2,1,0:T(8,128)(2,1)S(1)}, bf16[8,80,768]{2,1,0:T(8,128)(2,1)S(1)}, u32[]{:S(2)}, u32[]{:S(2)}) %collective-permute-start.2) | collective-permute-done | bytes 983072 | tf_op jit(solution)/shard_map/ppermute | solution.py:194
  21.1 0.1 shard_map.80
  21.2 2.1 %collective-permute-start.3 = (bf16[4,80,768]{2,1,0:T(8,128)(2,1)S(1)}, bf16[4,80,768]{2,1,0:T(8,128)(2,1)S(1)}, u32[]{:S(2)}, u32[]{:S(2)}) collective-permute-start(bf16[4,80,768]{2,1,0:T(8,128)(2,1)S(1)} %get-tuple-element.50), channel_id=1, source_target_pairs={{0,2},{1,15},{2,4},{3,1},{4,6},{5,3},{6,8},{7,5},{8,10},{9,7},{10,... | collective-permute-start | bytes 1474568 | tf_op jit(solution)/shard_map/ppermute | solution.py:215
  23.3 1.9 %collective-permute-start.4 = (bf16[4,80,768]{2,1,0:T(8,128)(2,1)S(1)}, bf16[4,80,768]{2,1,0:T(8,128)(2,1)}, u32[]{:S(2)}, u32[]{:S(2)}) collective-permute-start(bf16[4,80,768]{2,1,0:T(8,128)(2,1)S(1)} %get-tuple-element.51), channel_id=1, source_target_pairs={{0,4},{1,13},{2,6},{3,15},{4,8},{5,1},{6,10},{7,3},{8,12},{9,5},{1... | collective-permute-start | bytes 1474568 | tf_op jit(solution)/shard_map/ppermute | solution.py:215
  25.2 5.4 %collective-permute-start.5 = (bf16[2,80,768]{2,1,0:T(8,128)(2,1)S(1)}, bf16[2,80,768]{2,1,0:T(8,128)(2,1)S(1)}, u32[]{:S(2)}, u32[]{:S(2)}) collective-permute-start(bf16[2,80,768]{2,1,0:T(8,128)(2,1)S(1)} %get-tuple-element.47), channel_id=1, source_target_pairs={{0,6},{1,7},{2,8},{3,9},{4,10},{5,11},{6,12},{7,13},{8,14},{9,15},... | collective-permute-start | bytes 737288 | tf_op jit(solution)/shard_map/ppermute | solution.py:211
  30.7 2.9 %collective-permute-start.6 = (bf16[2,80,768]{2,1,0:T(8,128)(2,1)S(1)}, bf16[2,80,768]{2,1,0:T(8,128)(2,1)S(1)}, u32[]{:S(2)}, u32[]{:S(2)}) collective-permute-start(bf16[2,80,768]{2,1,0:T(8,128)(2,1)S(1)} %get-tuple-element.48), channel_id=1, source_target_pairs={{0,10},{1,11},{2,12},{3,13},{4,14},{5,15},{6,0},{7,1},{8,2},{9,3},... | collective-permute-start | bytes 737288 | tf_op jit(solution)/shard_map/ppermute | solution.py:211
  33.5 3.1 %collective-permute-start.7 = (bf16[2,80,768]{2,1,0:T(8,128)(2,1)S(1)}, bf16[2,80,768]{2,1,0:T(8,128)(2,1)S(1)}, u32[]{:S(2)}, u32[]{:S(2)}) collective-permute-start(bf16[2,80,768]{2,1,0:T(8,128)(2,1)S(1)} %get-tuple-element.49), channel_id=1, source_target_pairs={{0,8},{1,9},{2,10},{3,11},{4,12},{5,13},{6,14},{7,15},{8,0},{9,1},... | collective-permute-start | bytes 737288 | tf_op jit(solution)/shard_map/ppermute | solution.py:211
  36.6 0.2 shard_map.78
  36.8 0.5 slice.3
  38.0 47.0 %conditional.2 = (bf16[16,128]{1,0:T(8,128)(2,1)S(1)}, f32[128,8]{1,0:T(8,128)S(1)}, f32[8,1,3072]{2,1,0:T(1,128)S(1)}) conditional(s32[]{:T(128)} %bitcast.3, () %tuple.26, (s32[1,2,128]{2,1,0:T(2,128)S(1)}, f32[1,16,128]{2,1,0:T(8,128)S(1)}, f32[16,1,128]{2,1,0:T(1,128)S(1)}, bf16[1,128,3072]{2,1,0:T(8,128)(2,1)S(1)}) %tuple.39), branch_computations={%region_0.0_spmd, %region_1.0_spmd} | conditional | bytes 409624 | solution.py:262
  38.0 31.9 %all_to_all.16.refs_2_ = f32[16,1,128]{2,1,0:T(1,128)S(1)} all-to-all(f32[16,1,128]{2,1,0:T(1,128)S(1)} %get-tuple-element.18), channel_id=1, replica_groups=mesh['ctx'=64,'exp'=16] {'exp'}, dimensions={0} | all-to-all | bytes 16384 | tf_op jit(solution)/shard_map/cond/branch_1_fun/all_to_all | solution.py:239
  70.0 0.4 branch_1_fun.4
  70.4 14.5 %all_to_all.17.parts_ref = f32[16,1,3072]{2,1,0:T(1,128)S(1)} all-to-all(f32[16,1,3072]{2,1,0:T(1,128)S(1)} %get-tuple-element.22), channel_id=1, replica_groups=mesh['ctx'=64,'exp'=16] {'exp'}, dimensions={0} | all-to-all | bytes 393216 | tf_op jit(solution)/shard_map/cond/branch_1_fun/all_to_all | solution.py:245
  85.0 33.6 %conditional.3 = (f32[1,1,3072]{2,1,0:T(1,128)S(1)}, bf16[4,80,768]{2,1,0:T(8,128)(2,1)}, bf16[4,80,768]{2,1,0:T(8,128)(2,1)}) conditional(s32[]{:T(128)} %bitcast.3, () %tuple.29, (f32[8,1,3072]{2,1,0:T(1,128)S(1)}, bf16[4,80,768]{2,1,0:T(8,128)(2,1)S(1)}, bf16[4,80,768]{2,1,0:T(8,128)(2,1)}) %tuple.30), branch_computations={%region_2.0_spmd, %region_3.0_spmd} | conditional | bytes 4325480 | solution.py:262
  85.0 1.9 %collective-permute-start = (bf16[4,80,768]{2,1,0:T(8,128)(2,1)S(1)}, bf16[4,80,768]{2,1,0:T(8,128)(2,1)}, u32[]{:S(2)}, u32[]{:S(2)}) collective-permute-start(bf16[4,80,768]{2,1,0:T(8,128)(2,1)S(1)} %get-tuple-element.24), channel_id=1, source_target_pairs={{0,1},{1,0},{2,3},{3,2},{4,5},{5,4},{6,7},{7,6},{8,9},{9,8},{10,11... | collective-permute-start | bytes 1474568 | tf_op jit(solution)/shard_map/cond/branch_1_fun/ppermute | solution.py:194
  87.0 2.4 %collective-permute-start.1 = (bf16[4,80,768]{2,1,0:T(8,128)(2,1)}, bf16[4,80,768]{2,1,0:T(8,128)(2,1)}, u32[]{:S(2)}, u32[]{:S(2)}) collective-permute-start(bf16[4,80,768]{2,1,0:T(8,128)(2,1)} %get-tuple-element.25), channel_id=1, source_target_pairs={{0,1},{1,0},{2,3},{3,2},{4,5},{5,4},{6,7},{7,6},{8,9},{9,8},{10,11... | collective-permute-start | bytes 1474568 | tf_op jit(solution)/shard_map/cond/branch_1_fun/ppermute | solution.py:194
  89.4 10.5 %all_to_all.18.parts_ref = f32[8,1,3072]{2,1,0:T(1,128)S(1)} all-to-all(f32[8,1,3072]{2,1,0:T(1,128)S(1)} %get-tuple-element.23), channel_id=1, replica_groups={{0,128,256,384,512,640,768,896},{16,144,272,400,528,656,784,912},{32,16..., dimensions={0} | all-to-all | bytes 196608 | tf_op jit(solution)/shard_map/cond/branch_1_fun/all_to_all | solution.py:253
  99.9 18.7 %all_to_all.19.parts_ref = f32[8,1,3072]{2,1,0:T(1,128)S(1)} all-to-all(f32[8,1,3072]{2,1,0:T(1,128)S(1)} %branch_1_fun.6), channel_id=1, replica_groups={{0,16,32,48,64,80,96,112},{128,144,160,176,192,208,224,240},{256,272,28..., dimensions={0} | all-to-all | bytes 196608 | tf_op jit(solution)/shard_map/cond/branch_1_fun/all_to_all | solution.py:253
  118.6 3.0 %shard_map.81.refs_1_ = f32[128,3072]{1,0:T(8,128)S(1)} custom-call(f32[128,8]{1,0:T(8,128)S(1)} %get-tuple-element.56.refs_0_, bf16[16,128]{1,0:T(8,128)(2,1)S(1)} %get-tuple-element.57.refs_1_, bf16[16,3072]{1,0:T(8,128)(2,1)S(1)} %copy-done.1, bf16[4,80,768]{2,1,0:T(8,128)(2,1)S(1)} %collective-permute-done.3.refs_3_, ...), custom_call_target="tpu_custom_call" | custom-call | tf_op jit(solution)/shard_map/pallas_call | solution.py:270
  121.7 2.4 %shard_map.82 = bf16[128,3072]{1,0:T(8,128)(2,1)} custom-call(f32[128,8]{1,0:T(8,128)S(1)} %get-tuple-element.56.refs_0_, f32[128,3072]{1,0:T(8,128)S(1)} %shard_map.81.refs_1_, bf16[2,80,768]{2,1,0:T(8,128)(2,1)S(1)} %get-tuple-element.46.refs_2_, bf16[2,80,768]{2,1,0:T(8,128)(2,1)S(1)} %collective-permute-done.5.refs_3_, ...), custom_call_target="tpu_custom_call" | custom-call | tf_op jit(solution)/shard_map/pallas_call | solution.py:275
  (22 shorter events, 0.1 us)
Async XLA Ops:
  0.6 1.5 %copy-start = (bf16[1,1,320,3072]{3,2,1,0:T(8,128)(2,1)S(1)}, bf16[1,1,320,3072]{3,2,1,0:T(8,128)(2,1)}, u32[]{:S(2)}) copy-start(bf16[1,1,320,3072]{3,2,1,0:T(8,128)(2,1)} %param.14) | copy-start | bytes 5898244
  2.7 34.0 %copy-start.2 = (bf16[1,1,320]{2,1,0:T(2,128)(2,1)S(1)}, bf16[1,1,320]{2,1,0:T(2,128)(2,1)}, u32[]{:S(2)}) copy-start(bf16[1,1,320]{2,1,0:T(2,128)(2,1)} %param.15) | copy-start | bytes 1924
  2.7 34.2 %copy-start.6 = (s32[1,128,2]{1,2,0:T(2,128)S(1)}, s32[1,128,2]{1,2,0:T(2,128)}, u32[]{:S(2)}) copy-start(s32[1,128,2]{1,2,0:T(2,128)} %param.11) | copy-start | bytes 3076
  2.7 35.3 %copy-start.3 = (bf16[1,128,3072]{2,1,0:T(8,128)(2,1)S(1)}, bf16[1,128,3072]{2,1,0:T(8,128)(2,1)}, u32[]{:S(2)}) copy-start(bf16[1,128,3072]{2,1,0:T(8,128)(2,1)} %param.10) | copy-start | bytes 2359300
  2.7 35.3 %copy-start.5 = (f32[1,128,16]{1,2,0:T(8,128)S(1)}, f32[1,128,16]{1,2,0:T(8,128)}, u32[]{:S(2)}) copy-start(f32[1,128,16]{1,2,0:T(8,128)} %param.12) | copy-start | bytes 24580
  2.7 18.4 %collective-permute-start.2 = (bf16[8,80,768]{2,1,0:T(8,128)(2,1)S(1)}, bf16[8,80,768]{2,1,0:T(8,128)(2,1)S(1)}, u32[]{:S(2)}, u32[]{:S(2)}) collective-permute-start(bf16[8,80,768]{2,1,0:T(8,128)(2,1)S(1)} %get-tuple-element.45), channel_id=1, source_target_pairs={{0,1},{1,0},{2,3},{3,2},{4,5},{5,4},{6,7},{7,6},{8,9},{9,8},{10,11... | collective-permute-start | bytes 2949128 | tf_op jit(solution)/shard_map/ppermute | solution.py:194
  21.2 97.4 %copy-start.1 = (bf16[16,3072]{1,0:T(8,128)(2,1)S(1)}, bf16[16,3072]{1,0:T(8,128)(2,1)}, u32[]{:S(2)}) copy-start(bf16[16,3072]{1,0:T(8,128)(2,1)} %refs_2_.1) | copy-start | bytes 294916
  21.2 63.8 %collective-permute-start.3 = (bf16[4,80,768]{2,1,0:T(8,128)(2,1)S(1)}, bf16[4,80,768]{2,1,0:T(8,128)(2,1)S(1)}, u32[]{:S(2)}, u32[]{:S(2)}) collective-permute-start(bf16[4,80,768]{2,1,0:T(8,128)(2,1)S(1)} %get-tuple-element.50), channel_id=1, source_target_pairs={{0,2},{1,15},{2,4},{3,1},{4,6},{5,3},{6,8},{7,5},{8,10},{9,7},{10,... | collective-permute-start | bytes 1474568 | tf_op jit(solution)/shard_map/ppermute | solution.py:215
  23.3 61.7 %collective-permute-start.4 = (bf16[4,80,768]{2,1,0:T(8,128)(2,1)S(1)}, bf16[4,80,768]{2,1,0:T(8,128)(2,1)}, u32[]{:S(2)}, u32[]{:S(2)}) collective-permute-start(bf16[4,80,768]{2,1,0:T(8,128)(2,1)S(1)} %get-tuple-element.51), channel_id=1, source_target_pairs={{0,4},{1,13},{2,6},{3,15},{4,8},{5,1},{6,10},{7,3},{8,12},{9,5},{1... | collective-permute-start | bytes 1474568 | tf_op jit(solution)/shard_map/ppermute | solution.py:215
  25.2 96.5 %collective-permute-start.5 = (bf16[2,80,768]{2,1,0:T(8,128)(2,1)S(1)}, bf16[2,80,768]{2,1,0:T(8,128)(2,1)S(1)}, u32[]{:S(2)}, u32[]{:S(2)}) collective-permute-start(bf16[2,80,768]{2,1,0:T(8,128)(2,1)S(1)} %get-tuple-element.47), channel_id=1, source_target_pairs={{0,6},{1,7},{2,8},{3,9},{4,10},{5,11},{6,12},{7,13},{8,14},{9,15},... | collective-permute-start | bytes 737288 | tf_op jit(solution)/shard_map/ppermute | solution.py:211
  30.7 91.1 %collective-permute-start.6 = (bf16[2,80,768]{2,1,0:T(8,128)(2,1)S(1)}, bf16[2,80,768]{2,1,0:T(8,128)(2,1)S(1)}, u32[]{:S(2)}, u32[]{:S(2)}) collective-permute-start(bf16[2,80,768]{2,1,0:T(8,128)(2,1)S(1)} %get-tuple-element.48), channel_id=1, source_target_pairs={{0,10},{1,11},{2,12},{3,13},{4,14},{5,15},{6,0},{7,1},{8,2},{9,3},... | collective-permute-start | bytes 737288 | tf_op jit(solution)/shard_map/ppermute | solution.py:211
  33.5 88.2 %collective-permute-start.7 = (bf16[2,80,768]{2,1,0:T(8,128)(2,1)S(1)}, bf16[2,80,768]{2,1,0:T(8,128)(2,1)S(1)}, u32[]{:S(2)}, u32[]{:S(2)}) collective-permute-start(bf16[2,80,768]{2,1,0:T(8,128)(2,1)S(1)} %get-tuple-element.49), channel_id=1, source_target_pairs={{0,8},{1,9},{2,10},{3,11},{4,12},{5,13},{6,14},{7,15},{8,0},{9,1},... | collective-permute-start | bytes 737288 | tf_op jit(solution)/shard_map/ppermute | solution.py:211
  85.0 33.6 %collective-permute-start = (bf16[4,80,768]{2,1,0:T(8,128)(2,1)S(1)}, bf16[4,80,768]{2,1,0:T(8,128)(2,1)}, u32[]{:S(2)}, u32[]{:S(2)}) collective-permute-start(bf16[4,80,768]{2,1,0:T(8,128)(2,1)S(1)} %get-tuple-element.24), channel_id=1, source_target_pairs={{0,1},{1,0},{2,3},{3,2},{4,5},{5,4},{6,7},{7,6},{8,9},{9,8},{10,11... | collective-permute-start | bytes 1474568 | tf_op jit(solution)/shard_map/cond/branch_1_fun/ppermute | solution.py:194
  87.0 31.7 %collective-permute-start.1 = (bf16[4,80,768]{2,1,0:T(8,128)(2,1)}, bf16[4,80,768]{2,1,0:T(8,128)(2,1)}, u32[]{:S(2)}, u32[]{:S(2)}) collective-permute-start(bf16[4,80,768]{2,1,0:T(8,128)(2,1)} %get-tuple-element.25), channel_id=1, source_target_pairs={{0,1},{1,0},{2,3},{3,2},{4,5},{5,4},{6,7},{7,6},{8,9},{9,8},{10,11... | collective-permute-start | bytes 1474568 | tf_op jit(solution)/shard_map/cond/branch_1_fun/ppermute | solution.py:194
  118.6 5.5 %copy-start.4 = (f32[1,1,3072]{2,1,0:T(1,128)}, f32[1,1,3072]{2,1,0:T(1,128)S(1)}, u32[]{:S(2)}) copy-start(f32[1,1,3072]{2,1,0:T(1,128)S(1)} %get-tuple-element.55) | copy-start | bytes 36868

commit v4 on v3

--- a/solution.py
+++ b/solution.py
@@ -7,7 +7,7 @@
 
 QUARTERS = 4
 LANES = 128
-WHOLE = (0, 3, 5, 4)
+WHOLE = (3, 5, 4, 0)
 SPLIT = (1, 2)
 VMEM = 24 * 1024 * 1024
 
@@ -160,11 +160,12 @@
 
 
 def near_kernel(cap, place_ref, logit_ref, weight_ref, *refs):
-    out_ref, near = refs[-1], refs[:-1]
+    out_ref, local_ref, near = refs[-1], refs[0], refs[1:-1]
     split = len(SPLIT)
-    blocks = [ref[0:2] for ref in near[:split]] + [ref[2:4] for ref in near[split:]]
+    blocks = [local_ref[...]]
+    blocks += [ref[0:2] for ref in near[:split]] + [ref[2:4] for ref in near[split:]]
     part = out_ref.shape[1] // QUARTERS
-    for q, total in enumerate(weighted(cap, place_ref, blocks, 2 * len(WHOLE))):
+    for q, total in enumerate(weighted(cap, place_ref, blocks, 2 * len(WHOLE) - 2)):
         columns = slice(q * part, (q + 1) * part)
         out_ref[:, columns] = total + dot_rows(logit_ref[...], weight_ref[:, columns])
 
@@ -193,20 +194,27 @@
     def swap(block):
         return lax.ppermute(block, "exp", [(i, i ^ 1) for i in range(windows)])
 
+    laid = pl.pallas_call(
+        lambda *refs: gate_pack_kernel(cap, *refs),
+        out_shape=jax.ShapeDtypeStruct((windows, 1, LANES), jnp.float32),
+        compiler_params=params,
+    )(gate_dots[0])
+    dots = lax.all_to_all(laid, "exp", 0, 0, tiled=True)
+
     packed, given = pl.pallas_call(
         lambda *refs: pack_kernel(cap, *refs),
         out_shape=(blocks_of(windows), blocks_of(chips)),
         compiler_params=params,
     )(expert_grads[0, 0])
-    got = swap(given)
+    got, dots = lax.optimization_barrier((swap(given), dots))
 
     dealt = pl.pallas_call(
         deal_kernel,
         out_shape=(blocks_of(2),) * len(WHOLE) + (blocks_of(4),) * len(SPLIT),
         compiler_params=params,
     )(packed, got)
-    far = [dealt[0]]
-    for step, block in zip(WHOLE[1:], dealt[1:]):
+    far = []
+    for step, block in zip(WHOLE[:-1], dealt):
         moves = [(i, (i + 2 * step) % windows) for i in range(windows)]
         far.append(lax.ppermute(block, "exp", moves))
     near = []
@@ -214,11 +222,6 @@
         moves = [(i, (i + 2 * (step if i % 2 == 0 else -step)) % windows) for i in range(windows)]
         near.append(lax.ppermute(block, "exp", moves))
 
-    laid = pl.pallas_call(
-        lambda *refs: gate_pack_kernel(cap, *refs),
-        out_shape=jax.ShapeDtypeStruct((windows, 1, LANES), jnp.float32),
-        compiler_params=params,
-    )(gate_dots[0])
     ids = jnp.swapaxes(expert_ids, 1, 2)[0]
     probs = jnp.swapaxes(router_probs, 1, 2)[0]
 
@@ -235,8 +238,7 @@
         jax.ShapeDtypeStruct((experts, 1, width), jnp.float32),
     )
 
-    def over_exp(laid):
-        dots = lax.all_to_all(laid, "exp", 0, 0, tiled=True)
+    def over_exp(dots):
         logit, place, term = pl.pallas_call(
             lambda *refs: router_kernel(depth, *refs),
             out_shape=router_out,
@@ -245,14 +247,19 @@
         return logit, place, add(lax.all_to_all(term, "exp", 0, 0, tiled=True), side)
 
     def over_ctx(operand):
-        own, near = operand
+        own, near, *routed = operand
         swapped = [swap(block) for block in near]
+        partial = pl.pallas_call(
+            lambda *refs: near_kernel(cap, *refs),
+            out_shape=jax.ShapeDtypeStruct((tokens, width), jnp.float32),
+            compiler_params=params,
+        )(*routed, router_weight, dealt[len(WHOLE) - 1], *near, *swapped)
         across = [[x * side + z for x in range(side)] for z in range(side)]
         along = [[x * side + z for z in range(side)] for x in range(side)]
         for groups, count in ((across, side), (along, 1)):
             got = lax.all_to_all(own, "ctx", 0, 0, axis_index_groups=groups, tiled=True)
             own = add(got, count)
-        return own, swapped
+        return own, partial
 
     runs = expert_ids[0, 0, 0] >= 0
 
@@ -261,17 +268,8 @@
         empty = lambda _: jax.tree.map(lambda leaf: jnp.zeros(leaf.shape, leaf.dtype), out)
         return lax.cond(runs, step, empty, operand)
 
-    laid, _ = lax.optimization_barrier((laid, dealt))
-    logit, place, own = unit(over_exp, laid)
-    own, swapped = unit(over_ctx, (own, near))
-    near = near + swapped
-    place, _ = lax.optimization_barrier((place, own))
-
-    partial = pl.pallas_call(
-        lambda *refs: near_kernel(cap, *refs),
-        out_shape=jax.ShapeDtypeStruct((tokens, width), jnp.float32),
-        compiler_params=params,
-    )(place, logit, router_weight, *near)
+    logit, place, own = over_exp(dots)
+    own, partial = unit(over_ctx, (own, near, place, logit))
     combined = pl.pallas_call(
         lambda *refs: far_kernel(cap, *refs),
         out_shape=jax.ShapeDtypeStruct((tokens, width), jnp.bfloat16),

time: 125 us -> 110 us (0.88)
  blocking collectives: 75.7 us -> 39.4 us
  starting transfers between devices: 35.9 us -> 47.7 us
  waiting for transfers between devices: 2.19 us -> 9.42 us
    all_to_all x2 -> x1, blocking collectives: 46.5 us -> 9.46 us  [shards(): dots = lax.all_to_all(laid, 'exp', 0, 0, tiled=True)]
    all_to_all x0 -> x1, waiting for transfers between devices: none -> 9.4 us  [over_exp(): lax.all_to_all(term, 'exp', 0, 0, tiled=True)]
    all_to_all x0 -> x1, starting transfers between devices: none -> 6.97 us  [over_exp(): lax.all_to_all(term, 'exp', 0, 0, tiled=True)]
    ppermute x3, starting transfers between devices: 11.4 us -> 15.5 us  [shards(): far.append(lax.ppermute(block, 'exp', moves))]
    ppermute x3, waiting for transfers between devices: 2.18 us -> 0.01 us  [swap(): return lax.ppermute(block, 'exp', [(i, i ^ 1) for i in range(windows)])]
  transfers between devices with their start and end apart: 8 -> 9, of which waited for: 1 -> 1; matrix products, arithmetic and copies ran while one was open for 0% -> 0% of each run, Pallas kernels for 3% -> 4%
where the time goes in v4:
time: 110 us; the launch traced here: 108 us
  starting transfers between devices  47.7 us (43%)
  blocking collectives  39.4 us (36%)
  waiting for transfers between devices  9.42 us (9%)
  Pallas kernels  8.01 us (7%)
  local copies, waits for them, and re-layouts  2.09 us (2%)
  between operations  1.48 us (1%)
    all_to_all x2, blocking collectives, over_ctx(): got = lax.all_to_all(own, 'ctx', 0, 0, axis_index_groups=groups, tiled=True)  29.9 us
    ppermute x3, starting transfers between devices, swap(): return lax.ppermute(block, 'exp', [(i, i ^ 1) for i in range(windows)])  20.9 us
    ppermute x3, starting transfers between devices, shards(): far.append(lax.ppermute(block, 'exp', moves))  15.5 us
    all_to_all x1, blocking collectives, shards(): dots = lax.all_to_all(laid, 'exp', 0, 0, tiled=True)  9.46 us
    all_to_all x1, waiting for transfers between devices, over_exp(): lax.all_to_all(term, 'exp', 0, 0, tiled=True)  9.4 us
    all_to_all x1, starting transfers between devices, over_exp(): lax.all_to_all(term, 'exp', 0, 0, tiled=True)  6.97 us
    ppermute x2, starting transfers between devices, shards(): near.append(lax.ppermute(block, 'exp', moves))  4.39 us
    pallas_call x1, Pallas kernels, over_ctx(): pl.pallas_call(lambda *refs: near_kernel(cap, *refs), out_shape=jax.Shape...  3.32 us
  transfers between devices with their start and end apart: 9, of which 1 were waited for; matrix products, arithmetic and copies ran while one was open for 0% of the time, Pallas kernels for 4%

profile of v4, /device:TPU:1, one launch (start us, length us, event | category | flops | bytes accessed | tf_op | source)
XLA Modules:
  0.0 108.2 jit_solution(5125720506134366160)
XLA Ops:
  0.6 1.5 %copy-done = bf16[1,1,320,3072]{3,2,1,0:T(8,128)(2,1)S(1)} copy-done((bf16[1,1,320,3072]{3,2,1,0:T(8,128)(2,1)S(1)}, bf16[1,1,320,3072]{3,2,1,0:T(8,128)(2,1)}, u32[]{:S(2)}) %copy-start) | copy-done | bytes 1966104
  2.2 0.5 shard_map.78
  2.7 0.0 copy-start.1
  2.7 16.2 %collective-permute-start.2 = (bf16[8,80,768]{2,1,0:T(8,128)(2,1)S(1)}, bf16[8,80,768]{2,1,0:T(8,128)(2,1)S(1)}, u32[]{:S(2)}, u32[]{:S(2)}) collective-permute-start(bf16[8,80,768]{2,1,0:T(8,128)(2,1)S(1)} %get-tuple-element.39), channel_id=1, source_target_pairs={{0,1},{1,0},{2,3},{3,2},{4,5},{5,4},{6,7},{7,6},{8,9},{9,8},{10,11... | collective-permute-start | bytes 2949128 | tf_op jit(solution)/shard_map/ppermute | solution.py:195
  18.9 0.2 shard_map.79
  19.1 9.5 %all_to_all.20.refs_2_ = f32[16,1,128]{2,1,0:T(1,128)S(1)} all-to-all(f32[16,1,128]{2,1,0:T(1,128)S(1)} %shard_map.79), channel_id=1, replica_groups=mesh['ctx'=64,'exp'=16] {'exp'}, dimensions={0} | all-to-all | bytes 16384 | tf_op jit(solution)/shard_map/all_to_all | solution.py:202
  28.6 0.8 shard_map.81
  29.4 2.2 %collective-permute-start.3 = (bf16[4,80,768]{2,1,0:T(8,128)(2,1)S(1)}, bf16[4,80,768]{2,1,0:T(8,128)(2,1)S(1)}, u32[]{:S(2)}, u32[]{:S(2)}) collective-permute-start(bf16[4,80,768]{2,1,0:T(8,128)(2,1)S(1)} %get-tuple-element.44), channel_id=1, source_target_pairs={{0,2},{1,15},{2,4},{3,1},{4,6},{5,3},{6,8},{7,5},{8,10},{9,7},{10,... | collective-permute-start | bytes 1474568 | tf_op jit(solution)/shard_map/ppermute | solution.py:223
  31.6 2.2 %collective-permute-start.4 = (bf16[4,80,768]{2,1,0:T(8,128)(2,1)S(1)}, bf16[4,80,768]{2,1,0:T(8,128)(2,1)}, u32[]{:S(2)}, u32[]{:S(2)}) collective-permute-start(bf16[4,80,768]{2,1,0:T(8,128)(2,1)S(1)} %get-tuple-element.45), channel_id=1, source_target_pairs={{0,4},{1,13},{2,6},{3,15},{4,8},{5,1},{6,10},{7,3},{8,12},{9,5},{1... | collective-permute-start | bytes 1474568 | tf_op jit(solution)/shard_map/ppermute | solution.py:223
  33.8 1.1 %shard_map.80 = (bf16[16,128]{1,0:T(8,128)(2,1)S(1)}, f32[128,8]{1,0:T(8,128)S(1)}, f32[16,1,3072]{2,1,0:T(1,128)}) custom-call(s32[2,128]{1,0:T(2,128)S(1)} %bitcast.16, f32[16,128]{1,0:T(8,128)S(1)} %bitcast.14, f32[16,1,128]{2,1,0:T(1,128)S(1)} %all_to_all.20.refs_2_, bf16[128,3072]{1,0:T(8,128)(2,1)S(1)} %bitcast.13), custom_call_target="tpu_custom_call" | custom-call | tf_op jit(solution)/shard_map/pallas_call | solution.py:242
  35.0 7.0 %all-to-all-start.3 = ((f32[16,1,3072]{2,1,0:T(1,128)}), f32[16,1,3072]{2,1,0:T(1,128)S(1)}, u32[]{:S(2)}, u32[]{:S(2)}) async-start(f32[16,1,3072]{2,1,0:T(1,128)} %get-tuple-element.48), calls=%async_computation.3 | async-start | bytes 393216 | tf_op jit(solution)/shard_map/all_to_all | solution.py:247
  41.9 5.1 %collective-permute-start.5 = (bf16[2,80,768]{2,1,0:T(8,128)(2,1)S(1)}, bf16[2,80,768]{2,1,0:T(8,128)(2,1)S(1)}, u32[]{:S(2)}, u32[]{:S(2)}) collective-permute-start(bf16[2,80,768]{2,1,0:T(8,128)(2,1)S(1)} %get-tuple-element.50), channel_id=1, source_target_pairs={{0,6},{1,7},{2,8},{3,9},{4,10},{5,11},{6,12},{7,13},{8,14},{9,15},... | collective-permute-start | bytes 737288 | tf_op jit(solution)/shard_map/ppermute | solution.py:219
  47.0 3.2 %collective-permute-start.6 = (bf16[2,80,768]{2,1,0:T(8,128)(2,1)S(1)}, bf16[2,80,768]{2,1,0:T(8,128)(2,1)S(1)}, u32[]{:S(2)}, u32[]{:S(2)}) collective-permute-start(bf16[2,80,768]{2,1,0:T(8,128)(2,1)S(1)} %get-tuple-element.51), channel_id=1, source_target_pairs={{0,10},{1,11},{2,12},{3,13},{4,14},{5,15},{6,0},{7,1},{8,2},{9,3},... | collective-permute-start | bytes 737288 | tf_op jit(solution)/shard_map/ppermute | solution.py:219
  50.3 7.2 %collective-permute-start.7 = (bf16[2,80,768]{2,1,0:T(8,128)(2,1)S(1)}, bf16[2,80,768]{2,1,0:T(8,128)(2,1)S(1)}, u32[]{:S(2)}, u32[]{:S(2)}) collective-permute-start(bf16[2,80,768]{2,1,0:T(8,128)(2,1)S(1)} %get-tuple-element.52), channel_id=1, source_target_pairs={{0,8},{1,9},{2,10},{3,11},{4,12},{5,13},{6,14},{7,15},{8,0},{9,1},... | collective-permute-start | bytes 737288 | tf_op jit(solution)/shard_map/ppermute | solution.py:219
  57.5 0.5 slice.3
  58.6 9.4 %all-to-all-done.3.parts_ref = f32[16,1,3072]{2,1,0:T(1,128)S(1)} async-done(((f32[16,1,3072]{2,1,0:T(1,128)}), f32[16,1,3072]{2,1,0:T(1,128)S(1)}, u32[]{:S(2)}, u32[]{:S(2)}) %all-to-all-start.3) | async-done | bytes 196640 | tf_op jit(solution)/shard_map/all_to_all | solution.py:247
  68.1 38.0 %conditional.1 = (f32[128,3072]{1,0:T(8,128)S(1)}, f32[1,3072]{1,0:T(1,128)S(1)}) conditional(s32[]{:T(128)} %bitcast.8, () %tuple.20, (bf16[4,80,768]{2,1,0:T(8,128)(2,1)S(1)}, bf16[4,80,768]{2,1,0:T(8,128)(2,1)}, f32[128,8]{1,0:T(8,128)S(1)}, bf16[16,128]{1,0:T(8,128)(2,1)S(1)}, bf16[16,3072]{1,0:T(8,128)(2,1)S(1)}, ...), branch_computations={%region_0.0_spmd, %region_1.0_spmd} | conditional | bytes 4325472 | solution.py:269
  68.1 2.8 %collective-permute-start = (bf16[4,80,768]{2,1,0:T(8,128)(2,1)S(1)}, bf16[4,80,768]{2,1,0:T(8,128)(2,1)S(1)}, u32[]{:S(2)}, u32[]{:S(2)}) collective-permute-start(bf16[4,80,768]{2,1,0:T(8,128)(2,1)S(1)} %get-tuple-element.19.refs_4_), channel_id=1, source_target_pairs={{0,1},{1,0},{2,3},{3,2},{4,5},{5,4},{6,7},{7,6},{8,9},{9,8},{10,11... | collective-permute-start | bytes 1474568 | tf_op jit(solution)/shard_map/cond/branch_1_fun/ppermute | solution.py:195
  70.9 1.9 %collective-permute-start.1 = (bf16[4,80,768]{2,1,0:T(8,128)(2,1)}, bf16[4,80,768]{2,1,0:T(8,128)(2,1)S(1)}, u32[]{:S(2)}, u32[]{:S(2)}) collective-permute-start(bf16[4,80,768]{2,1,0:T(8,128)(2,1)} %get-tuple-element.20.refs_5_), channel_id=1, source_target_pairs={{0,1},{1,0},{2,3},{3,2},{4,5},{5,4},{6,7},{7,6},{8,9},{9,8},{10,11... | collective-permute-start | bytes 1474568 | tf_op jit(solution)/shard_map/cond/branch_1_fun/ppermute | solution.py:195
  72.8 9.8 %all_to_all.18.parts_ref = f32[8,1,3072]{2,1,0:T(1,128)S(1)} all-to-all(f32[8,1,3072]{2,1,0:T(1,128)S(1)} %get-tuple-element.21), channel_id=1, replica_groups={{0,128,256,384,512,640,768,896},{16,144,272,400,528,656,784,912},{32,16..., dimensions={0} | all-to-all | bytes 196608 | tf_op jit(solution)/shard_map/cond/branch_1_fun/all_to_all | solution.py:260
  82.6 20.1 %all_to_all.19.parts_ref = f32[8,1,3072]{2,1,0:T(1,128)S(1)} all-to-all(f32[8,1,3072]{2,1,0:T(1,128)S(1)} %branch_1_fun.4), channel_id=1, replica_groups={{0,16,32,48,64,80,96,112},{128,144,160,176,192,208,224,240},{256,272,28..., dimensions={0} | all-to-all | bytes 196608 | tf_op jit(solution)/shard_map/cond/branch_1_fun/all_to_all | solution.py:260
  102.8 3.3 %branch_1_fun.3 = f32[128,3072]{1,0:T(8,128)S(1)} custom-call(f32[128,8]{1,0:T(8,128)S(1)} %get-tuple-element.15.refs_0_, bf16[16,128]{1,0:T(8,128)(2,1)S(1)} %get-tuple-element.16.refs_1_, bf16[16,3072]{1,0:T(8,128)(2,1)S(1)} %get-tuple-element.55.refs_2_, bf16[2,80,768]{2,1,0:T(8,128)(2,1)} %get-tuple-element.18.refs_3_, ...), custom_call_target="tpu_custom_call" | custom-call | tf_op jit(solution)/shard_map/cond/branch_1_fun/pallas_call | solution.py:252
  106.1 0.0 copy-start.6
  106.2 2.0 %shard_map.83 = bf16[128,3072]{1,0:T(8,128)(2,1)} custom-call(f32[128,8]{1,0:T(8,128)S(1)} %get-tuple-element.41.refs_0_, f32[128,3072]{1,0:T(8,128)S(1)} %get-tuple-element.49.refs_1_, bf16[2,80,768]{2,1,0:T(8,128)(2,1)S(1)} %collective-permute-done.5.refs_2_, bf16[2,80,768]{2,1,0:T(8,128)(2,1)S(1)} %collective-permute-done.6.refs_3_, ...), custom_call_target="tpu_custom_call" | custom-call | tf_op jit(solution)/shard_map/pallas_call | solution.py:273
  (22 shorter events, 0.1 us)
Async XLA Ops:
  0.6 18.3 %copy-start.3 = (bf16[1,1,320]{2,1,0:T(2,128)(2,1)S(1)}, bf16[1,1,320]{2,1,0:T(2,128)(2,1)}, u32[]{:S(2)}) copy-start(bf16[1,1,320]{2,1,0:T(2,128)(2,1)} %param.13) | copy-start | bytes 1924
  0.6 1.6 %copy-start = (bf16[1,1,320,3072]{3,2,1,0:T(8,128)(2,1)S(1)}, bf16[1,1,320,3072]{3,2,1,0:T(8,128)(2,1)}, u32[]{:S(2)}) copy-start(bf16[1,1,320,3072]{3,2,1,0:T(8,128)(2,1)} %param.12) | copy-start | bytes 5898244
  2.7 31.1 %copy-start.1 = (bf16[1,128,3072]{2,1,0:T(8,128)(2,1)S(1)}, bf16[1,128,3072]{2,1,0:T(8,128)(2,1)}, u32[]{:S(2)}) copy-start(bf16[1,128,3072]{2,1,0:T(8,128)(2,1)} %param.8) | copy-start | bytes 2359300
  2.7 31.1 %copy-start.2 = (f32[1,128,16]{1,2,0:T(8,128)S(1)}, f32[1,128,16]{1,2,0:T(8,128)}, u32[]{:S(2)}) copy-start(f32[1,128,16]{1,2,0:T(8,128)} %param.10) | copy-start | bytes 24580
  2.7 31.1 %copy-start.4 = (s32[1,128,2]{1,2,0:T(2,128)S(1)}, s32[1,128,2]{1,2,0:T(2,128)}, u32[]{:S(2)}) copy-start(s32[1,128,2]{1,2,0:T(2,128)} %param.9) | copy-start | bytes 3076
  2.7 25.9 %collective-permute-start.2 = (bf16[8,80,768]{2,1,0:T(8,128)(2,1)S(1)}, bf16[8,80,768]{2,1,0:T(8,128)(2,1)S(1)}, u32[]{:S(2)}, u32[]{:S(2)}) collective-permute-start(bf16[8,80,768]{2,1,0:T(8,128)(2,1)S(1)} %get-tuple-element.39), channel_id=1, source_target_pairs={{0,1},{1,0},{2,3},{3,2},{4,5},{5,4},{6,7},{7,6},{8,9},{9,8},{10,11... | collective-permute-start | bytes 2949128 | tf_op jit(solution)/shard_map/ppermute | solution.py:195
  28.6 39.5 %copy-start.5 = (bf16[16,3072]{1,0:T(8,128)(2,1)S(1)}, bf16[16,3072]{1,0:T(8,128)(2,1)}, u32[]{:S(2)}) copy-start(bf16[16,3072]{1,0:T(8,128)(2,1)} %param.11) | copy-start | bytes 294916
  29.4 38.6 %collective-permute-start.3 = (bf16[4,80,768]{2,1,0:T(8,128)(2,1)S(1)}, bf16[4,80,768]{2,1,0:T(8,128)(2,1)S(1)}, u32[]{:S(2)}, u32[]{:S(2)}) collective-permute-start(bf16[4,80,768]{2,1,0:T(8,128)(2,1)S(1)} %get-tuple-element.44), channel_id=1, source_target_pairs={{0,2},{1,15},{2,4},{3,1},{4,6},{5,3},{6,8},{7,5},{8,10},{9,7},{10,... | collective-permute-start | bytes 1474568 | tf_op jit(solution)/shard_map/ppermute | solution.py:223
  31.6 36.5 %collective-permute-start.4 = (bf16[4,80,768]{2,1,0:T(8,128)(2,1)S(1)}, bf16[4,80,768]{2,1,0:T(8,128)(2,1)}, u32[]{:S(2)}, u32[]{:S(2)}) collective-permute-start(bf16[4,80,768]{2,1,0:T(8,128)(2,1)S(1)} %get-tuple-element.45), channel_id=1, source_target_pairs={{0,4},{1,13},{2,6},{3,15},{4,8},{5,1},{6,10},{7,3},{8,12},{9,5},{1... | collective-permute-start | bytes 1474568 | tf_op jit(solution)/shard_map/ppermute | solution.py:223
  35.0 33.0 %all-to-all-start.3 = ((f32[16,1,3072]{2,1,0:T(1,128)}), f32[16,1,3072]{2,1,0:T(1,128)S(1)}, u32[]{:S(2)}, u32[]{:S(2)}) async-start(f32[16,1,3072]{2,1,0:T(1,128)} %get-tuple-element.48), calls=%async_computation.3 | async-start | bytes 393216 | tf_op jit(solution)/shard_map/all_to_all | solution.py:247
  41.9 64.2 %collective-permute-start.5 = (bf16[2,80,768]{2,1,0:T(8,128)(2,1)S(1)}, bf16[2,80,768]{2,1,0:T(8,128)(2,1)S(1)}, u32[]{:S(2)}, u32[]{:S(2)}) collective-permute-start(bf16[2,80,768]{2,1,0:T(8,128)(2,1)S(1)} %get-tuple-element.50), channel_id=1, source_target_pairs={{0,6},{1,7},{2,8},{3,9},{4,10},{5,11},{6,12},{7,13},{8,14},{9,15},... | collective-permute-start | bytes 737288 | tf_op jit(solution)/shard_map/ppermute | solution.py:219
  47.0 59.1 %collective-permute-start.6 = (bf16[2,80,768]{2,1,0:T(8,128)(2,1)S(1)}, bf16[2,80,768]{2,1,0:T(8,128)(2,1)S(1)}, u32[]{:S(2)}, u32[]{:S(2)}) collective-permute-start(bf16[2,80,768]{2,1,0:T(8,128)(2,1)S(1)} %get-tuple-element.51), channel_id=1, source_target_pairs={{0,10},{1,11},{2,12},{3,13},{4,14},{5,15},{6,0},{7,1},{8,2},{9,3},... | collective-permute-start | bytes 737288 | tf_op jit(solution)/shard_map/ppermute | solution.py:219
  50.3 55.9 %collective-permute-start.7 = (bf16[2,80,768]{2,1,0:T(8,128)(2,1)S(1)}, bf16[2,80,768]{2,1,0:T(8,128)(2,1)S(1)}, u32[]{:S(2)}, u32[]{:S(2)}) collective-permute-start(bf16[2,80,768]{2,1,0:T(8,128)(2,1)S(1)} %get-tuple-element.52), channel_id=1, source_target_pairs={{0,8},{1,9},{2,10},{3,11},{4,12},{5,13},{6,14},{7,15},{8,0},{9,1},... | collective-permute-start | bytes 737288 | tf_op jit(solution)/shard_map/ppermute | solution.py:219
  68.1 34.7 %collective-permute-start = (bf16[4,80,768]{2,1,0:T(8,128)(2,1)S(1)}, bf16[4,80,768]{2,1,0:T(8,128)(2,1)S(1)}, u32[]{:S(2)}, u32[]{:S(2)}) collective-permute-start(bf16[4,80,768]{2,1,0:T(8,128)(2,1)S(1)} %get-tuple-element.19.refs_4_), channel_id=1, source_target_pairs={{0,1},{1,0},{2,3},{3,2},{4,5},{5,4},{6,7},{7,6},{8,9},{9,8},{10,11... | collective-permute-start | bytes 1474568 | tf_op jit(solution)/shard_map/cond/branch_1_fun/ppermute | solution.py:195
  70.9 31.9 %collective-permute-start.1 = (bf16[4,80,768]{2,1,0:T(8,128)(2,1)}, bf16[4,80,768]{2,1,0:T(8,128)(2,1)S(1)}, u32[]{:S(2)}, u32[]{:S(2)}) collective-permute-start(bf16[4,80,768]{2,1,0:T(8,128)(2,1)} %get-tuple-element.20.refs_5_), channel_id=1, source_target_pairs={{0,1},{1,0},{2,3},{3,2},{4,5},{5,4},{6,7},{7,6},{8,9},{9,8},{10,11... | collective-permute-start | bytes 1474568 | tf_op jit(solution)/shard_map/cond/branch_1_fun/ppermute | solution.py:195
  106.1 2.1 %copy-start.6 = (f32[1,3072]{1,0:T(1,128)}, f32[1,3072]{1,0:T(1,128)S(1)}, u32[]{:S(2)}) copy-start(f32[1,3072]{1,0:T(1,128)S(1)} %get-tuple-element.38) | copy-start | bytes 36868

commit v5 on v2

--- a/solution.py
+++ b/solution.py
@@ -6,9 +6,10 @@
 from jax.sharding import PartitionSpec as P
 
 QUARTERS = 4
-STEPS = (0, 3, 5, 2, 6, 4, 1, 7)
+STEPS = (0, 1, 7, 3, 5, 4, 2, 6)
 LANES = 128
-VMEM = 48 * 1024 * 1024
+SUBLANES = 8
+VMEM = 24 * 1024 * 1024
 
 
 def dot_rows(left, right):
@@ -56,6 +57,14 @@
         target = (chip + step) % chips
         out_ref[0] = kept_ref[target]
         out_ref[1] = got_ref[target]
+
+
+def sum_kernel(parts_ref, out_ref):
+    total = parts_ref[0]
+    for n in range(1, parts_ref.shape[0]):
+        total = total + parts_ref[n]
+    for n in range(out_ref.shape[0]):
+        out_ref[n] = total
 
 
 def router_kernel(depth, ids_ref, probs_ref, dots_ref, input_ref, logit_ref, place_ref, term_ref):
@@ -108,26 +117,29 @@
     term_ref[...] = term[:, None, :]
 
 
-def combine_kernel(cap, place_ref, logit_ref, weight_ref, *refs):
+def combine_kernel(cap, depth, place_ref, logit_ref, weight_ref, *refs):
     out_ref = refs[-1]
-    depth, part = refs[0].shape[1:]
-    tokens = place_ref.shape[0]
-    copies = jnp.concatenate([ref[...].reshape(2 * depth, part) for ref in refs[:-1]], axis=0)
+    tokens, width = out_ref.shape
+    filler = jnp.zeros((depth - cap, width), jnp.float32)
+    table = []
+    for ref in refs[:-1]:
+        for core in range(2):
+            stacked = ref[core].astype(jnp.float32)
+            rows = [stacked[q * cap : (q + 1) * cap] for q in range(QUARTERS)]
+            table += [jnp.concatenate(rows, axis=1), filler]
+    copies = jnp.concatenate(table, axis=0).astype(jnp.bfloat16)
     column = lax.broadcasted_iota(jnp.int32, (tokens, copies.shape[0]), 1)
-    gates = [place_ref[:, k : k + 1] for k in range(2)]
-    base = [place_ref[:, 2 + k : 3 + k].astype(jnp.int32) for k in range(2)]
-    for q in range(QUARTERS):
-        spread = jnp.where(column == base[0] + q * cap, gates[0], 0.0)
-        spread = jnp.where(column == base[1] + q * cap, gates[1], spread)
-        high = spread.astype(jnp.bfloat16)
-        low = (spread - high.astype(jnp.float32)).astype(jnp.bfloat16)
-        both = jnp.dot(
-            jnp.concatenate([high, low], axis=0), copies, preferred_element_type=jnp.float32
-        )
-        columns = slice(q * part, (q + 1) * part)
-        total = both[:tokens] + both[tokens:]
-        total = total + dot_rows(logit_ref[...], weight_ref[:, columns])
-        out_ref[:, columns] = total.astype(jnp.bfloat16)
+    spread = jnp.zeros(column.shape, jnp.float32)
+    for k in range(2):
+        base = place_ref[:, 2 + k : 3 + k].astype(jnp.int32)
+        spread = jnp.where(column == base, place_ref[:, k : k + 1], spread)
+    high = spread.astype(jnp.bfloat16)
+    low = (spread - high.astype(jnp.float32)).astype(jnp.bfloat16)
+    both = jnp.dot(
+        jnp.concatenate([high, low], axis=0), copies, preferred_element_type=jnp.float32
+    )
+    total = both[:tokens] + both[tokens:] + dot_rows(logit_ref[...], weight_ref[...])
+    out_ref[...] = total.astype(jnp.bfloat16)
 
 
 def shards(side, layer_input, expert_ids, router_probs, router_weight, expert_grads, gate_dots):
@@ -137,19 +149,16 @@
     chips = windows // 2
     cap = slots // windows
     part = width // QUARTERS
-    depth = cap * QUARTERS
+    stack = cap * QUARTERS
+    depth = -(-cap // SUBLANES) * SUBLANES
     params = pltpu.CompilerParams(vmem_limit_bytes=VMEM)
 
-    half = jax.ShapeDtypeStruct((chips, depth, part), jnp.bfloat16)
-    kept, given = pl.pallas_call(
-        lambda *refs: pack_kernel(cap, *refs),
-        out_shape=(half, half),
-        grid=(windows // 4,),
-        in_specs=[pl.BlockSpec((4 * cap, width), lambda g: (g, 0))],
-        out_specs=(pl.BlockSpec((2, depth, part), lambda g: (g, 0, 0)),) * 2,
-        compiler_params=params,
-    )(expert_grads[0, 0])
-    got = lax.ppermute(given, "exp", [(i, i ^ 1) for i in range(windows)])
+    runs = expert_ids[0, 0, 0] >= 0
+
+    def unit(step, operand):
+        out = jax.eval_shape(step, operand)
+        empty = lambda _: jax.tree.map(lambda leaf: jnp.zeros(leaf.shape, leaf.dtype), out)
+        return lax.cond(runs, step, empty, operand)
 
     laid = pl.pallas_call(
         lambda *refs: gate_pack_kernel(cap, *refs),
@@ -158,16 +167,17 @@
     )(gate_dots[0])
     dots = lax.all_to_all(laid, "exp", 0, 0, tiled=True)
 
-    dealt = pl.pallas_call(
-        deal_kernel,
-        out_shape=(jax.ShapeDtypeStruct((2, depth, part), jnp.bfloat16),) * chips,
-        compiler_params=params,
-    )(kept, got)
-    copies = [dealt[0]]
-    for step, block in zip(STEPS[1:], dealt[1:]):
-        moves = [(i, (i + 2 * step) % windows) for i in range(windows)]
-        copies.append(lax.ppermute(block, "exp", moves))
-    dots, _ = lax.optimization_barrier((dots, dealt))
+    half = jax.ShapeDtypeStruct((chips, stack, part), jnp.bfloat16)
+
+    def share(rows):
+        kept, given = pl.pallas_call(
+            lambda *refs: pack_kernel(cap, *refs),
+            out_shape=(half, half),
+            compiler_params=params,
+        )(rows)
+        return kept, lax.ppermute(given, "exp", [(i, i ^ 1) for i in range(windows)])
+
+    kept, got = unit(share, expert_grads[0, 0])
 
     ids = jnp.swapaxes(expert_ids, 1, 2)[0]
     probs = jnp.swapaxes(router_probs, 1, 2)[0]
@@ -180,22 +190,43 @@
         ),
         compiler_params=params,
     )(ids, probs, dots, layer_input[0])
-
-    own = jnp.sum(lax.all_to_all(term, "exp", 0, 0, tiled=True), axis=0)
-    across = [[x * side + z for x in range(side)] for z in range(side)]
-    along = [[x * side + z for z in range(side)] for x in range(side)]
-    for groups in (across, along):
-        copied = jnp.broadcast_to(own[None], (side,) + own.shape)
-        own = jnp.sum(
-            lax.all_to_all(copied, "ctx", 0, 0, axis_index_groups=groups, tiled=True), axis=0
-        )
-
+    got, term = lax.optimization_barrier((got, term))
+
+    def add(parts, count):
+        return pl.pallas_call(
+            sum_kernel,
+            out_shape=jax.ShapeDtypeStruct((count, 1, width), jnp.float32),
+            compiler_params=params,
+        )(parts)
+
+    own = add(lax.all_to_all(term, "exp", 0, 0, tiled=True), side)
+
+    dealt = pl.pallas_call(
+        deal_kernel,
+        out_shape=(jax.ShapeDtypeStruct((2, stack, part), jnp.bfloat16),) * chips,
+        compiler_params=params,
+    )(kept, got)
+    copies = [dealt[0]]
+    for step, block in zip(STEPS[1:], dealt[1:]):
+        moves = [(i, (i + 2 * step) % windows) for i in range(windows)]
+        copies.append(lax.ppermute(block, "exp", moves))
+
+    def over_ctx(own):
+        across = [[x * side + z for x in range(side)] for z in range(side)]
+        along = [[x * side + z for z in range(side)] for x in range(side)]
+        for groups, count in ((across, side), (along, 1)):
+            parts = lax.all_to_all(own, "ctx", 0, 0, axis_index_groups=groups, tiled=True)
+            own = add(parts, count)
+        return own
+
+    own = unit(over_ctx, own)
+    place, own = lax.optimization_barrier((place, own))
     combined = pl.pallas_call(
-        lambda *refs: combine_kernel(cap, *refs),
+        lambda *refs: combine_kernel(cap, depth, *refs),
         out_shape=jax.ShapeDtypeStruct((tokens, width), jnp.bfloat16),
         compiler_params=params,
     )(place, logit, router_weight, *copies)
-    return combined[None], own
+    return combined[None], own[0]
 
 
 def solution(mesh):

time: 99.1 us -> 104 us (1.049)
  the two profiles are of different devices: /device:TPU:46 before, /device:TPU:2 now
where the time goes in v5:
time: 104 us
  starting transfers between devices  48.7 us (47%)
  blocking collectives  39.6 us (38%)
  Pallas kernels  9.46 us (9%)
  waiting for transfers between devices  2.33 us (2%)
  local copies, waits for them, and re-layouts  1.9 us (2%)
  between operations  1.5 us (1%)
    all_to_all x2, blocking collectives, over_ctx(): lax.all_to_all(own, 'ctx', 0, 0, axis_index_groups=groups, tiled=True)  39.6 us
    ppermute x7, starting transfers between devices, shards(): copies.append(lax.ppermute(block, 'exp', moves))  31.6 us
    all_to_all x1, starting transfers between devices, shards(): dots = lax.all_to_all(laid, 'exp', 0, 0, tiled=True)  7.66 us
    all_to_all x1, starting transfers between devices, shards(): own = add(lax.all_to_all(term, 'exp', 0, 0, tiled=True), side)  7.18 us
    pallas_call x1, Pallas kernels, share(): pl.pallas_call(lambda *refs: pack_kernel(cap, *refs), out_shape=(half, ha...  2.98 us
    pallas_call x1, Pallas kernels, shards(): pl.pallas_call(deal_kernel, out_shape=(jax.ShapeDtypeStruct((2, stack, pa...  2.32 us
    ppermute x1, starting transfers between devices, share(): lax.ppermute(given, 'exp', [(i, i ^ 1) for i in range(windows)])  2.3 us
    ppermute x1, waiting for transfers between devices, share(): lax.ppermute(given, 'exp', [(i, i ^ 1) for i in range(windows)])  2.3 us
  transfers between devices with their start and end apart: 10, of which 1 were waited for; matrix products, arithmetic and copies ran while one was open for 1% of the time, Pallas kernels for 3%

profile of v5, /device:TPU:2, one launch (start us, length us, event | category | flops | bytes accessed | tf_op | source)
XLA Modules:
  0.0 103.5 jit_solution(14437925495031483295)
XLA Ops:
  0.6 0.7 copy-done.3
  1.3 0.8 shard_map.79
  2.1 7.7 %all-to-all-start.2 = ((f32[16,1,128]{2,1,0:T(1,128)}), f32[16,1,128]{2,1,0:T(1,128)S(1)}, u32[]{:S(2)}, u32[]{:S(2)}) async-start(f32[16,1,128]{2,1,0:T(1,128)} %shard_map.79), calls=%async_computation.2 | async-start | bytes 16384 | tf_op jit(solution)/shard_map/all_to_all | solution.py:168
  9.8 1.2 %slice.3 = s32[1,1,1]{1,2,0:T(1,128)} slice(s32[1,128,2]{1,2,0:T(2,128)} %param.11), slice={[0:1], [0:1], [0:1]} | slice | bytes 8 | tf_op jit(solution)/shard_map/slice | solution.py:156
  11.6 0.0 copy-start.4
  11.7 7.6 %conditional.2 = (bf16[8,80,768]{2,1,0:T(8,128)(2,1)}, bf16[8,80,768]{2,1,0:T(8,128)(2,1)}) conditional(s32[]{:T(128)} %bitcast.7, () %tuple.25, (bf16[1,1,320,3072]{3,2,1,0:T(8,128)(2,1)}) %tuple.29), branch_computations={%region_0.0_spmd, %region_1.0_spmd} | conditional | bytes 3932216 | solution.py:161
  11.7 3.0 %branch_1_fun.3 = (bf16[8,80,768]{2,1,0:T(8,128)(2,1)}, bf16[8,80,768]{2,1,0:T(8,128)(2,1)S(1)}) custom-call(bf16[320,3072]{1,0:T(8,128)(2,1)} %bitcast.16), custom_call_target="tpu_custom_call" | custom-call | tf_op jit(solution)/shard_map/cond/branch_1_fun/pallas_call | solution.py:173
  14.6 2.3 %collective-permute-start = (bf16[8,80,768]{2,1,0:T(8,128)(2,1)S(1)}, bf16[8,80,768]{2,1,0:T(8,128)(2,1)}, u32[]{:S(2)}, u32[]{:S(2)}) collective-permute-start(bf16[8,80,768]{2,1,0:T(8,128)(2,1)S(1)} %get-tuple-element.7), channel_id=1, source_target_pairs={{0,1},{1,0},{2,3},{3,2},{4,5},{5,4},{6,7},{7,6},{8,9},{9,8},{10,11... | collective-permute-start | bytes 2949128 | tf_op jit(solution)/shard_map/cond/branch_1_fun/ppermute | solution.py:178
  17.0 2.3 %collective-permute-done = bf16[8,80,768]{2,1,0:T(8,128)(2,1)} collective-permute-done((bf16[8,80,768]{2,1,0:T(8,128)(2,1)S(1)}, bf16[8,80,768]{2,1,0:T(8,128)(2,1)}, u32[]{:S(2)}, u32[]{:S(2)}) %collective-permute-start) | collective-permute-done | bytes 983072 | tf_op jit(solution)/shard_map/cond/branch_1_fun/ppermute | solution.py:178
  19.3 0.0 copy-start.1
  19.3 1.1 %shard_map.80 = (bf16[16,128]{1,0:T(8,128)(2,1)S(1)}, f32[128,8]{1,0:T(8,128)S(1)}, f32[16,1,3072]{2,1,0:T(1,128)}) custom-call(s32[2,128]{1,0:T(2,128)S(1)} %bitcast.15, f32[16,128]{1,0:T(8,128)S(1)} %bitcast.13, f32[16,1,128]{2,1,0:T(1,128)S(1)} %all-to-all-done.2.refs_2_, bf16[128,3072]{1,0:T(8,128)(2,1)S(1)} %bitcast.12), custom_call_target="tpu_custom_call" | custom-call | tf_op jit(solution)/shard_map/pallas_call | solution.py:184
  20.4 2.3 %shard_map.82 = (bf16[2,80,768]{2,1,0:T(8,128)(2,1)S(1)}, bf16[2,80,768]{2,1,0:T(8,128)(2,1)S(1)}, bf16[2,80,768]{2,1,0:T(8,128)(2,1)S(1)}, bf16[2,80,768]{2,1,0...) custom-call(bf16[8,80,768]{2,1,0:T(8,128)(2,1)} %get-tuple-element.3, ...), custom_call_target="tpu_custom_call" | custom-call | tf_op jit(solution)/shard_map/pallas_call | solution.py:204
  22.7 3.8 %collective-permute-start.1 = (bf16[2,80,768]{2,1,0:T(8,128)(2,1)S(1)}, bf16[2,80,768]{2,1,0:T(8,128)(2,1)S(1)}, u32[]{:S(2)}, u32[]{:S(2)}) collective-permute-start(bf16[2,80,768]{2,1,0:T(8,128)(2,1)S(1)} %get-tuple-element.36), channel_id=1, source_target_pairs={{0,2},{1,3},{2,4},{3,5},{4,6},{5,7},{6,8},{7,9},{8,10},{9,11},{10,... | collective-permute-start | bytes 737288 | tf_op jit(solution)/shard_map/ppermute | solution.py:212
  26.5 3.3 %collective-permute-start.2 = (bf16[2,80,768]{2,1,0:T(8,128)(2,1)S(1)}, bf16[2,80,768]{2,1,0:T(8,128)(2,1)S(1)}, u32[]{:S(2)}, u32[]{:S(2)}) collective-permute-start(bf16[2,80,768]{2,1,0:T(8,128)(2,1)S(1)} %get-tuple-element.37), channel_id=1, source_target_pairs={{0,14},{1,15},{2,0},{3,1},{4,2},{5,3},{6,4},{7,5},{8,6},{9,7},{10,... | collective-permute-start | bytes 737288 | tf_op jit(solution)/shard_map/ppermute | solution.py:212
  29.8 7.2 %all-to-all-start.3 = ((f32[16,1,3072]{2,1,0:T(1,128)}), f32[16,1,3072]{2,1,0:T(1,128)S(1)}, u32[]{:S(2)}, u32[]{:S(2)}) async-start(f32[16,1,3072]{2,1,0:T(1,128)} %get-tuple-element.30), calls=%async_computation.3 | async-start | bytes 393216 | tf_op jit(solution)/shard_map/all_to_all | solution.py:202
  37.0 5.6 %collective-permute-start.3 = (bf16[2,80,768]{2,1,0:T(8,128)(2,1)}, bf16[2,80,768]{2,1,0:T(8,128)(2,1)S(1)}, u32[]{:S(2)}, u32[]{:S(2)}) collective-permute-start(bf16[2,80,768]{2,1,0:T(8,128)(2,1)} %get-tuple-element.38), channel_id=1, source_target_pairs={{0,6},{1,7},{2,8},{3,9},{4,10},{5,11},{6,12},{7,13},{8,14},{9,15},... | collective-permute-start | bytes 737288 | tf_op jit(solution)/shard_map/ppermute | solution.py:212
  42.6 3.2 %collective-permute-start.4 = (bf16[2,80,768]{2,1,0:T(8,128)(2,1)S(1)}, bf16[2,80,768]{2,1,0:T(8,128)(2,1)S(1)}, u32[]{:S(2)}, u32[]{:S(2)}) collective-permute-start(bf16[2,80,768]{2,1,0:T(8,128)(2,1)S(1)} %get-tuple-element.39), channel_id=1, source_target_pairs={{0,10},{1,11},{2,12},{3,13},{4,14},{5,15},{6,0},{7,1},{8,2},{9,3},... | collective-permute-start | bytes 737288 | tf_op jit(solution)/shard_map/ppermute | solution.py:212
  45.9 7.7 %collective-permute-start.5 = (bf16[2,80,768]{2,1,0:T(8,128)(2,1)S(1)}, bf16[2,80,768]{2,1,0:T(8,128)(2,1)S(1)}, u32[]{:S(2)}, u32[]{:S(2)}) collective-permute-start(bf16[2,80,768]{2,1,0:T(8,128)(2,1)S(1)} %get-tuple-element.40), channel_id=1, source_target_pairs={{0,8},{1,9},{2,10},{3,11},{4,12},{5,13},{6,14},{7,15},{8,0},{9,1},... | collective-permute-start | bytes 737288 | tf_op jit(solution)/shard_map/ppermute | solution.py:212
  53.6 2.5 %collective-permute-start.6 = (bf16[2,80,768]{2,1,0:T(8,128)(2,1)S(1)}, bf16[2,80,768]{2,1,0:T(8,128)(2,1)S(1)}, u32[]{:S(2)}, u32[]{:S(2)}) collective-permute-start(bf16[2,80,768]{2,1,0:T(8,128)(2,1)S(1)} %get-tuple-element.41), channel_id=1, source_target_pairs={{0,4},{1,5},{2,6},{3,7},{4,8},{5,9},{6,10},{7,11},{8,12},{9,13},{1... | collective-permute-start | bytes 737288 | tf_op jit(solution)/shard_map/ppermute | solution.py:212
  56.1 5.5 %collective-permute-start.7 = (bf16[2,80,768]{2,1,0:T(8,128)(2,1)S(1)}, bf16[2,80,768]{2,1,0:T(8,128)(2,1)S(1)}, u32[]{:S(2)}, u32[]{:S(2)}) collective-permute-start(bf16[2,80,768]{2,1,0:T(8,128)(2,1)S(1)} %get-tuple-element.42), channel_id=1, source_target_pairs={{0,12},{1,13},{2,14},{3,15},{4,0},{5,1},{6,2},{7,3},{8,4},{9,5},{1... | collective-permute-start | bytes 737288 | tf_op jit(solution)/shard_map/ppermute | solution.py:212
  61.6 39.6 %conditional.3 = (f32[1,1,3072]{2,1,0:T(1,128)S(1)}) conditional(s32[]{:T(128)} %bitcast.7, () %tuple.24, f32[8,1,3072]{2,1,0:T(1,128)S(1)} %shard_map.81), branch_computations={%region_2.0_spmd, %region_3.0_spmd} | conditional | bytes 393224 | solution.py:161
  61.6 18.6 %all_to_all.18.parts_ref = f32[8,1,3072]{2,1,0:T(1,128)S(1)} all-to-all(f32[8,1,3072]{2,1,0:T(1,128)S(1)} %param.3), channel_id=1, replica_groups={{0,128,256,384,512,640,768,896},{16,144,272,400,528,656,784,912},{32,16..., dimensions={0} | all-to-all | bytes 196608 | tf_op jit(solution)/shard_map/cond/branch_1_fun/all_to_all | solution.py:218
  80.2 21.0 %all_to_all.19.parts_ref = f32[8,1,3072]{2,1,0:T(1,128)S(1)} all-to-all(f32[8,1,3072]{2,1,0:T(1,128)S(1)} %branch_1_fun.4), channel_id=1, replica_groups={{0,16,32,48,64,80,96,112},{128,144,160,176,192,208,224,240},{256,272,28..., dimensions={0} | all-to-all | bytes 196608 | tf_op jit(solution)/shard_map/cond/branch_1_fun/all_to_all | solution.py:218
  101.3 2.2 %shard_map.83 = bf16[128,3072]{1,0:T(8,128)(2,1)} custom-call(f32[128,8]{1,0:T(8,128)S(1)} %get-tuple-element.31.refs_0_, bf16[16,128]{1,0:T(8,128)(2,1)S(1)} %get-tuple-element.32.refs_1_, bf16[16,3072]{1,0:T(8,128)(2,1)S(1)} %copy-done.1, bf16[2,80,768]{2,1,0:T(8,128)(2,1)S(1)} %get-tuple-element.35.refs_3_, ...), custom_call_target="tpu_custom_call" | custom-call | tf_op jit(solution)/shard_map/pallas_call | solution.py:224
  (21 shorter events, 0.1 us)
Async XLA Ops:
  0.6 0.7 copy-start.3
  2.1 17.2 %all-to-all-start.2 = ((f32[16,1,128]{2,1,0:T(1,128)}), f32[16,1,128]{2,1,0:T(1,128)S(1)}, u32[]{:S(2)}, u32[]{:S(2)}) async-start(f32[16,1,128]{2,1,0:T(1,128)} %shard_map.79), calls=%async_computation.2 | async-start | bytes 16384 | tf_op jit(solution)/shard_map/all_to_all | solution.py:168
  11.6 7.7 %copy-start = (bf16[1,128,3072]{2,1,0:T(8,128)(2,1)S(1)}, bf16[1,128,3072]{2,1,0:T(8,128)(2,1)}, u32[]{:S(2)}) copy-start(bf16[1,128,3072]{2,1,0:T(8,128)(2,1)} %param.10) | copy-start | bytes 2359300
  11.6 7.6 %copy-start.2 = (f32[1,128,16]{1,2,0:T(8,128)S(1)}, f32[1,128,16]{1,2,0:T(8,128)}, u32[]{:S(2)}) copy-start(f32[1,128,16]{1,2,0:T(8,128)} %param.12) | copy-start | bytes 24580
  11.6 7.6 %copy-start.4 = (s32[1,128,2]{1,2,0:T(2,128)S(1)}, s32[1,128,2]{1,2,0:T(2,128)}, u32[]{:S(2)}) copy-start(s32[1,128,2]{1,2,0:T(2,128)} %param.11) | copy-start | bytes 3076
  14.6 4.6 %collective-permute-start = (bf16[8,80,768]{2,1,0:T(8,128)(2,1)S(1)}, bf16[8,80,768]{2,1,0:T(8,128)(2,1)}, u32[]{:S(2)}, u32[]{:S(2)}) collective-permute-start(bf16[8,80,768]{2,1,0:T(8,128)(2,1)S(1)} %get-tuple-element.7), channel_id=1, source_target_pairs={{0,1},{1,0},{2,3},{3,2},{4,5},{5,4},{6,7},{7,6},{8,9},{9,8},{10,11... | collective-permute-start | bytes 2949128 | tf_op jit(solution)/shard_map/cond/branch_1_fun/ppermute | solution.py:178
  19.3 82.0 %copy-start.1 = (bf16[16,3072]{1,0:T(8,128)(2,1)S(1)}, bf16[16,3072]{1,0:T(8,128)(2,1)}, u32[]{:S(2)}) copy-start(bf16[16,3072]{1,0:T(8,128)(2,1)} %refs_2_.1) | copy-start | bytes 294916
  22.7 30.9 %collective-permute-start.1 = (bf16[2,80,768]{2,1,0:T(8,128)(2,1)S(1)}, bf16[2,80,768]{2,1,0:T(8,128)(2,1)S(1)}, u32[]{:S(2)}, u32[]{:S(2)}) collective-permute-start(bf16[2,80,768]{2,1,0:T(8,128)(2,1)S(1)} %get-tuple-element.36), channel_id=1, source_target_pairs={{0,2},{1,3},{2,4},{3,5},{4,6},{5,7},{6,8},{7,9},{8,10},{9,11},{10,... | collective-permute-start | bytes 737288 | tf_op jit(solution)/shard_map/ppermute | solution.py:212
  26.5 29.6 %collective-permute-start.2 = (bf16[2,80,768]{2,1,0:T(8,128)(2,1)S(1)}, bf16[2,80,768]{2,1,0:T(8,128)(2,1)S(1)}, u32[]{:S(2)}, u32[]{:S(2)}) collective-permute-start(bf16[2,80,768]{2,1,0:T(8,128)(2,1)S(1)} %get-tuple-element.37), channel_id=1, source_target_pairs={{0,14},{1,15},{2,0},{3,1},{4,2},{5,3},{6,4},{7,5},{8,6},{9,7},{10,... | collective-permute-start | bytes 737288 | tf_op jit(solution)/shard_map/ppermute | solution.py:212
  29.8 31.8 %all-to-all-start.3 = ((f32[16,1,3072]{2,1,0:T(1,128)}), f32[16,1,3072]{2,1,0:T(1,128)S(1)}, u32[]{:S(2)}, u32[]{:S(2)}) async-start(f32[16,1,3072]{2,1,0:T(1,128)} %get-tuple-element.30), calls=%async_computation.3 | async-start | bytes 393216 | tf_op jit(solution)/shard_map/all_to_all | solution.py:202
  37.0 64.3 %collective-permute-start.3 = (bf16[2,80,768]{2,1,0:T(8,128)(2,1)}, bf16[2,80,768]{2,1,0:T(8,128)(2,1)S(1)}, u32[]{:S(2)}, u32[]{:S(2)}) collective-permute-start(bf16[2,80,768]{2,1,0:T(8,128)(2,1)} %get-tuple-element.38), channel_id=1, source_target_pairs={{0,6},{1,7},{2,8},{3,9},{4,10},{5,11},{6,12},{7,13},{8,14},{9,15},... | collective-permute-start | bytes 737288 | tf_op jit(solution)/shard_map/ppermute | solution.py:212
  42.6 58.7 %collective-permute-start.4 = (bf16[2,80,768]{2,1,0:T(8,128)(2,1)S(1)}, bf16[2,80,768]{2,1,0:T(8,128)(2,1)S(1)}, u32[]{:S(2)}, u32[]{:S(2)}) collective-permute-start(bf16[2,80,768]{2,1,0:T(8,128)(2,1)S(1)} %get-tuple-element.39), channel_id=1, source_target_pairs={{0,10},{1,11},{2,12},{3,13},{4,14},{5,15},{6,0},{7,1},{8,2},{9,3},... | collective-permute-start | bytes 737288 | tf_op jit(solution)/shard_map/ppermute | solution.py:212
  45.9 55.4 %collective-permute-start.5 = (bf16[2,80,768]{2,1,0:T(8,128)(2,1)S(1)}, bf16[2,80,768]{2,1,0:T(8,128)(2,1)S(1)}, u32[]{:S(2)}, u32[]{:S(2)}) collective-permute-start(bf16[2,80,768]{2,1,0:T(8,128)(2,1)S(1)} %get-tuple-element.40), channel_id=1, source_target_pairs={{0,8},{1,9},{2,10},{3,11},{4,12},{5,13},{6,14},{7,15},{8,0},{9,1},... | collective-permute-start | bytes 737288 | tf_op jit(solution)/shard_map/ppermute | solution.py:212
  53.6 47.7 %collective-permute-start.6 = (bf16[2,80,768]{2,1,0:T(8,128)(2,1)S(1)}, bf16[2,80,768]{2,1,0:T(8,128)(2,1)S(1)}, u32[]{:S(2)}, u32[]{:S(2)}) collective-permute-start(bf16[2,80,768]{2,1,0:T(8,128)(2,1)S(1)} %get-tuple-element.41), channel_id=1, source_target_pairs={{0,4},{1,5},{2,6},{3,7},{4,8},{5,9},{6,10},{7,11},{8,12},{9,13},{1... | collective-permute-start | bytes 737288 | tf_op jit(solution)/shard_map/ppermute | solution.py:212
  56.1 45.2 %collective-permute-start.7 = (bf16[2,80,768]{2,1,0:T(8,128)(2,1)S(1)}, bf16[2,80,768]{2,1,0:T(8,128)(2,1)S(1)}, u32[]{:S(2)}, u32[]{:S(2)}) collective-permute-start(bf16[2,80,768]{2,1,0:T(8,128)(2,1)S(1)} %get-tuple-element.42), channel_id=1, source_target_pairs={{0,12},{1,13},{2,14},{3,15},{4,0},{5,1},{6,2},{7,3},{8,4},{9,5},{1... | collective-permute-start | bytes 737288 | tf_op jit(solution)/shard_map/ppermute | solution.py:212
  101.3 2.3 %copy-start.5 = (f32[1,1,3072]{2,1,0:T(1,128)}, f32[1,1,3072]{2,1,0:T(1,128)S(1)}, u32[]{:S(2)}) copy-start(f32[1,1,3072]{2,1,0:T(1,128)S(1)} %get-tuple-element.50) | copy-start | bytes 36868

commit v6 on v5

--- a/solution.py
+++ b/solution.py
@@ -6,7 +6,7 @@
 from jax.sharding import PartitionSpec as P
 
 QUARTERS = 4
-STEPS = (0, 1, 7, 3, 5, 4, 2, 6)
+STEPS = (3, 5, 1, 7)
 LANES = 128
 SUBLANES = 8
 VMEM = 24 * 1024 * 1024
@@ -34,27 +34,32 @@
     out_ref[...] = laid[:, None, :]
 
 
-def pack_kernel(cap, rows_ref, kept_ref, given_ref):
-    part = kept_ref.shape[2]
-    core = lax.axis_index("exp") % 2
+def pack_kernel(cap, rows_ref, even_ref, kept_ref, given_ref):
+    part = even_ref.shape[2]
+    chip, core = lax.axis_index("exp") // 2, lax.axis_index("exp") % 2
     rows = rows_ref[...].astype(jnp.float32)
-    for pair in range(kept_ref.shape[0]):
+    for group in range(kept_ref.shape[0]):
         stacks = []
-        for w in (2 * pair, 2 * pair + 1):
+        for w in range(4 * group, 4 * group + 4):
             window = rows[w * cap : (w + 1) * cap]
             stacked = jnp.concatenate(
                 [window[:, q * part : (q + 1) * part] for q in range(QUARTERS)], axis=0
             )
             stacks.append(stacked)
-        kept_ref[pair] = jnp.where(core == 0, stacks[0], stacks[1]).astype(jnp.bfloat16)
-        given_ref[pair] = jnp.where(core == 0, stacks[1], stacks[0]).astype(jnp.bfloat16)
+        same = chip % 2 == 0
+        for n in range(2):
+            even = jnp.where(same, stacks[n], stacks[2 + n])
+            even_ref[2 * group + n] = even.astype(jnp.bfloat16)
+        odd = [jnp.where(same, stacks[2 + n], stacks[n]) for n in range(2)]
+        kept_ref[group] = jnp.where(core == 0, odd[0], odd[1]).astype(jnp.bfloat16)
+        given_ref[group] = jnp.where(core == 0, odd[1], odd[0]).astype(jnp.bfloat16)
 
 
 def deal_kernel(kept_ref, got_ref, *out_refs):
-    chips = kept_ref.shape[0]
+    chips = 2 * kept_ref.shape[0]
     chip = lax.axis_index("exp") // 2
     for step, out_ref in zip(STEPS, out_refs):
-        target = (chip + step) % chips
+        target = (chip + step) % chips // 2
         out_ref[0] = kept_ref[target]
         out_ref[1] = got_ref[target]
 
@@ -106,7 +111,8 @@
         ids = ids_ref[k : k + 1, :]
         step = (chip - ids // 2 + experts // 2) % (experts // 2)
         place = sum(jnp.where(step == STEPS[n], n, 0) for n in range(len(STEPS)))
-        block = place * 2 + (ids % 2 + core) % 2
+        odd = place * 2 + (ids % 2 + core) % 2
+        block = jnp.where(step % 2 == 1, odd, experts // 2 + ids // 4 * 2 + ids % 2)
         rows.append((block * depth + slots[k]).astype(jnp.float32))
     place = jnp.concatenate(
         [picked[0] / total, picked[1] / total] + rows + [jnp.zeros((4, tokens), jnp.float32)],
@@ -123,8 +129,8 @@
     filler = jnp.zeros((depth - cap, width), jnp.float32)
     table = []
     for ref in refs[:-1]:
-        for core in range(2):
-            stacked = ref[core].astype(jnp.float32)
+        for n in range(ref.shape[0]):
+            stacked = ref[n].astype(jnp.float32)
             rows = [stacked[q * cap : (q + 1) * cap] for q in range(QUARTERS)]
             table += [jnp.concatenate(rows, axis=1), filler]
     copies = jnp.concatenate(table, axis=0).astype(jnp.bfloat16)
@@ -167,17 +173,18 @@
     )(gate_dots[0])
     dots = lax.all_to_all(laid, "exp", 0, 0, tiled=True)
 
-    half = jax.ShapeDtypeStruct((chips, stack, part), jnp.bfloat16)
+    def blocks_of(count):
+        return jax.ShapeDtypeStruct((count, stack, part), jnp.bfloat16)
 
     def share(rows):
-        kept, given = pl.pallas_call(
+        even, kept, given = pl.pallas_call(
             lambda *refs: pack_kernel(cap, *refs),
-            out_shape=(half, half),
+            out_shape=(blocks_of(chips), blocks_of(chips // 2), blocks_of(chips // 2)),
             compiler_params=params,
         )(rows)
-        return kept, lax.ppermute(given, "exp", [(i, i ^ 1) for i in range(windows)])
-
-    kept, got = unit(share, expert_grads[0, 0])
+        return even, kept, lax.ppermute(given, "exp", [(i, i ^ 1) for i in range(windows)])
+
+    even, kept, got = unit(share, expert_grads[0, 0])
 
     ids = jnp.swapaxes(expert_ids, 1, 2)[0]
     probs = jnp.swapaxes(router_probs, 1, 2)[0]
@@ -199,24 +206,27 @@
             compiler_params=params,
         )(parts)
 
-    own = add(lax.all_to_all(term, "exp", 0, 0, tiled=True), side)
+    own = add(lax.all_to_all(term, "exp", 0, 0, tiled=True), 1)
 
     dealt = pl.pallas_call(
         deal_kernel,
-        out_shape=(jax.ShapeDtypeStruct((2, stack, part), jnp.bfloat16),) * chips,
+        out_shape=(blocks_of(2),) * len(STEPS),
         compiler_params=params,
     )(kept, got)
-    copies = [dealt[0]]
-    for step, block in zip(STEPS[1:], dealt[1:]):
+    copies = []
+    for step, block in zip(STEPS, dealt):
         moves = [(i, (i + 2 * step) % windows) for i in range(windows)]
         copies.append(lax.ppermute(block, "exp", moves))
+    alike = [[i for i in range(windows) if i // 2 % 2 == parity] for parity in range(2)]
+    even, own, *copies[:2] = lax.optimization_barrier((even, own, *copies[:2]))
+    copies.append(lax.all_to_all(even, "exp", 0, 0, axis_index_groups=alike, tiled=True))
 
     def over_ctx(own):
-        across = [[x * side + z for x in range(side)] for z in range(side)]
-        along = [[x * side + z for z in range(side)] for x in range(side)]
-        for groups, count in ((across, side), (along, 1)):
-            parts = lax.all_to_all(own, "ctx", 0, 0, axis_index_groups=groups, tiled=True)
-            own = add(parts, count)
+        bit = 1
+        while bit < side * side:
+            moves = [(i, i ^ bit) for i in range(side * side)]
+            own = own + lax.ppermute(own, "ctx", moves)
+            bit *= 2
         return own
 
     own = unit(over_ctx, own)

time: 104 us -> 125 us (1.20)
  the two profiles are of different devices: /device:TPU:2 before, /device:TPU:10 now
where the time goes in v6:
time: 125 us; the launch traced here: 124 us
  starting transfers between devices  74.9 us (60%)
  waiting for transfers between devices  37.1 us (30%)
  Pallas kernels  8.24 us (7%)
  local copies, waits for them, and re-layouts  1.89 us (2%)
  between operations  1.44 us (1%)
    ppermute x6, starting transfers between devices, over_ctx(): own = own + lax.ppermute(own, 'ctx', moves)  34 us
    ppermute x4, starting transfers between devices, shards(): copies.append(lax.ppermute(block, 'exp', moves))  18.5 us
    ppermute x4, waiting for transfers between devices, shards(): copies.append(lax.ppermute(block, 'exp', moves))  17.8 us
    ppermute x6, waiting for transfers between devices, over_ctx(): own = own + lax.ppermute(own, 'ctx', moves)  17.7 us
    all_to_all x1, starting transfers between devices, shards(): dots = lax.all_to_all(laid, 'exp', 0, 0, tiled=True)  7.66 us
    all_to_all x1, starting transfers between devices, shards(): own = add(lax.all_to_all(term, 'exp', 0, 0, tiled=True), 1)  7.31 us
    all_to_all x1, starting transfers between devices, shards(): lax.all_to_all(even, 'exp', 0, 0, axis_index_groups=alike, tiled=True)  5.17 us
    pallas_call x1, Pallas kernels, share(): pl.pallas_call(lambda *refs: pack_kernel(cap, *refs), out_shape=(blocks_o...  3.01 us
  transfers between devices with their start and end apart: 14, of which 9 were waited for; matrix products, arithmetic and copies ran while one was open for 1% of the time, Pallas kernels for 3%

profile of v6, /device:TPU:10, one launch (start us, length us, event | category | flops | bytes accessed | tf_op | source)
XLA Modules:
  0.0 123.8 jit_solution(2906312428656207834)
XLA Ops:
  2.1 7.7 %all-to-all-start = ((f32[16,1,128]{2,1,0:T(1,128)}), f32[16,1,128]{2,1,0:T(1,128)S(1)}, u32[]{:S(2)}, u32[]{:S(2)}) async-start(f32[16,1,128]{2,1,0:T(1,128)} %shard_map.79), calls=%async_computation | async-start | bytes 16384 | tf_op jit(solution)/shard_map/all_to_all | solution.py:174
  11.7 6.9 %conditional.2 = (bf16[8,80,768]{2,1,0:T(8,128)(2,1)}, bf16[4,80,768]{2,1,0:T(8,128)(2,1)S(1)}, bf16[4,80,768]{2,1,0:T(8,128)(2,1)}) conditional(s32[]{:T(128)} %bitcast.7, () %tuple.26, (bf16[1,1,320,3072]{3,2,1,0:T(8,128)(2,1)}) %tuple.31), branch_computations={%region_0.0_spmd, %region_1.0_spmd} | conditional | bytes 1966144 | solution.py:167
  11.7 3.0 %branch_1_fun.1 = (bf16[8,80,768]{2,1,0:T(8,128)(2,1)}, bf16[4,80,768]{2,1,0:T(8,128)(2,1)S(1)}, bf16[4,80,768]{2,1,0:T(8,128)(2,1)S(1)}) custom-call(bf16[320,3072]{1,0:T(8,128)(2,1)} %bitcast.16), custom_call_target="tpu_custom_call" | custom-call | tf_op jit(solution)/shard_map/cond/branch_1_fun/pallas_call | solution.py:180
  14.7 2.3 %collective-permute-start = (bf16[4,80,768]{2,1,0:T(8,128)(2,1)S(1)}, bf16[4,80,768]{2,1,0:T(8,128)(2,1)}, u32[]{:S(2)}, u32[]{:S(2)}) collective-permute-start(bf16[4,80,768]{2,1,0:T(8,128)(2,1)S(1)} %get-tuple-element.8), channel_id=1, source_target_pairs={{0,1},{1,0},{2,3},{3,2},{4,5},{5,4},{6,7},{7,6},{8,9},{9,8},{10,11... | collective-permute-start | bytes 1474568 | tf_op jit(solution)/shard_map/cond/branch_1_fun/ppermute | solution.py:185
  19.7 7.3 %all-to-all-start.1 = ((f32[16,1,3072]{2,1,0:T(1,128)}), f32[16,1,3072]{2,1,0:T(1,128)S(1)}, u32[]{:S(2)}, u32[]{:S(2)}) async-start(f32[16,1,3072]{2,1,0:T(1,128)} %get-tuple-element.33), calls=%async_computation.1 | async-start | bytes 393216 | tf_op jit(solution)/shard_map/all_to_all | solution.py:209
  28.2 5.6 %collective-permute-start.7 = (bf16[2,80,768]{2,1,0:T(8,128)(2,1)S(1)}, bf16[2,80,768]{2,1,0:T(8,128)(2,1)S(1)}, u32[]{:S(2)}, u32[]{:S(2)}) collective-permute-start(bf16[2,80,768]{2,1,0:T(8,128)(2,1)S(1)} %get-tuple-element.36), channel_id=1, source_target_pairs={{0,6},{1,7},{2,8},{3,9},{4,10},{5,11},{6,12},{7,13},{8,14},{9,15},... | collective-permute-start | bytes 737288 | tf_op jit(solution)/shard_map/ppermute | solution.py:219
  33.8 3.2 %collective-permute-start.8 = (bf16[2,80,768]{2,1,0:T(8,128)(2,1)S(1)}, bf16[2,80,768]{2,1,0:T(8,128)(2,1)S(1)}, u32[]{:S(2)}, u32[]{:S(2)}) collective-permute-start(bf16[2,80,768]{2,1,0:T(8,128)(2,1)S(1)} %get-tuple-element.37), channel_id=1, source_target_pairs={{0,10},{1,11},{2,12},{3,13},{4,14},{5,15},{6,0},{7,1},{8,2},{9,3},... | collective-permute-start | bytes 737288 | tf_op jit(solution)/shard_map/ppermute | solution.py:219
  37.1 14.9 %collective-permute-done.7.refs_3_ = bf16[2,80,768]{2,1,0:T(8,128)(2,1)S(1)} collective-permute-done((bf16[2,80,768]{2,1,0:T(8,128)(2,1)S(1)}, bf16[2,80,768]{2,1,0:T(8,128)(2,1)S(1)}, u32[]{:S(2)}, u32[]{:S(2)}) %collective-permute-start.7) | collective-permute-done | bytes 245792 | tf_op jit(solution)/shard_map/ppermute | solution.py:219
  52.0 2.9 %collective-permute-done.8.refs_4_ = bf16[2,80,768]{2,1,0:T(8,128)(2,1)S(1)} collective-permute-done((bf16[2,80,768]{2,1,0:T(8,128)(2,1)S(1)}, bf16[2,80,768]{2,1,0:T(8,128)(2,1)S(1)}, u32[]{:S(2)}, u32[]{:S(2)}) %collective-permute-start.8) | collective-permute-done | bytes 245792 | tf_op jit(solution)/shard_map/ppermute | solution.py:219
  54.9 5.2 %all-to-all-start.2 = ((bf16[8,80,768]{2,1,0:T(8,128)(2,1)}), bf16[8,80,768]{2,1,0:T(8,128)(2,1)S(1)}, u32[]{:S(2)}, u32[]{:S(2)}) async-start(bf16[8,80,768]{2,1,0:T(8,128)(2,1)} %get-tuple-element.45), calls=%async_computation.2 | async-start | bytes 1966080 | tf_op jit(solution)/shard_map/all_to_all | solution.py:222
  60.1 7.7 %collective-permute-start.10 = (bf16[2,80,768]{2,1,0:T(8,128)(2,1)S(1)}, bf16[2,80,768]{2,1,0:T(8,128)(2,1)S(1)}, u32[]{:S(2)}, u32[]{:S(2)}) collective-permute-start(bf16[2,80,768]{2,1,0:T(8,128)(2,1)S(1)} %get-tuple-element.44), channel_id=1, source_target_pairs={{0,14},{1,15},{2,0},{3,1},{4,2},{5,3},{6,4},{7,5},{8,6},{9,7},{10,... | collective-permute-start | bytes 737288 | tf_op jit(solution)/shard_map/ppermute | solution.py:219
  67.8 1.9 %collective-permute-start.9 = (bf16[2,80,768]{2,1,0:T(8,128)(2,1)S(1)}, bf16[2,80,768]{2,1,0:T(8,128)(2,1)S(1)}, u32[]{:S(2)}, u32[]{:S(2)}) collective-permute-start(bf16[2,80,768]{2,1,0:T(8,128)(2,1)S(1)} %get-tuple-element.43), channel_id=1, source_target_pairs={{0,2},{1,3},{2,4},{3,5},{4,6},{5,7},{6,8},{7,9},{8,10},{9,11},{10,... | collective-permute-start | bytes 737288 | tf_op jit(solution)/shard_map/ppermute | solution.py:219
  69.7 51.9 %conditional.3 = (f32[1,1,3072]{2,1,0:T(1,128)S(1)}) conditional(s32[]{:T(128)} %bitcast.7, () %tuple.25, f32[1,1,3072]{2,1,0:T(1,128)S(1)} %shard_map.81), branch_computations={%region_2.0_spmd, %region_3.0_spmd} | conditional | flops 18432 | bytes 516344 | solution.py:167
  69.8 5.2 %collective-permute-start.1 = (f32[1,1,3072]{2,1,0:T(1,128)S(1)}, f32[1,1,3072]{2,1,0:T(1,128)S(1)}, u32[]{:S(2)}, u32[]{:S(2)}) collective-permute-start(f32[1,1,3072]{2,1,0:T(1,128)S(1)} %param.3), channel_id=1, source_target_pairs={{0,16},{16,0},{32,48},{48,32},{64,80},{80,64},{96,112},{112,96},{1... | collective-permute-start | bytes 36872 | tf_op jit(solution)/shard_map/cond/branch_1_fun/ppermute | solution.py:228
  76.6 7.9 %collective-permute-start.2 = (f32[1,1,3072]{2,1,0:T(1,128)S(1)}, f32[1,1,3072]{2,1,0:T(1,128)S(1)}, u32[]{:S(2)}, u32[]{:S(2)}) collective-permute-start(f32[1,1,3072]{2,1,0:T(1,128)S(1)} %add.12), channel_id=1, source_target_pairs={{0,32},{16,48},{32,0},{48,16},{64,96},{80,112},{96,64},{112,80},{1... | collective-permute-start | bytes 36872 | tf_op jit(solution)/shard_map/cond/branch_1_fun/ppermute | solution.py:228
  84.5 1.7 %collective-permute-done.2 = f32[1,1,3072]{2,1,0:T(1,128)S(1)} collective-permute-done((f32[1,1,3072]{2,1,0:T(1,128)S(1)}, f32[1,1,3072]{2,1,0:T(1,128)S(1)}, u32[]{:S(2)}, u32[]{:S(2)}) %collective-permute-start.2) | collective-permute-done | bytes 12320 | tf_op jit(solution)/shard_map/cond/branch_1_fun/ppermute | solution.py:228
  86.2 11.9 %collective-permute-start.3 = (f32[1,1,3072]{2,1,0:T(1,128)S(1)}, f32[1,1,3072]{2,1,0:T(1,128)S(1)}, u32[]{:S(2)}, u32[]{:S(2)}) collective-permute-start(f32[1,1,3072]{2,1,0:T(1,128)S(1)} %add.13), channel_id=1, source_target_pairs={{0,64},{16,80},{32,96},{48,112},{64,0},{80,16},{96,32},{112,48},{1... | collective-permute-start | bytes 36872 | tf_op jit(solution)/shard_map/cond/branch_1_fun/ppermute | solution.py:228
  99.8 3.3 %collective-permute-start.4 = (f32[1,1,3072]{2,1,0:T(1,128)S(1)}, f32[1,1,3072]{2,1,0:T(1,128)S(1)}, u32[]{:S(2)}, u32[]{:S(2)}) collective-permute-start(f32[1,1,3072]{2,1,0:T(1,128)S(1)} %add.14), channel_id=1, source_target_pairs={{0,128},{16,144},{32,160},{48,176},{64,192},{80,208},{96,224},{112... | collective-permute-start | bytes 36872 | tf_op jit(solution)/shard_map/cond/branch_1_fun/ppermute | solution.py:228
  103.1 2.2 %collective-permute-done.4 = f32[1,1,3072]{2,1,0:T(1,128)S(1)} collective-permute-done((f32[1,1,3072]{2,1,0:T(1,128)S(1)}, f32[1,1,3072]{2,1,0:T(1,128)S(1)}, u32[]{:S(2)}, u32[]{:S(2)}) %collective-permute-start.4) | collective-permute-done | bytes 12320 | tf_op jit(solution)/shard_map/cond/branch_1_fun/ppermute | solution.py:228
  105.4 2.5 %collective-permute-start.5 = (f32[1,1,3072]{2,1,0:T(1,128)S(1)}, f32[1,1,3072]{2,1,0:T(1,128)S(1)}, u32[]{:S(2)}, u32[]{:S(2)}) collective-permute-start(f32[1,1,3072]{2,1,0:T(1,128)S(1)} %add.15), channel_id=1, source_target_pairs={{0,256},{16,272},{32,288},{48,304},{64,320},{80,336},{96,352},{112... | collective-permute-start | bytes 36872 | tf_op jit(solution)/shard_map/cond/branch_1_fun/ppermute | solution.py:228
  107.9 4.1 %collective-permute-done.5 = f32[1,1,3072]{2,1,0:T(1,128)S(1)} collective-permute-done((f32[1,1,3072]{2,1,0:T(1,128)S(1)}, f32[1,1,3072]{2,1,0:T(1,128)S(1)}, u32[]{:S(2)}, u32[]{:S(2)}) %collective-permute-start.5) | collective-permute-done | bytes 12320 | tf_op jit(solution)/shard_map/cond/branch_1_fun/ppermute | solution.py:228
  112.0 3.2 %collective-permute-start.6 = (f32[1,1,3072]{2,1,0:T(1,128)S(1)}, f32[1,1,3072]{2,1,0:T(1,128)S(1)}, u32[]{:S(2)}, u32[]{:S(2)}) collective-permute-start(f32[1,1,3072]{2,1,0:T(1,128)S(1)} %add.16), channel_id=1, source_target_pairs={{0,512},{16,528},{32,544},{48,560},{64,576},{80,592},{96,608},{112... | collective-permute-start | bytes 36872 | tf_op jit(solution)/shard_map/cond/branch_1_fun/ppermute | solution.py:228
  115.1 6.4 %collective-permute-done.6 = f32[1,1,3072]{2,1,0:T(1,128)S(1)} collective-permute-done((f32[1,1,3072]{2,1,0:T(1,128)S(1)}, f32[1,1,3072]{2,1,0:T(1,128)S(1)}, u32[]{:S(2)}, u32[]{:S(2)}) %collective-permute-start.6) | collective-permute-done | bytes 12320 | tf_op jit(solution)/shard_map/cond/branch_1_fun/ppermute | solution.py:228
  121.6 2.2 %shard_map.83 = bf16[128,3072]{1,0:T(8,128)(2,1)} custom-call(f32[128,8]{1,0:T(8,128)S(1)} %get-tuple-element.39.refs_0_, bf16[16,128]{1,0:T(8,128)(2,1)S(1)} %get-tuple-element.40.refs_1_, bf16[16,3072]{1,0:T(8,128)(2,1)S(1)} %copy-done.1, bf16[2,80,768]{2,1,0:T(8,128)(2,1)S(1)} %collective-permute-done.7.refs_3_, ...), custom_call_target="tpu_custom_call" | custom-call | tf_op jit(solution)/shard_map/pallas_call | solution.py:234
  (31 shorter events, 9.9 us)
Async XLA Ops:
  0.6 0.7 copy-start.3
  2.1 16.5 %all-to-all-start = ((f32[16,1,128]{2,1,0:T(1,128)}), f32[16,1,128]{2,1,0:T(1,128)S(1)}, u32[]{:S(2)}, u32[]{:S(2)}) async-start(f32[16,1,128]{2,1,0:T(1,128)} %shard_map.79), calls=%async_computation | async-start | bytes 16384 | tf_op jit(solution)/shard_map/all_to_all | solution.py:174
  11.6 7.0 %copy-start = (bf16[1,128,3072]{2,1,0:T(8,128)(2,1)S(1)}, bf16[1,128,3072]{2,1,0:T(8,128)(2,1)}, u32[]{:S(2)}) copy-start(bf16[1,128,3072]{2,1,0:T(8,128)(2,1)} %param.10) | copy-start | bytes 2359300
  11.6 7.0 %copy-start.2 = (f32[1,128,16]{1,2,0:T(8,128)S(1)}, f32[1,128,16]{1,2,0:T(8,128)}, u32[]{:S(2)}) copy-start(f32[1,128,16]{1,2,0:T(8,128)} %param.12) | copy-start | bytes 24580
  11.6 7.0 %copy-start.4 = (s32[1,128,2]{1,2,0:T(2,128)S(1)}, s32[1,128,2]{1,2,0:T(2,128)}, u32[]{:S(2)}) copy-start(s32[1,128,2]{1,2,0:T(2,128)} %param.11) | copy-start | bytes 3076
  14.7 3.9 %collective-permute-start = (bf16[4,80,768]{2,1,0:T(8,128)(2,1)S(1)}, bf16[4,80,768]{2,1,0:T(8,128)(2,1)}, u32[]{:S(2)}, u32[]{:S(2)}) collective-permute-start(bf16[4,80,768]{2,1,0:T(8,128)(2,1)S(1)} %get-tuple-element.8), channel_id=1, source_target_pairs={{0,1},{1,0},{2,3},{3,2},{4,5},{5,4},{6,7},{7,6},{8,9},{9,8},{10,11... | collective-permute-start | bytes 1474568 | tf_op jit(solution)/shard_map/cond/branch_1_fun/ppermute | solution.py:185
  19.7 101.9 %copy-start.1 = (bf16[16,3072]{1,0:T(8,128)(2,1)S(1)}, bf16[16,3072]{1,0:T(8,128)(2,1)}, u32[]{:S(2)}) copy-start(bf16[16,3072]{1,0:T(8,128)(2,1)} %refs_2_.1) | copy-start | bytes 294916
  19.7 17.3 %all-to-all-start.1 = ((f32[16,1,3072]{2,1,0:T(1,128)}), f32[16,1,3072]{2,1,0:T(1,128)S(1)}, u32[]{:S(2)}, u32[]{:S(2)}) async-start(f32[16,1,3072]{2,1,0:T(1,128)} %get-tuple-element.33), calls=%async_computation.1 | async-start | bytes 393216 | tf_op jit(solution)/shard_map/all_to_all | solution.py:209
  28.2 23.8 %collective-permute-start.7 = (bf16[2,80,768]{2,1,0:T(8,128)(2,1)S(1)}, bf16[2,80,768]{2,1,0:T(8,128)(2,1)S(1)}, u32[]{:S(2)}, u32[]{:S(2)}) collective-permute-start(bf16[2,80,768]{2,1,0:T(8,128)(2,1)S(1)} %get-tuple-element.36), channel_id=1, source_target_pairs={{0,6},{1,7},{2,8},{3,9},{4,10},{5,11},{6,12},{7,13},{8,14},{9,15},... | collective-permute-start | bytes 737288 | tf_op jit(solution)/shard_map/ppermute | solution.py:219
  33.8 21.1 %collective-permute-start.8 = (bf16[2,80,768]{2,1,0:T(8,128)(2,1)S(1)}, bf16[2,80,768]{2,1,0:T(8,128)(2,1)S(1)}, u32[]{:S(2)}, u32[]{:S(2)}) collective-permute-start(bf16[2,80,768]{2,1,0:T(8,128)(2,1)S(1)} %get-tuple-element.37), channel_id=1, source_target_pairs={{0,10},{1,11},{2,12},{3,13},{4,14},{5,15},{6,0},{7,1},{8,2},{9,3},... | collective-permute-start | bytes 737288 | tf_op jit(solution)/shard_map/ppermute | solution.py:219
  54.9 66.7 %all-to-all-start.2 = ((bf16[8,80,768]{2,1,0:T(8,128)(2,1)}), bf16[8,80,768]{2,1,0:T(8,128)(2,1)S(1)}, u32[]{:S(2)}, u32[]{:S(2)}) async-start(bf16[8,80,768]{2,1,0:T(8,128)(2,1)} %get-tuple-element.45), calls=%async_computation.2 | async-start | bytes 1966080 | tf_op jit(solution)/shard_map/all_to_all | solution.py:222
  60.1 61.5 %collective-permute-start.10 = (bf16[2,80,768]{2,1,0:T(8,128)(2,1)S(1)}, bf16[2,80,768]{2,1,0:T(8,128)(2,1)S(1)}, u32[]{:S(2)}, u32[]{:S(2)}) collective-permute-start(bf16[2,80,768]{2,1,0:T(8,128)(2,1)S(1)} %get-tuple-element.44), channel_id=1, source_target_pairs={{0,14},{1,15},{2,0},{3,1},{4,2},{5,3},{6,4},{7,5},{8,6},{9,7},{10,... | collective-permute-start | bytes 737288 | tf_op jit(solution)/shard_map/ppermute | solution.py:219
  67.8 53.8 %collective-permute-start.9 = (bf16[2,80,768]{2,1,0:T(8,128)(2,1)S(1)}, bf16[2,80,768]{2,1,0:T(8,128)(2,1)S(1)}, u32[]{:S(2)}, u32[]{:S(2)}) collective-permute-start(bf16[2,80,768]{2,1,0:T(8,128)(2,1)S(1)} %get-tuple-element.43), channel_id=1, source_target_pairs={{0,2},{1,3},{2,4},{3,5},{4,6},{5,7},{6,8},{7,9},{8,10},{9,11},{10,... | collective-permute-start | bytes 737288 | tf_op jit(solution)/shard_map/ppermute | solution.py:219
  69.8 6.9 %collective-permute-start.1 = (f32[1,1,3072]{2,1,0:T(1,128)S(1)}, f32[1,1,3072]{2,1,0:T(1,128)S(1)}, u32[]{:S(2)}, u32[]{:S(2)}) collective-permute-start(f32[1,1,3072]{2,1,0:T(1,128)S(1)} %param.3), channel_id=1, source_target_pairs={{0,16},{16,0},{32,48},{48,32},{64,80},{80,64},{96,112},{112,96},{1... | collective-permute-start | bytes 36872 | tf_op jit(solution)/shard_map/cond/branch_1_fun/ppermute | solution.py:228
  76.6 9.6 %collective-permute-start.2 = (f32[1,1,3072]{2,1,0:T(1,128)S(1)}, f32[1,1,3072]{2,1,0:T(1,128)S(1)}, u32[]{:S(2)}, u32[]{:S(2)}) collective-permute-start(f32[1,1,3072]{2,1,0:T(1,128)S(1)} %add.12), channel_id=1, source_target_pairs={{0,32},{16,48},{32,0},{48,16},{64,96},{80,112},{96,64},{112,80},{1... | collective-permute-start | bytes 36872 | tf_op jit(solution)/shard_map/cond/branch_1_fun/ppermute | solution.py:228
  86.2 13.5 %collective-permute-start.3 = (f32[1,1,3072]{2,1,0:T(1,128)S(1)}, f32[1,1,3072]{2,1,0:T(1,128)S(1)}, u32[]{:S(2)}, u32[]{:S(2)}) collective-permute-start(f32[1,1,3072]{2,1,0:T(1,128)S(1)} %add.13), channel_id=1, source_target_pairs={{0,64},{16,80},{32,96},{48,112},{64,0},{80,16},{96,32},{112,48},{1... | collective-permute-start | bytes 36872 | tf_op jit(solution)/shard_map/cond/branch_1_fun/ppermute | solution.py:228
  99.8 5.6 %collective-permute-start.4 = (f32[1,1,3072]{2,1,0:T(1,128)S(1)}, f32[1,1,3072]{2,1,0:T(1,128)S(1)}, u32[]{:S(2)}, u32[]{:S(2)}) collective-permute-start(f32[1,1,3072]{2,1,0:T(1,128)S(1)} %add.14), channel_id=1, source_target_pairs={{0,128},{16,144},{32,160},{48,176},{64,192},{80,208},{96,224},{112... | collective-permute-start | bytes 36872 | tf_op jit(solution)/shard_map/cond/branch_1_fun/ppermute | solution.py:228
  105.4 6.6 %collective-permute-start.5 = (f32[1,1,3072]{2,1,0:T(1,128)S(1)}, f32[1,1,3072]{2,1,0:T(1,128)S(1)}, u32[]{:S(2)}, u32[]{:S(2)}) collective-permute-start(f32[1,1,3072]{2,1,0:T(1,128)S(1)} %add.15), channel_id=1, source_target_pairs={{0,256},{16,272},{32,288},{48,304},{64,320},{80,336},{96,352},{112... | collective-permute-start | bytes 36872 | tf_op jit(solution)/shard_map/cond/branch_1_fun/ppermute | solution.py:228
  112.0 9.6 %collective-permute-start.6 = (f32[1,1,3072]{2,1,0:T(1,128)S(1)}, f32[1,1,3072]{2,1,0:T(1,128)S(1)}, u32[]{:S(2)}, u32[]{:S(2)}) collective-permute-start(f32[1,1,3072]{2,1,0:T(1,128)S(1)} %add.16), channel_id=1, source_target_pairs={{0,512},{16,528},{32,544},{48,560},{64,576},{80,592},{96,608},{112... | collective-permute-start | bytes 36872 | tf_op jit(solution)/shard_map/cond/branch_1_fun/ppermute | solution.py:228
  121.6 2.2 %copy-start.5 = (f32[1,1,3072]{2,1,0:T(1,128)}, f32[1,1,3072]{2,1,0:T(1,128)S(1)}, u32[]{:S(2)}) copy-start(f32[1,1,3072]{2,1,0:T(1,128)S(1)} %get-tuple-element.55) | copy-start | bytes 36868

commit v7 on v5

--- a/solution.py
+++ b/solution.py
@@ -6,7 +6,7 @@
 from jax.sharding import PartitionSpec as P
 
 QUARTERS = 4
-STEPS = (0, 1, 7, 3, 5, 4, 2, 6)
+STEPS = (0, 3, 5, 2, 6, 4, 1, 7)
 LANES = 128
 SUBLANES = 8
 VMEM = 24 * 1024 * 1024
@@ -199,28 +199,28 @@
             compiler_params=params,
         )(parts)
 
-    own = add(lax.all_to_all(term, "exp", 0, 0, tiled=True), side)
-
     dealt = pl.pallas_call(
         deal_kernel,
         out_shape=(jax.ShapeDtypeStruct((2, stack, part), jnp.bfloat16),) * chips,
         compiler_params=params,
     )(kept, got)
-    copies = [dealt[0]]
-    for step, block in zip(STEPS[1:], dealt[1:]):
-        moves = [(i, (i + 2 * step) % windows) for i in range(windows)]
-        copies.append(lax.ppermute(block, "exp", moves))
-
-    def over_ctx(own):
-        across = [[x * side + z for x in range(side)] for z in range(side)]
-        along = [[x * side + z for z in range(side)] for x in range(side)]
-        for groups, count in ((across, side), (along, 1)):
-            parts = lax.all_to_all(own, "ctx", 0, 0, axis_index_groups=groups, tiled=True)
-            own = add(parts, count)
-        return own
-
-    own = unit(over_ctx, own)
-    place, own = lax.optimization_barrier((place, own))
+    across = [[x * side + z for x in range(side)] for z in range(side)]
+    along = [[x * side + z for z in range(side)] for x in range(side)]
+    copies, first = [dealt[0]], 1
+    own = term
+    for count, axis, groups, number in (
+        (side, "exp", None, 2),
+        (side, "ctx", across, 3),
+        (1, "ctx", along, 2),
+    ):
+        *blocks, own = lax.optimization_barrier((*dealt[first : first + number], own))
+        parts = lax.all_to_all(own, axis, 0, 0, axis_index_groups=groups, tiled=True)
+        for step, block in zip(STEPS[first:], blocks):
+            moves = [(i, (i + 2 * step) % windows) for i in range(windows)]
+            copies.append(lax.ppermute(block, "exp", moves))
+        own = add(parts, count)
+        first += number
+
     combined = pl.pallas_call(
         lambda *refs: combine_kernel(cap, depth, *refs),
         out_shape=jax.ShapeDtypeStruct((tokens, width), jnp.bfloat16),

time: 104 us -> 103 us (level)
  the two profiles are of different devices: /device:TPU:2 before, /device:TPU:44 now
where the time goes in v7:
time: 103 us; the launch traced here: 102 us
  starting transfers between devices  57 us (55%)
  blocking collectives  28.6 us (28%)
  Pallas kernels  10.7 us (10%)
  waiting for transfers between devices  2.55 us (2%)
  local copies, waits for them, and re-layouts  1.89 us (2%)
  between operations  1.46 us (1%)
    all_to_all x1, blocking collectives, shards(): lax.all_to_all(own, axis, 0, 0, axis_index_groups=groups, tiled=True)  28.6 us
    ppermute x7, starting transfers between devices, shards(): copies.append(lax.ppermute(block, 'exp', moves))  27.9 us
    all_to_all x2, starting transfers between devices, shards(): lax.all_to_all(own, axis, 0, 0, axis_index_groups=groups, tiled=True)  19.3 us
    all_to_all x1, starting transfers between devices, shards(): dots = lax.all_to_all(laid, 'exp', 0, 0, tiled=True)  7.68 us
    pallas_call x1, Pallas kernels, share(): pl.pallas_call(lambda *refs: pack_kernel(cap, *refs), out_shape=(half, ha...  2.98 us
    ppermute x1, waiting for transfers between devices, share(): lax.ppermute(given, 'exp', [(i, i ^ 1) for i in range(windows)])  2.53 us
    pallas_call x1, Pallas kernels, shards(): pl.pallas_call(deal_kernel, out_shape=(jax.ShapeDtypeStruct((2, stack, pa...  2.32 us
    pallas_call x1, Pallas kernels, shards(): pl.pallas_call(lambda *refs: combine_kernel(cap, depth, *refs), out_shape...  2.21 us
  transfers between devices with their start and end apart: 11, of which 1 were waited for; matrix products, arithmetic and copies ran while one was open for 1% of the time, Pallas kernels for 4%

profile of v7, /device:TPU:44, one launch (start us, length us, event | category | flops | bytes accessed | tf_op | source)
XLA Modules:
  0.0 102.2 jit_solution(5197905678936122143)
XLA Ops:
  0.6 0.7 copy-done.3
  1.3 0.8 shard_map.79
  2.1 7.7 %all-to-all-start = ((f32[16,1,128]{2,1,0:T(1,128)}), f32[16,1,128]{2,1,0:T(1,128)S(1)}, u32[]{:S(2)}, u32[]{:S(2)}) async-start(f32[16,1,128]{2,1,0:T(1,128)} %shard_map.79), calls=%async_computation | async-start | bytes 16384 | tf_op jit(solution)/shard_map/all_to_all | solution.py:168
  9.8 1.2 %slice.3 = s32[1,1,1]{1,2,0:T(1,128)} slice(s32[1,128,2]{1,2,0:T(2,128)} %param.9), slice={[0:1], [0:1], [0:1]} | slice | bytes 8 | tf_op jit(solution)/shard_map/slice | solution.py:156
  11.6 0.0 copy-start.4
  11.7 7.6 %conditional.1 = (bf16[8,80,768]{2,1,0:T(8,128)(2,1)}, bf16[8,80,768]{2,1,0:T(8,128)(2,1)}) conditional(s32[]{:T(128)} %bitcast.7, () %tuple.20, (bf16[1,1,320,3072]{3,2,1,0:T(8,128)(2,1)}) %tuple.26), branch_computations={%region_0.0_spmd, %region_1.0_spmd} | conditional | bytes 3932216 | solution.py:161
  11.7 3.0 %branch_1_fun.1 = (bf16[8,80,768]{2,1,0:T(8,128)(2,1)}, bf16[8,80,768]{2,1,0:T(8,128)(2,1)S(1)}) custom-call(bf16[320,3072]{1,0:T(8,128)(2,1)} %bitcast.16), custom_call_target="tpu_custom_call" | custom-call | tf_op jit(solution)/shard_map/cond/branch_1_fun/pallas_call | solution.py:173
  14.7 2.0 %collective-permute-start = (bf16[8,80,768]{2,1,0:T(8,128)(2,1)S(1)}, bf16[8,80,768]{2,1,0:T(8,128)(2,1)}, u32[]{:S(2)}, u32[]{:S(2)}) collective-permute-start(bf16[8,80,768]{2,1,0:T(8,128)(2,1)S(1)} %get-tuple-element.3), channel_id=1, source_target_pairs={{0,1},{1,0},{2,3},{3,2},{4,5},{5,4},{6,7},{7,6},{8,9},{9,8},{10,11... | collective-permute-start | bytes 2949128 | tf_op jit(solution)/shard_map/cond/branch_1_fun/ppermute | solution.py:178
  16.7 2.5 %collective-permute-done = bf16[8,80,768]{2,1,0:T(8,128)(2,1)} collective-permute-done((bf16[8,80,768]{2,1,0:T(8,128)(2,1)S(1)}, bf16[8,80,768]{2,1,0:T(8,128)(2,1)}, u32[]{:S(2)}, u32[]{:S(2)}) %collective-permute-start) | collective-permute-done | bytes 983072 | tf_op jit(solution)/shard_map/cond/branch_1_fun/ppermute | solution.py:178
  19.3 1.1 %shard_map.80 = (bf16[16,128]{1,0:T(8,128)(2,1)S(1)}, f32[128,8]{1,0:T(8,128)S(1)}, f32[16,1,3072]{2,1,0:T(1,128)}) custom-call(s32[2,128]{1,0:T(2,128)S(1)} %bitcast.15, f32[16,128]{1,0:T(8,128)S(1)} %bitcast.13, f32[16,1,128]{2,1,0:T(1,128)S(1)} %all-to-all-done.refs_2_, bf16[128,3072]{1,0:T(8,128)(2,1)S(1)} %bitcast.12), custom_call_target="tpu_custom_call" | custom-call | tf_op jit(solution)/shard_map/pallas_call | solution.py:184
  20.4 2.3 %shard_map.81 = (bf16[2,80,768]{2,1,0:T(8,128)(2,1)S(1)}, bf16[2,80,768]{2,1,0:T(8,128)(2,1)}, bf16[2,80,768]{2,1,0:T(8,128)(2,1)S(1)}, bf16[2,80,768]{2,1,0:T(8...) custom-call(bf16[8,80,768]{2,1,0:T(8,128)(2,1)} %get-tuple-element.3, ...), custom_call_target="tpu_custom_call" | custom-call | tf_op jit(solution)/shard_map/pallas_call | solution.py:202
  22.7 7.2 %all-to-all-start.1 = ((f32[16,1,3072]{2,1,0:T(1,128)}), f32[16,1,3072]{2,1,0:T(1,128)S(1)}, u32[]{:S(2)}, u32[]{:S(2)}) async-start(f32[16,1,3072]{2,1,0:T(1,128)} %get-tuple-element.46), calls=%async_computation.1 | async-start | bytes 393216 | tf_op jit(solution)/shard_map/all_to_all | solution.py:217
  29.9 5.5 %collective-permute-start.1 = (bf16[2,80,768]{2,1,0:T(8,128)(2,1)}, bf16[2,80,768]{2,1,0:T(8,128)(2,1)S(1)}, u32[]{:S(2)}, u32[]{:S(2)}) collective-permute-start(bf16[2,80,768]{2,1,0:T(8,128)(2,1)} %get-tuple-element.41), channel_id=1, source_target_pairs={{0,6},{1,7},{2,8},{3,9},{4,10},{5,11},{6,12},{7,13},{8,14},{9,15},... | collective-permute-start | bytes 737288 | tf_op jit(solution)/shard_map/ppermute | solution.py:220
  35.4 3.4 %collective-permute-start.2 = (bf16[2,80,768]{2,1,0:T(8,128)(2,1)S(1)}, bf16[2,80,768]{2,1,0:T(8,128)(2,1)S(1)}, u32[]{:S(2)}, u32[]{:S(2)}) collective-permute-start(bf16[2,80,768]{2,1,0:T(8,128)(2,1)S(1)} %get-tuple-element.42), channel_id=1, source_target_pairs={{0,10},{1,11},{2,12},{3,13},{4,14},{5,15},{6,0},{7,1},{8,2},{9,3},... | collective-permute-start | bytes 737288 | tf_op jit(solution)/shard_map/ppermute | solution.py:220
  38.8 0.7 shard_map.82
  39.5 12.1 %all-to-all-start.2 = ((f32[8,1,3072]{2,1,0:T(1,128)}), f32[8,1,3072]{2,1,0:T(1,128)S(1)}, u32[]{:S(2)}, u32[]{:S(2)}) async-start(f32[8,1,3072]{2,1,0:T(1,128)} %shard_map.82), calls=%async_computation.2 | async-start | bytes 196608 | tf_op jit(solution)/shard_map/all_to_all | solution.py:217
  51.5 5.5 %collective-permute-start.3 = (bf16[2,80,768]{2,1,0:T(8,128)(2,1)S(1)}, bf16[2,80,768]{2,1,0:T(8,128)(2,1)S(1)}, u32[]{:S(2)}, u32[]{:S(2)}) collective-permute-start(bf16[2,80,768]{2,1,0:T(8,128)(2,1)S(1)} %get-tuple-element.47), channel_id=1, source_target_pairs={{0,4},{1,5},{2,6},{3,7},{4,8},{5,9},{6,10},{7,11},{8,12},{9,13},{1... | collective-permute-start | bytes 737288 | tf_op jit(solution)/shard_map/ppermute | solution.py:220
  57.0 1.9 %collective-permute-start.4 = (bf16[2,80,768]{2,1,0:T(8,128)(2,1)S(1)}, bf16[2,80,768]{2,1,0:T(8,128)(2,1)S(1)}, u32[]{:S(2)}, u32[]{:S(2)}) collective-permute-start(bf16[2,80,768]{2,1,0:T(8,128)(2,1)S(1)} %get-tuple-element.48), channel_id=1, source_target_pairs={{0,12},{1,13},{2,14},{3,15},{4,0},{5,1},{6,2},{7,3},{8,4},{9,5},{1... | collective-permute-start | bytes 737288 | tf_op jit(solution)/shard_map/ppermute | solution.py:220
  58.9 4.8 %collective-permute-start.5 = (bf16[2,80,768]{2,1,0:T(8,128)(2,1)S(1)}, bf16[2,80,768]{2,1,0:T(8,128)(2,1)S(1)}, u32[]{:S(2)}, u32[]{:S(2)}) collective-permute-start(bf16[2,80,768]{2,1,0:T(8,128)(2,1)S(1)} %get-tuple-element.49), channel_id=1, source_target_pairs={{0,8},{1,9},{2,10},{3,11},{4,12},{5,13},{6,14},{7,15},{8,0},{9,1},... | collective-permute-start | bytes 737288 | tf_op jit(solution)/shard_map/ppermute | solution.py:220
  63.8 2.3 %collective-permute-start.6 = (bf16[2,80,768]{2,1,0:T(8,128)(2,1)S(1)}, bf16[2,80,768]{2,1,0:T(8,128)(2,1)S(1)}, u32[]{:S(2)}, u32[]{:S(2)}) collective-permute-start(bf16[2,80,768]{2,1,0:T(8,128)(2,1)S(1)} %get-tuple-element.53), channel_id=1, source_target_pairs={{0,2},{1,3},{2,4},{3,5},{4,6},{5,7},{6,8},{7,9},{8,10},{9,11},{10,... | collective-permute-start | bytes 737288 | tf_op jit(solution)/shard_map/ppermute | solution.py:220
  66.1 4.6 %collective-permute-start.7 = (bf16[2,80,768]{2,1,0:T(8,128)(2,1)S(1)}, bf16[2,80,768]{2,1,0:T(8,128)(2,1)S(1)}, u32[]{:S(2)}, u32[]{:S(2)}) collective-permute-start(bf16[2,80,768]{2,1,0:T(8,128)(2,1)S(1)} %get-tuple-element.54), channel_id=1, source_target_pairs={{0,14},{1,15},{2,0},{3,1},{4,2},{5,3},{6,4},{7,5},{8,6},{9,7},{10,... | collective-permute-start | bytes 737288 | tf_op jit(solution)/shard_map/ppermute | solution.py:220
  70.7 28.6 %all_to_all.20.parts_ref = f32[8,1,3072]{2,1,0:T(1,128)S(1)} all-to-all(f32[8,1,3072]{2,1,0:T(1,128)S(1)} %shard_map.83), channel_id=1, replica_groups={{0,16,32,48,64,80,96,112},{128,144,160,176,192,208,224,240},{256,272,28..., dimensions={0} | all-to-all | bytes 196608 | tf_op jit(solution)/shard_map/all_to_all | solution.py:217
  99.4 0.6 shard_map.85
  100.0 2.2 %shard_map.84 = bf16[128,3072]{1,0:T(8,128)(2,1)} custom-call(f32[128,8]{1,0:T(8,128)S(1)} %get-tuple-element.31.refs_0_, bf16[16,128]{1,0:T(8,128)(2,1)S(1)} %get-tuple-element.32.refs_1_, bf16[16,3072]{1,0:T(8,128)(2,1)S(1)} %copy-done.1, bf16[2,80,768]{2,1,0:T(8,128)(2,1)S(1)} %get-tuple-element.37.refs_3_, ...), custom_call_target="tpu_custom_call" | custom-call | tf_op jit(solution)/shard_map/pallas_call | solution.py:224
  (19 shorter events, 0.1 us)
Async XLA Ops:
  0.6 0.7 copy-start.3
  2.1 17.1 %all-to-all-start = ((f32[16,1,128]{2,1,0:T(1,128)}), f32[16,1,128]{2,1,0:T(1,128)S(1)}, u32[]{:S(2)}, u32[]{:S(2)}) async-start(f32[16,1,128]{2,1,0:T(1,128)} %shard_map.79), calls=%async_computation | async-start | bytes 16384 | tf_op jit(solution)/shard_map/all_to_all | solution.py:168
  11.6 7.6 %copy-start = (bf16[1,128,3072]{2,1,0:T(8,128)(2,1)S(1)}, bf16[1,128,3072]{2,1,0:T(8,128)(2,1)}, u32[]{:S(2)}) copy-start(bf16[1,128,3072]{2,1,0:T(8,128)(2,1)} %param.8) | copy-start | bytes 2359300
  11.6 7.6 %copy-start.2 = (f32[1,128,16]{1,2,0:T(8,128)S(1)}, f32[1,128,16]{1,2,0:T(8,128)}, u32[]{:S(2)}) copy-start(f32[1,128,16]{1,2,0:T(8,128)} %param.10) | copy-start | bytes 24580
  11.6 7.6 %copy-start.4 = (s32[1,128,2]{1,2,0:T(2,128)S(1)}, s32[1,128,2]{1,2,0:T(2,128)}, u32[]{:S(2)}) copy-start(s32[1,128,2]{1,2,0:T(2,128)} %param.9) | copy-start | bytes 3076
  14.7 4.6 %collective-permute-start = (bf16[8,80,768]{2,1,0:T(8,128)(2,1)S(1)}, bf16[8,80,768]{2,1,0:T(8,128)(2,1)}, u32[]{:S(2)}, u32[]{:S(2)}) collective-permute-start(bf16[8,80,768]{2,1,0:T(8,128)(2,1)S(1)} %get-tuple-element.3), channel_id=1, source_target_pairs={{0,1},{1,0},{2,3},{3,2},{4,5},{5,4},{6,7},{7,6},{8,9},{9,8},{10,11... | collective-permute-start | bytes 2949128 | tf_op jit(solution)/shard_map/cond/branch_1_fun/ppermute | solution.py:178
  19.3 80.8 %copy-start.1 = (bf16[16,3072]{1,0:T(8,128)(2,1)S(1)}, bf16[16,3072]{1,0:T(8,128)(2,1)}, u32[]{:S(2)}) copy-start(bf16[16,3072]{1,0:T(8,128)(2,1)} %refs_2_.1) | copy-start | bytes 294916
  22.7 16.1 %all-to-all-start.1 = ((f32[16,1,3072]{2,1,0:T(1,128)}), f32[16,1,3072]{2,1,0:T(1,128)S(1)}, u32[]{:S(2)}, u32[]{:S(2)}) async-start(f32[16,1,3072]{2,1,0:T(1,128)} %get-tuple-element.46), calls=%async_computation.1 | async-start | bytes 393216 | tf_op jit(solution)/shard_map/all_to_all | solution.py:217
  29.9 33.9 %collective-permute-start.1 = (bf16[2,80,768]{2,1,0:T(8,128)(2,1)}, bf16[2,80,768]{2,1,0:T(8,128)(2,1)S(1)}, u32[]{:S(2)}, u32[]{:S(2)}) collective-permute-start(bf16[2,80,768]{2,1,0:T(8,128)(2,1)} %get-tuple-element.41), channel_id=1, source_target_pairs={{0,6},{1,7},{2,8},{3,9},{4,10},{5,11},{6,12},{7,13},{8,14},{9,15},... | collective-permute-start | bytes 737288 | tf_op jit(solution)/shard_map/ppermute | solution.py:220
  35.4 30.7 %collective-permute-start.2 = (bf16[2,80,768]{2,1,0:T(8,128)(2,1)S(1)}, bf16[2,80,768]{2,1,0:T(8,128)(2,1)S(1)}, u32[]{:S(2)}, u32[]{:S(2)}) collective-permute-start(bf16[2,80,768]{2,1,0:T(8,128)(2,1)S(1)} %get-tuple-element.42), channel_id=1, source_target_pairs={{0,10},{1,11},{2,12},{3,13},{4,14},{5,15},{6,0},{7,1},{8,2},{9,3},... | collective-permute-start | bytes 737288 | tf_op jit(solution)/shard_map/ppermute | solution.py:220
  39.5 24.3 %all-to-all-start.2 = ((f32[8,1,3072]{2,1,0:T(1,128)}), f32[8,1,3072]{2,1,0:T(1,128)S(1)}, u32[]{:S(2)}, u32[]{:S(2)}) async-start(f32[8,1,3072]{2,1,0:T(1,128)} %shard_map.82), calls=%async_computation.2 | async-start | bytes 196608 | tf_op jit(solution)/shard_map/all_to_all | solution.py:217
  51.5 48.5 %collective-permute-start.3 = (bf16[2,80,768]{2,1,0:T(8,128)(2,1)S(1)}, bf16[2,80,768]{2,1,0:T(8,128)(2,1)S(1)}, u32[]{:S(2)}, u32[]{:S(2)}) collective-permute-start(bf16[2,80,768]{2,1,0:T(8,128)(2,1)S(1)} %get-tuple-element.47), channel_id=1, source_target_pairs={{0,4},{1,5},{2,6},{3,7},{4,8},{5,9},{6,10},{7,11},{8,12},{9,13},{1... | collective-permute-start | bytes 737288 | tf_op jit(solution)/shard_map/ppermute | solution.py:220
  57.0 43.0 %collective-permute-start.4 = (bf16[2,80,768]{2,1,0:T(8,128)(2,1)S(1)}, bf16[2,80,768]{2,1,0:T(8,128)(2,1)S(1)}, u32[]{:S(2)}, u32[]{:S(2)}) collective-permute-start(bf16[2,80,768]{2,1,0:T(8,128)(2,1)S(1)} %get-tuple-element.48), channel_id=1, source_target_pairs={{0,12},{1,13},{2,14},{3,15},{4,0},{5,1},{6,2},{7,3},{8,4},{9,5},{1... | collective-permute-start | bytes 737288 | tf_op jit(solution)/shard_map/ppermute | solution.py:220
  58.9 41.1 %collective-permute-start.5 = (bf16[2,80,768]{2,1,0:T(8,128)(2,1)S(1)}, bf16[2,80,768]{2,1,0:T(8,128)(2,1)S(1)}, u32[]{:S(2)}, u32[]{:S(2)}) collective-permute-start(bf16[2,80,768]{2,1,0:T(8,128)(2,1)S(1)} %get-tuple-element.49), channel_id=1, source_target_pairs={{0,8},{1,9},{2,10},{3,11},{4,12},{5,13},{6,14},{7,15},{8,0},{9,1},... | collective-permute-start | bytes 737288 | tf_op jit(solution)/shard_map/ppermute | solution.py:220
  63.8 36.2 %collective-permute-start.6 = (bf16[2,80,768]{2,1,0:T(8,128)(2,1)S(1)}, bf16[2,80,768]{2,1,0:T(8,128)(2,1)S(1)}, u32[]{:S(2)}, u32[]{:S(2)}) collective-permute-start(bf16[2,80,768]{2,1,0:T(8,128)(2,1)S(1)} %get-tuple-element.53), channel_id=1, source_target_pairs={{0,2},{1,3},{2,4},{3,5},{4,6},{5,7},{6,8},{7,9},{8,10},{9,11},{10,... | collective-permute-start | bytes 737288 | tf_op jit(solution)/shard_map/ppermute | solution.py:220
  66.1 33.9 %collective-permute-start.7 = (bf16[2,80,768]{2,1,0:T(8,128)(2,1)S(1)}, bf16[2,80,768]{2,1,0:T(8,128)(2,1)S(1)}, u32[]{:S(2)}, u32[]{:S(2)}) collective-permute-start(bf16[2,80,768]{2,1,0:T(8,128)(2,1)S(1)} %get-tuple-element.54), channel_id=1, source_target_pairs={{0,14},{1,15},{2,0},{3,1},{4,2},{5,3},{6,4},{7,5},{8,6},{9,7},{10,... | collective-permute-start | bytes 737288 | tf_op jit(solution)/shard_map/ppermute | solution.py:220

commit v8 on v6

--- a/solution.py
+++ b/solution.py
@@ -6,7 +6,6 @@
 from jax.sharding import PartitionSpec as P
 
 QUARTERS = 4
-STEPS = (3, 5, 1, 7)
 LANES = 128
 SUBLANES = 8
 VMEM = 24 * 1024 * 1024
@@ -34,34 +33,15 @@
     out_ref[...] = laid[:, None, :]
 
 
-def pack_kernel(cap, rows_ref, even_ref, kept_ref, given_ref):
-    part = even_ref.shape[2]
-    chip, core = lax.axis_index("exp") // 2, lax.axis_index("exp") % 2
+def pack_kernel(cap, rows_ref, out_ref):
+    part = out_ref.shape[2]
     rows = rows_ref[...].astype(jnp.float32)
-    for group in range(kept_ref.shape[0]):
-        stacks = []
-        for w in range(4 * group, 4 * group + 4):
-            window = rows[w * cap : (w + 1) * cap]
-            stacked = jnp.concatenate(
-                [window[:, q * part : (q + 1) * part] for q in range(QUARTERS)], axis=0
-            )
-            stacks.append(stacked)
-        same = chip % 2 == 0
-        for n in range(2):
-            even = jnp.where(same, stacks[n], stacks[2 + n])
-            even_ref[2 * group + n] = even.astype(jnp.bfloat16)
-        odd = [jnp.where(same, stacks[2 + n], stacks[n]) for n in range(2)]
-        kept_ref[group] = jnp.where(core == 0, odd[0], odd[1]).astype(jnp.bfloat16)
-        given_ref[group] = jnp.where(core == 0, odd[1], odd[0]).astype(jnp.bfloat16)
-
-
-def deal_kernel(kept_ref, got_ref, *out_refs):
-    chips = 2 * kept_ref.shape[0]
-    chip = lax.axis_index("exp") // 2
-    for step, out_ref in zip(STEPS, out_refs):
-        target = (chip + step) % chips // 2
-        out_ref[0] = kept_ref[target]
-        out_ref[1] = got_ref[target]
+    for w in range(out_ref.shape[0]):
+        window = rows[w * cap : (w + 1) * cap]
+        stacked = jnp.concatenate(
+            [window[:, q * part : (q + 1) * part] for q in range(QUARTERS)], axis=0
+        )
+        out_ref[w] = stacked.astype(jnp.bfloat16)
 
 
 def sum_kernel(parts_ref, out_ref):
@@ -105,14 +85,9 @@
     logit = probs * (router_grad - jnp.sum(probs * router_grad, axis=0, keepdims=True))
     logit = logit.astype(jnp.bfloat16)
     logit_ref[...] = logit
-    chip, core = lax.axis_index("exp") // 2, lax.axis_index("exp") % 2
     rows = []
     for k in range(2):
-        ids = ids_ref[k : k + 1, :]
-        step = (chip - ids // 2 + experts // 2) % (experts // 2)
-        place = sum(jnp.where(step == STEPS[n], n, 0) for n in range(len(STEPS)))
-        odd = place * 2 + (ids % 2 + core) % 2
-        block = jnp.where(step % 2 == 1, odd, experts // 2 + ids // 4 * 2 + ids % 2)
+        block = ids_ref[k : k + 1, :]
         rows.append((block * depth + slots[k]).astype(jnp.float32))
     place = jnp.concatenate(
         [picked[0] / total, picked[1] / total] + rows + [jnp.zeros((4, tokens), jnp.float32)],
@@ -123,16 +98,14 @@
     term_ref[...] = term[:, None, :]
 
 
-def combine_kernel(cap, depth, place_ref, logit_ref, weight_ref, *refs):
-    out_ref = refs[-1]
+def combine_kernel(cap, depth, place_ref, logit_ref, weight_ref, copies_ref, out_ref):
     tokens, width = out_ref.shape
     filler = jnp.zeros((depth - cap, width), jnp.float32)
     table = []
-    for ref in refs[:-1]:
-        for n in range(ref.shape[0]):
-            stacked = ref[n].astype(jnp.float32)
-            rows = [stacked[q * cap : (q + 1) * cap] for q in range(QUARTERS)]
-            table += [jnp.concatenate(rows, axis=1), filler]
+    for expert in range(copies_ref.shape[0]):
+        stacked = copies_ref[expert].astype(jnp.float32)
+        rows = [stacked[q * cap : (q + 1) * cap] for q in range(QUARTERS)]
+        table += [jnp.concatenate(rows, axis=1), filler]
     copies = jnp.concatenate(table, axis=0).astype(jnp.bfloat16)
     column = lax.broadcasted_iota(jnp.int32, (tokens, copies.shape[0]), 1)
     spread = jnp.zeros(column.shape, jnp.float32)
@@ -152,7 +125,6 @@
     slots, width = expert_grads.shape[2:]
     tokens, experts = router_probs.shape[1:]
     windows = lax.axis_size("exp")
-    chips = windows // 2
     cap = slots // windows
     part = width // QUARTERS
     stack = cap * QUARTERS
@@ -173,19 +145,13 @@
     )(gate_dots[0])
     dots = lax.all_to_all(laid, "exp", 0, 0, tiled=True)
 
-    def blocks_of(count):
-        return jax.ShapeDtypeStruct((count, stack, part), jnp.bfloat16)
-
-    def share(rows):
-        even, kept, given = pl.pallas_call(
-            lambda *refs: pack_kernel(cap, *refs),
-            out_shape=(blocks_of(chips), blocks_of(chips // 2), blocks_of(chips // 2)),
-            compiler_params=params,
-        )(rows)
-        return even, kept, lax.ppermute(given, "exp", [(i, i ^ 1) for i in range(windows)])
-
-    even, kept, got = unit(share, expert_grads[0, 0])
-
+    packed = pl.pallas_call(
+        lambda *refs: pack_kernel(cap, *refs),
+        out_shape=jax.ShapeDtypeStruct((windows, stack, part), jnp.bfloat16),
+        compiler_params=params,
+    )(expert_grads[0, 0])
+
+    dots, packed = lax.optimization_barrier((dots, packed))
     ids = jnp.swapaxes(expert_ids, 1, 2)[0]
     probs = jnp.swapaxes(router_probs, 1, 2)[0]
     logit, place, term = pl.pallas_call(
@@ -197,8 +163,6 @@
         ),
         compiler_params=params,
     )(ids, probs, dots, layer_input[0])
-    got, term = lax.optimization_barrier((got, term))
-
     def add(parts, count):
         return pl.pallas_call(
             sum_kernel,
@@ -208,18 +172,8 @@
 
     own = add(lax.all_to_all(term, "exp", 0, 0, tiled=True), 1)
 
-    dealt = pl.pallas_call(
-        deal_kernel,
-        out_shape=(blocks_of(2),) * len(STEPS),
-        compiler_params=params,
-    )(kept, got)
-    copies = []
-    for step, block in zip(STEPS, dealt):
-        moves = [(i, (i + 2 * step) % windows) for i in range(windows)]
-        copies.append(lax.ppermute(block, "exp", moves))
-    alike = [[i for i in range(windows) if i // 2 % 2 == parity] for parity in range(2)]
-    even, own, *copies[:2] = lax.optimization_barrier((even, own, *copies[:2]))
-    copies.append(lax.all_to_all(even, "exp", 0, 0, axis_index_groups=alike, tiled=True))
+    packed, own = lax.optimization_barrier((packed, own))
+    copies = lax.all_to_all(packed, "exp", 0, 0, tiled=True)
 
     def over_ctx(own):
         bit = 1
@@ -235,7 +189,7 @@
         lambda *refs: combine_kernel(cap, depth, *refs),
         out_shape=jax.ShapeDtypeStruct((tokens, width), jnp.bfloat16),
         compiler_params=params,
-    )(place, logit, router_weight, *copies)
+    )(place, logit, router_weight, copies)
     return combined[None], own[0]
 
 

time: 125 us -> 92.9 us (0.74)
  the two profiles are of different devices: /device:TPU:10 before, /device:TPU:1 now
where the time goes in v8:
time: 92.9 us; the launch traced here: 92.4 us
  starting transfers between devices  46.7 us (50%)
  waiting for transfers between devices  22.9 us (25%)
  blocking collectives  13.5 us (15%)
  Pallas kernels  5.02 us (5%)
  local copies, waits for them, and re-layouts  2.75 us (3%)
  between operations  1.35 us (1%)
    ppermute x6, starting transfers between devices, over_ctx(): own = own + lax.ppermute(own, 'ctx', moves)  25.5 us
    all_to_all x1, starting transfers between devices, shards(): dots = lax.all_to_all(laid, 'exp', 0, 0, tiled=True)  17.4 us
    all_to_all x1, blocking collectives, shards(): own = add(lax.all_to_all(term, 'exp', 0, 0, tiled=True), 1)  13.5 us
    ppermute x6, waiting for transfers between devices, over_ctx(): own = own + lax.ppermute(own, 'ctx', moves)  13.4 us
    all_to_all x1, waiting for transfers between devices, shards(): copies = lax.all_to_all(packed, 'exp', 0, 0, tiled=True)  5.61 us
    all_to_all x1, waiting for transfers between devices, shards(): dots = lax.all_to_all(laid, 'exp', 0, 0, tiled=True)  3.87 us
    all_to_all x1, starting transfers between devices, shards(): copies = lax.all_to_all(packed, 'exp', 0, 0, tiled=True)  3.76 us
    unnamed x14, local copies, waits for them, and re-layouts  2.24 us
  transfers between devices with their start and end apart: 8, of which 8 were waited for; matrix products, arithmetic and copies ran while one was open for 1% of the time, Pallas kernels for 2%

profile of v8, /device:TPU:1, one launch (start us, length us, event | category | flops | bytes accessed | tf_op | source)
XLA Modules:
  0.0 92.4 jit_solution(13179432589478826935)
XLA Ops:
  0.6 0.7 copy-done.4
  1.3 0.8 shard_map.77
  2.1 17.4 %all-to-all-start = ((f32[16,1,128]{2,1,0:T(1,128)}), f32[16,1,128]{2,1,0:T(1,128)S(1)}, u32[]{:S(2)}, u32[]{:S(2)}) async-start(f32[16,1,128]{2,1,0:T(1,128)} %shard_map.77), calls=%async_computation | async-start | bytes 16384 | tf_op jit(solution)/shard_map/all_to_all | solution.py:146
  19.5 1.5 %copy-done = bf16[1,1,320,3072]{3,2,1,0:T(8,128)(2,1)S(1)} copy-done((bf16[1,1,320,3072]{3,2,1,0:T(8,128)(2,1)S(1)}, bf16[1,1,320,3072]{3,2,1,0:T(8,128)(2,1)}, u32[]{:S(2)}) %copy-start) | copy-done | bytes 1966104
  21.1 1.6 %shard_map.78 = bf16[16,80,768]{2,1,0:T(8,128)(2,1)} custom-call(bf16[320,3072]{1,0:T(8,128)(2,1)S(1)} %bitcast.12), custom_call_target="tpu_custom_call" | custom-call | tf_op jit(solution)/shard_map/pallas_call | solution.py:148
  22.6 3.9 %all-to-all-done.refs_2_ = f32[16,1,128]{2,1,0:T(1,128)S(1)} async-done(((f32[16,1,128]{2,1,0:T(1,128)}), f32[16,1,128]{2,1,0:T(1,128)S(1)}, u32[]{:S(2)}, u32[]{:S(2)}) %all-to-all-start) | async-done | bytes 8224 | tf_op jit(solution)/shard_map/all_to_all | solution.py:146
  27.0 13.5 %all_to_all.15.parts_ref = f32[16,1,3072]{2,1,0:T(1,128)S(1)} all-to-all(f32[16,1,3072]{2,1,0:T(1,128)S(1)} %get-tuple-element.18), channel_id=1, replica_groups=mesh['ctx'=64,'exp'=16] {'exp'}, dimensions={0} | all-to-all | bytes 393216 | tf_op jit(solution)/shard_map/all_to_all | solution.py:173
  40.5 3.8 %all-to-all-start.2 = ((bf16[16,80,768]{2,1,0:T(8,128)(2,1)}), bf16[16,80,768]{2,1,0:T(8,128)(2,1)S(1)}, u32[]{:S(2)}, u32[]{:S(2)}) async-start(bf16[16,80,768]{2,1,0:T(8,128)(2,1)} %shard_map.78), calls=%async_computation.2 | async-start | bytes 3932160 | tf_op jit(solution)/shard_map/all_to_all | solution.py:176
  44.3 0.5 slice.3
  45.5 39.1 %conditional.1 = (f32[1,1,3072]{2,1,0:T(1,128)S(1)}) conditional(s32[]{:T(128)} %bitcast.7, () %tuple.18, f32[1,1,3072]{2,1,0:T(1,128)S(1)} %shard_map.80), branch_computations={%region_0.0_spmd, %region_1.0_spmd} | conditional | flops 18432 | bytes 516344 | solution.py:139
  45.5 1.9 %collective-permute-start = (f32[1,1,3072]{2,1,0:T(1,128)S(1)}, f32[1,1,3072]{2,1,0:T(1,128)S(1)}, u32[]{:S(2)}, u32[]{:S(2)}) collective-permute-start(f32[1,1,3072]{2,1,0:T(1,128)S(1)} %param.1), channel_id=1, source_target_pairs={{0,16},{16,0},{32,48},{48,32},{64,80},{80,64},{96,112},{112,96},{1... | collective-permute-start | bytes 36872 | tf_op jit(solution)/shard_map/cond/branch_1_fun/ppermute | solution.py:182
  47.4 2.8 %collective-permute-done = f32[1,1,3072]{2,1,0:T(1,128)S(1)} collective-permute-done((f32[1,1,3072]{2,1,0:T(1,128)S(1)}, f32[1,1,3072]{2,1,0:T(1,128)S(1)}, u32[]{:S(2)}, u32[]{:S(2)}) %collective-permute-start) | collective-permute-done | bytes 12320 | tf_op jit(solution)/shard_map/cond/branch_1_fun/ppermute | solution.py:182
  50.2 1.9 %collective-permute-start.1 = (f32[1,1,3072]{2,1,0:T(1,128)S(1)}, f32[1,1,3072]{2,1,0:T(1,128)S(1)}, u32[]{:S(2)}, u32[]{:S(2)}) collective-permute-start(f32[1,1,3072]{2,1,0:T(1,128)S(1)} %add.12), channel_id=1, source_target_pairs={{0,32},{16,48},{32,0},{48,16},{64,96},{80,112},{96,64},{112,80},{1... | collective-permute-start | bytes 36872 | tf_op jit(solution)/shard_map/cond/branch_1_fun/ppermute | solution.py:182
  52.2 3.7 %collective-permute-done.1 = f32[1,1,3072]{2,1,0:T(1,128)S(1)} collective-permute-done((f32[1,1,3072]{2,1,0:T(1,128)S(1)}, f32[1,1,3072]{2,1,0:T(1,128)S(1)}, u32[]{:S(2)}, u32[]{:S(2)}) %collective-permute-start.1) | collective-permute-done | bytes 12320 | tf_op jit(solution)/shard_map/cond/branch_1_fun/ppermute | solution.py:182
  55.9 8.2 %collective-permute-start.2 = (f32[1,1,3072]{2,1,0:T(1,128)S(1)}, f32[1,1,3072]{2,1,0:T(1,128)S(1)}, u32[]{:S(2)}, u32[]{:S(2)}) collective-permute-start(f32[1,1,3072]{2,1,0:T(1,128)S(1)} %add.13), channel_id=1, source_target_pairs={{0,64},{16,80},{32,96},{48,112},{64,0},{80,16},{96,32},{112,48},{1... | collective-permute-start | bytes 36872 | tf_op jit(solution)/shard_map/cond/branch_1_fun/ppermute | solution.py:182
  64.1 1.4 %collective-permute-done.2 = f32[1,1,3072]{2,1,0:T(1,128)S(1)} collective-permute-done((f32[1,1,3072]{2,1,0:T(1,128)S(1)}, f32[1,1,3072]{2,1,0:T(1,128)S(1)}, u32[]{:S(2)}, u32[]{:S(2)}) %collective-permute-start.2) | collective-permute-done | bytes 12320 | tf_op jit(solution)/shard_map/cond/branch_1_fun/ppermute | solution.py:182
  65.5 2.8 %collective-permute-start.3 = (f32[1,1,3072]{2,1,0:T(1,128)S(1)}, f32[1,1,3072]{2,1,0:T(1,128)S(1)}, u32[]{:S(2)}, u32[]{:S(2)}) collective-permute-start(f32[1,1,3072]{2,1,0:T(1,128)S(1)} %add.14), channel_id=1, source_target_pairs={{0,128},{16,144},{32,160},{48,176},{64,192},{80,208},{96,224},{112... | collective-permute-start | bytes 36872 | tf_op jit(solution)/shard_map/cond/branch_1_fun/ppermute | solution.py:182
  68.3 1.9 %collective-permute-done.3 = f32[1,1,3072]{2,1,0:T(1,128)S(1)} collective-permute-done((f32[1,1,3072]{2,1,0:T(1,128)S(1)}, f32[1,1,3072]{2,1,0:T(1,128)S(1)}, u32[]{:S(2)}, u32[]{:S(2)}) %collective-permute-start.3) | collective-permute-done | bytes 12320 | tf_op jit(solution)/shard_map/cond/branch_1_fun/ppermute | solution.py:182
  70.3 3.8 %collective-permute-start.4 = (f32[1,1,3072]{2,1,0:T(1,128)S(1)}, f32[1,1,3072]{2,1,0:T(1,128)S(1)}, u32[]{:S(2)}, u32[]{:S(2)}) collective-permute-start(f32[1,1,3072]{2,1,0:T(1,128)S(1)} %add.15), channel_id=1, source_target_pairs={{0,256},{16,272},{32,288},{48,304},{64,320},{80,336},{96,352},{112... | collective-permute-start | bytes 36872 | tf_op jit(solution)/shard_map/cond/branch_1_fun/ppermute | solution.py:182
  74.0 1.9 %collective-permute-done.4 = f32[1,1,3072]{2,1,0:T(1,128)S(1)} collective-permute-done((f32[1,1,3072]{2,1,0:T(1,128)S(1)}, f32[1,1,3072]{2,1,0:T(1,128)S(1)}, u32[]{:S(2)}, u32[]{:S(2)}) %collective-permute-start.4) | collective-permute-done | bytes 12320 | tf_op jit(solution)/shard_map/cond/branch_1_fun/ppermute | solution.py:182
  75.9 6.8 %collective-permute-start.5 = (f32[1,1,3072]{2,1,0:T(1,128)S(1)}, f32[1,1,3072]{2,1,0:T(1,128)S(1)}, u32[]{:S(2)}, u32[]{:S(2)}) collective-permute-start(f32[1,1,3072]{2,1,0:T(1,128)S(1)} %add.16), channel_id=1, source_target_pairs={{0,512},{16,528},{32,544},{48,560},{64,576},{80,592},{96,608},{112... | collective-permute-start | bytes 36872 | tf_op jit(solution)/shard_map/cond/branch_1_fun/ppermute | solution.py:182
  82.7 1.8 %collective-permute-done.5 = f32[1,1,3072]{2,1,0:T(1,128)S(1)} collective-permute-done((f32[1,1,3072]{2,1,0:T(1,128)S(1)}, f32[1,1,3072]{2,1,0:T(1,128)S(1)}, u32[]{:S(2)}, u32[]{:S(2)}) %collective-permute-start.5) | collective-permute-done | bytes 12320 | tf_op jit(solution)/shard_map/cond/branch_1_fun/ppermute | solution.py:182
  84.6 5.6 %all-to-all-done.2.refs_3_ = bf16[16,80,768]{2,1,0:T(8,128)(2,1)S(1)} async-done(((bf16[16,80,768]{2,1,0:T(8,128)(2,1)}), bf16[16,80,768]{2,1,0:T(8,128)(2,1)S(1)}, u32[]{:S(2)}, u32[]{:S(2)}) %all-to-all-start.2) | async-done | bytes 1966112 | tf_op jit(solution)/shard_map/all_to_all | solution.py:176
  90.2 2.2 %shard_map.81 = bf16[128,3072]{1,0:T(8,128)(2,1)} custom-call(f32[128,8]{1,0:T(8,128)S(1)} %get-tuple-element.20.refs_0_, bf16[16,128]{1,0:T(8,128)(2,1)S(1)} %get-tuple-element.21.refs_1_, bf16[16,3072]{1,0:T(8,128)(2,1)S(1)} %copy-done.2, bf16[16,80,768]{2,1,0:T(8,128)(2,1)S(1)} %all-to-all-done.2.refs_3_), custom_call_target="tpu_custom_call" | custom-call | tf_op jit(solution)/shard_map/pallas_call | solution.py:188
  (20 shorter events, 0.6 us)
Async XLA Ops:
  0.6 0.7 copy-start.4
  2.1 24.4 %all-to-all-start = ((f32[16,1,128]{2,1,0:T(1,128)}), f32[16,1,128]{2,1,0:T(1,128)S(1)}, u32[]{:S(2)}, u32[]{:S(2)}) async-start(f32[16,1,128]{2,1,0:T(1,128)} %shard_map.77), calls=%async_computation | async-start | bytes 16384 | tf_op jit(solution)/shard_map/all_to_all | solution.py:146
  19.5 1.5 %copy-start = (bf16[1,1,320,3072]{3,2,1,0:T(8,128)(2,1)S(1)}, bf16[1,1,320,3072]{3,2,1,0:T(8,128)(2,1)}, u32[]{:S(2)}) copy-start(bf16[1,1,320,3072]{3,2,1,0:T(8,128)(2,1)} %param.12) | copy-start | bytes 5898244
  21.1 5.4 %copy-start.1 = (bf16[1,128,3072]{2,1,0:T(8,128)(2,1)S(1)}, bf16[1,128,3072]{2,1,0:T(8,128)(2,1)}, u32[]{:S(2)}) copy-start(bf16[1,128,3072]{2,1,0:T(8,128)(2,1)} %param.8) | copy-start | bytes 2359300
  21.1 5.4 %copy-start.3 = (f32[1,128,16]{1,2,0:T(8,128)S(1)}, f32[1,128,16]{1,2,0:T(8,128)}, u32[]{:S(2)}) copy-start(f32[1,128,16]{1,2,0:T(8,128)} %param.10) | copy-start | bytes 24580
  21.1 5.4 %copy-start.5 = (s32[1,128,2]{1,2,0:T(2,128)S(1)}, s32[1,128,2]{1,2,0:T(2,128)}, u32[]{:S(2)}) copy-start(s32[1,128,2]{1,2,0:T(2,128)} %param.9) | copy-start | bytes 3076
  40.5 49.7 %copy-start.2 = (bf16[16,3072]{1,0:T(8,128)(2,1)S(1)}, bf16[16,3072]{1,0:T(8,128)(2,1)}, u32[]{:S(2)}) copy-start(bf16[16,3072]{1,0:T(8,128)(2,1)} %refs_2_.1) | copy-start | bytes 294916
  40.5 49.7 %all-to-all-start.2 = ((bf16[16,80,768]{2,1,0:T(8,128)(2,1)}), bf16[16,80,768]{2,1,0:T(8,128)(2,1)S(1)}, u32[]{:S(2)}, u32[]{:S(2)}) async-start(bf16[16,80,768]{2,1,0:T(8,128)(2,1)} %shard_map.78), calls=%async_computation.2 | async-start | bytes 3932160 | tf_op jit(solution)/shard_map/all_to_all | solution.py:176
  45.5 4.7 %collective-permute-start = (f32[1,1,3072]{2,1,0:T(1,128)S(1)}, f32[1,1,3072]{2,1,0:T(1,128)S(1)}, u32[]{:S(2)}, u32[]{:S(2)}) collective-permute-start(f32[1,1,3072]{2,1,0:T(1,128)S(1)} %param.1), channel_id=1, source_target_pairs={{0,16},{16,0},{32,48},{48,32},{64,80},{80,64},{96,112},{112,96},{1... | collective-permute-start | bytes 36872 | tf_op jit(solution)/shard_map/cond/branch_1_fun/ppermute | solution.py:182
  50.2 5.6 %collective-permute-start.1 = (f32[1,1,3072]{2,1,0:T(1,128)S(1)}, f32[1,1,3072]{2,1,0:T(1,128)S(1)}, u32[]{:S(2)}, u32[]{:S(2)}) collective-permute-start(f32[1,1,3072]{2,1,0:T(1,128)S(1)} %add.12), channel_id=1, source_target_pairs={{0,32},{16,48},{32,0},{48,16},{64,96},{80,112},{96,64},{112,80},{1... | collective-permute-start | bytes 36872 | tf_op jit(solution)/shard_map/cond/branch_1_fun/ppermute | solution.py:182
  55.9 9.6 %collective-permute-start.2 = (f32[1,1,3072]{2,1,0:T(1,128)S(1)}, f32[1,1,3072]{2,1,0:T(1,128)S(1)}, u32[]{:S(2)}, u32[]{:S(2)}) collective-permute-start(f32[1,1,3072]{2,1,0:T(1,128)S(1)} %add.13), channel_id=1, source_target_pairs={{0,64},{16,80},{32,96},{48,112},{64,0},{80,16},{96,32},{112,48},{1... | collective-permute-start | bytes 36872 | tf_op jit(solution)/shard_map/cond/branch_1_fun/ppermute | solution.py:182
  65.5 4.7 %collective-permute-start.3 = (f32[1,1,3072]{2,1,0:T(1,128)S(1)}, f32[1,1,3072]{2,1,0:T(1,128)S(1)}, u32[]{:S(2)}, u32[]{:S(2)}) collective-permute-start(f32[1,1,3072]{2,1,0:T(1,128)S(1)} %add.14), channel_id=1, source_target_pairs={{0,128},{16,144},{32,160},{48,176},{64,192},{80,208},{96,224},{112... | collective-permute-start | bytes 36872 | tf_op jit(solution)/shard_map/cond/branch_1_fun/ppermute | solution.py:182
  70.3 5.6 %collective-permute-start.4 = (f32[1,1,3072]{2,1,0:T(1,128)S(1)}, f32[1,1,3072]{2,1,0:T(1,128)S(1)}, u32[]{:S(2)}, u32[]{:S(2)}) collective-permute-start(f32[1,1,3072]{2,1,0:T(1,128)S(1)} %add.15), channel_id=1, source_target_pairs={{0,256},{16,272},{32,288},{48,304},{64,320},{80,336},{96,352},{112... | collective-permute-start | bytes 36872 | tf_op jit(solution)/shard_map/cond/branch_1_fun/ppermute | solution.py:182
  75.9 8.6 %collective-permute-start.5 = (f32[1,1,3072]{2,1,0:T(1,128)S(1)}, f32[1,1,3072]{2,1,0:T(1,128)S(1)}, u32[]{:S(2)}, u32[]{:S(2)}) collective-permute-start(f32[1,1,3072]{2,1,0:T(1,128)S(1)} %add.16), channel_id=1, source_target_pairs={{0,512},{16,528},{32,544},{48,560},{64,576},{80,592},{96,608},{112... | collective-permute-start | bytes 36872 | tf_op jit(solution)/shard_map/cond/branch_1_fun/ppermute | solution.py:182
  84.6 7.8 %copy-start.6 = (f32[1,1,3072]{2,1,0:T(1,128)}, f32[1,1,3072]{2,1,0:T(1,128)S(1)}, u32[]{:S(2)}) copy-start(f32[1,1,3072]{2,1,0:T(1,128)S(1)} %get-tuple-element.24) | copy-start | bytes 36868

commit v9 on v8

--- a/solution.py
+++ b/solution.py
@@ -8,6 +8,7 @@
 QUARTERS = 4
 LANES = 128
 SUBLANES = 8
+TILE = 16
 VMEM = 24 * 1024 * 1024
 
 
@@ -98,27 +99,44 @@
     term_ref[...] = term[:, None, :]
 
 
-def combine_kernel(cap, depth, place_ref, logit_ref, weight_ref, copies_ref, out_ref):
-    tokens, width = out_ref.shape
-    filler = jnp.zeros((depth - cap, width), jnp.float32)
-    table = []
-    for expert in range(copies_ref.shape[0]):
-        stacked = copies_ref[expert].astype(jnp.float32)
-        rows = [stacked[q * cap : (q + 1) * cap] for q in range(QUARTERS)]
-        table += [jnp.concatenate(rows, axis=1), filler]
-    copies = jnp.concatenate(table, axis=0).astype(jnp.bfloat16)
-    column = lax.broadcasted_iota(jnp.int32, (tokens, copies.shape[0]), 1)
+def spread_kernel(slots, place_ref, logit_ref, out_ref):
+    tokens = place_ref.shape[0]
+    column = lax.broadcasted_iota(jnp.int32, (tokens, slots), 1)
     spread = jnp.zeros(column.shape, jnp.float32)
     for k in range(2):
         base = place_ref[:, 2 + k : 3 + k].astype(jnp.int32)
         spread = jnp.where(column == base, place_ref[:, k : k + 1], spread)
     high = spread.astype(jnp.bfloat16)
     low = (spread - high.astype(jnp.float32)).astype(jnp.bfloat16)
-    both = jnp.dot(
-        jnp.concatenate([high, low], axis=0), copies, preferred_element_type=jnp.float32
-    )
-    total = both[:tokens] + both[tokens:] + dot_rows(logit_ref[...], weight_ref[...])
-    out_ref[...] = total.astype(jnp.bfloat16)
+    out_ref[:tokens, :slots] = high
+    out_ref[tokens:, :slots] = low
+    logit = logit_ref[...].astype(jnp.float32).T.astype(jnp.bfloat16)
+    out_ref[:tokens, slots:] = logit
+    out_ref[tokens:, slots:] = jnp.zeros_like(logit)
+
+
+def combine_kernel(cap, depth, spread_ref, weight_ref, copies_ref, out_ref, held, sems):
+    tokens = out_ref.shape[0]
+    part = copies_ref.shape[2]
+    filler = jnp.zeros((depth - cap, part), jnp.float32)
+    writes = []
+    for q in range(QUARTERS):
+        table = []
+        start = q * cap // TILE * TILE
+        stop = -(-(q + 1) * cap // TILE) * TILE
+        for expert in range(copies_ref.shape[0]):
+            rows = copies_ref[expert, start:stop, :].astype(jnp.float32)
+            table += [rows[q * cap - start : (q + 1) * cap - start], filler]
+        columns = slice(q * part, (q + 1) * part)
+        copies = jnp.concatenate(table, axis=0).astype(jnp.bfloat16)
+        right = jnp.concatenate([copies, weight_ref[:, columns]], axis=0)
+        both = jnp.dot(spread_ref[...], right, preferred_element_type=jnp.float32)
+        held[q] = (both[:tokens] + both[tokens:]).astype(jnp.bfloat16)
+        write = pltpu.make_async_copy(held.at[q], out_ref.at[:, columns], sems.at[q])
+        write.start()
+        writes.append(write)
+    for write in writes:
+        write.wait()
 
 
 def shards(side, layer_input, expert_ids, router_probs, router_weight, expert_grads, gate_dots):
@@ -175,21 +193,31 @@
     packed, own = lax.optimization_barrier((packed, own))
     copies = lax.all_to_all(packed, "exp", 0, 0, tiled=True)
 
-    def over_ctx(own):
+    def over_ctx(operand):
+        own, place, logit = operand
+        spread = pl.pallas_call(
+            lambda *refs: spread_kernel(experts * depth, *refs),
+            out_shape=jax.ShapeDtypeStruct((2 * tokens, experts * (depth + 1)), jnp.bfloat16),
+            compiler_params=params,
+        )(place, logit)
         bit = 1
         while bit < side * side:
             moves = [(i, i ^ bit) for i in range(side * side)]
             own = own + lax.ppermute(own, "ctx", moves)
             bit *= 2
-        return own
-
-    own = unit(over_ctx, own)
-    place, own = lax.optimization_barrier((place, own))
+        return own, spread
+
+    own, spread = unit(over_ctx, (own, place, logit))
     combined = pl.pallas_call(
         lambda *refs: combine_kernel(cap, depth, *refs),
         out_shape=jax.ShapeDtypeStruct((tokens, width), jnp.bfloat16),
-        compiler_params=params,
-    )(place, logit, router_weight, copies)
+        out_specs=pl.BlockSpec(memory_space=pl.ANY),
+        scratch_shapes=[
+            pltpu.VMEM((QUARTERS, tokens, part), jnp.bfloat16),
+            pltpu.SemaphoreType.DMA((QUARTERS,)),
+        ],
+        compiler_params=params,
+    )(spread, router_weight, copies)
     return combined[None], own[0]
 
 

time: 92.9 us -> 92.4 us (level)
  no operation moved by 1% of the time
where the time goes in v9:
time: 92.4 us; the launch traced here: 91.9 us
  starting transfers between devices  46.8 us (51%)
  waiting for transfers between devices  22.6 us (24%)
  blocking collectives  13.5 us (15%)
  Pallas kernels  4.72 us (5%)
  local copies, waits for them, and re-layouts  2.75 us (3%)
  between operations  1.35 us (1%)
    ppermute x6, starting transfers between devices, over_ctx(): own = own + lax.ppermute(own, 'ctx', moves)  25.6 us
    all_to_all x1, starting transfers between devices, shards(): dots = lax.all_to_all(laid, 'exp', 0, 0, tiled=True)  17.4 us
    all_to_all x1, blocking collectives, shards(): own = add(lax.all_to_all(term, 'exp', 0, 0, tiled=True), 1)  13.5 us
    ppermute x6, waiting for transfers between devices, over_ctx(): own = own + lax.ppermute(own, 'ctx', moves)  13.1 us
    all_to_all x1, waiting for transfers between devices, shards(): copies = lax.all_to_all(packed, 'exp', 0, 0, tiled=True)  5.62 us
    all_to_all x1, waiting for transfers between devices, shards(): dots = lax.all_to_all(laid, 'exp', 0, 0, tiled=True)  3.87 us
    all_to_all x1, starting transfers between devices, shards(): copies = lax.all_to_all(packed, 'exp', 0, 0, tiled=True)  3.76 us
    unnamed x14, local copies, waits for them, and re-layouts  2.24 us
  transfers between devices with their start and end apart: 8, of which 8 were waited for; matrix products, arithmetic and copies ran while one was open for 1% of the time, Pallas kernels for 2%

profile of v9, /device:TPU:1, one launch (start us, length us, event | category | flops | bytes accessed | tf_op | source)
XLA Modules:
  0.0 91.9 jit_solution(18306858032062968639)
XLA Ops:
  0.6 0.7 copy-done.4
  1.3 0.8 shard_map.77
  2.1 17.4 %all-to-all-start = ((f32[16,1,128]{2,1,0:T(1,128)}), f32[16,1,128]{2,1,0:T(1,128)S(1)}, u32[]{:S(2)}, u32[]{:S(2)}) async-start(f32[16,1,128]{2,1,0:T(1,128)} %shard_map.77), calls=%async_computation | async-start | bytes 16384 | tf_op jit(solution)/shard_map/all_to_all | solution.py:164
  19.5 1.5 %copy-done = bf16[1,1,320,3072]{3,2,1,0:T(8,128)(2,1)S(1)} copy-done((bf16[1,1,320,3072]{3,2,1,0:T(8,128)(2,1)S(1)}, bf16[1,1,320,3072]{3,2,1,0:T(8,128)(2,1)}, u32[]{:S(2)}) %copy-start) | copy-done | bytes 1966104
  21.1 1.6 %shard_map.78 = bf16[16,80,768]{2,1,0:T(8,128)(2,1)} custom-call(bf16[320,3072]{1,0:T(8,128)(2,1)S(1)} %bitcast.13), custom_call_target="tpu_custom_call" | custom-call | tf_op jit(solution)/shard_map/pallas_call | solution.py:166
  22.6 3.9 %all-to-all-done.refs_2_ = f32[16,1,128]{2,1,0:T(1,128)S(1)} async-done(((f32[16,1,128]{2,1,0:T(1,128)}), f32[16,1,128]{2,1,0:T(1,128)S(1)}, u32[]{:S(2)}, u32[]{:S(2)}) %all-to-all-start) | async-done | bytes 8224 | tf_op jit(solution)/shard_map/all_to_all | solution.py:164
  27.0 13.5 %all_to_all.15.parts_ref = f32[16,1,3072]{2,1,0:T(1,128)S(1)} all-to-all(f32[16,1,3072]{2,1,0:T(1,128)S(1)} %get-tuple-element.25), channel_id=1, replica_groups=mesh['ctx'=64,'exp'=16] {'exp'}, dimensions={0} | all-to-all | bytes 393216 | tf_op jit(solution)/shard_map/all_to_all | solution.py:191
  40.5 3.8 %all-to-all-start.2 = ((bf16[16,80,768]{2,1,0:T(8,128)(2,1)}), bf16[16,80,768]{2,1,0:T(8,128)(2,1)S(1)}, u32[]{:S(2)}, u32[]{:S(2)}) async-start(bf16[16,80,768]{2,1,0:T(8,128)(2,1)} %shard_map.78), calls=%async_computation.2 | async-start | bytes 3932160 | tf_op jit(solution)/shard_map/all_to_all | solution.py:194
  44.3 0.5 slice.3
  45.5 39.1 %conditional.1 = (bf16[256,400]{1,0:T(8,128)(2,1)S(1)}, f32[1,3072]{1,0:T(1,128)S(1)}) conditional(s32[]{:T(128)} %bitcast.1, () %tuple.20, (f32[128,8]{1,0:T(8,128)S(1)}, bf16[16,128]{1,0:T(8,128)(2,1)S(1)}, f32[1,1,3072]{2,1,0:T(1,128)S(1)}) %tuple.23), branch_computations={%region_0.0_spmd, %region_1.0_spmd} | conditional | flops 18432 | bytes 516352 | solution.py:157
  45.5 1.9 %collective-permute-start = (f32[1,1,3072]{2,1,0:T(1,128)S(1)}, f32[1,1,3072]{2,1,0:T(1,128)S(1)}, u32[]{:S(2)}, u32[]{:S(2)}) collective-permute-start(f32[1,1,3072]{2,1,0:T(1,128)S(1)} %get-tuple-element.9), channel_id=1, source_target_pairs={{0,16},{16,0},{32,48},{48,32},{64,80},{80,64},{96,112},{112,96},{1... | collective-permute-start | bytes 36872 | tf_op jit(solution)/shard_map/cond/branch_1_fun/ppermute | solution.py:206
  47.4 2.8 %collective-permute-done = f32[1,1,3072]{2,1,0:T(1,128)S(1)} collective-permute-done((f32[1,1,3072]{2,1,0:T(1,128)S(1)}, f32[1,1,3072]{2,1,0:T(1,128)S(1)}, u32[]{:S(2)}, u32[]{:S(2)}) %collective-permute-start) | collective-permute-done | bytes 12320 | tf_op jit(solution)/shard_map/cond/branch_1_fun/ppermute | solution.py:206
  50.2 1.9 %collective-permute-start.1 = (f32[1,1,3072]{2,1,0:T(1,128)S(1)}, f32[1,1,3072]{2,1,0:T(1,128)S(1)}, u32[]{:S(2)}, u32[]{:S(2)}) collective-permute-start(f32[1,1,3072]{2,1,0:T(1,128)S(1)} %add.12), channel_id=1, source_target_pairs={{0,32},{16,48},{32,0},{48,16},{64,96},{80,112},{96,64},{112,80},{1... | collective-permute-start | bytes 36872 | tf_op jit(solution)/shard_map/cond/branch_1_fun/ppermute | solution.py:206
  52.2 3.7 %collective-permute-done.1 = f32[1,1,3072]{2,1,0:T(1,128)S(1)} collective-permute-done((f32[1,1,3072]{2,1,0:T(1,128)S(1)}, f32[1,1,3072]{2,1,0:T(1,128)S(1)}, u32[]{:S(2)}, u32[]{:S(2)}) %collective-permute-start.1) | collective-permute-done | bytes 12320 | tf_op jit(solution)/shard_map/cond/branch_1_fun/ppermute | solution.py:206
  55.9 8.2 %collective-permute-start.2 = (f32[1,1,3072]{2,1,0:T(1,128)S(1)}, f32[1,1,3072]{2,1,0:T(1,128)S(1)}, u32[]{:S(2)}, u32[]{:S(2)}) collective-permute-start(f32[1,1,3072]{2,1,0:T(1,128)S(1)} %add.13), channel_id=1, source_target_pairs={{0,64},{16,80},{32,96},{48,112},{64,0},{80,16},{96,32},{112,48},{1... | collective-permute-start | bytes 36872 | tf_op jit(solution)/shard_map/cond/branch_1_fun/ppermute | solution.py:206
  64.1 1.4 %collective-permute-done.2 = f32[1,1,3072]{2,1,0:T(1,128)S(1)} collective-permute-done((f32[1,1,3072]{2,1,0:T(1,128)S(1)}, f32[1,1,3072]{2,1,0:T(1,128)S(1)}, u32[]{:S(2)}, u32[]{:S(2)}) %collective-permute-start.2) | collective-permute-done | bytes 12320 | tf_op jit(solution)/shard_map/cond/branch_1_fun/ppermute | solution.py:206
  65.5 2.8 %collective-permute-start.3 = (f32[1,1,3072]{2,1,0:T(1,128)S(1)}, f32[1,1,3072]{2,1,0:T(1,128)S(1)}, u32[]{:S(2)}, u32[]{:S(2)}) collective-permute-start(f32[1,1,3072]{2,1,0:T(1,128)S(1)} %add.14), channel_id=1, source_target_pairs={{0,128},{16,144},{32,160},{48,176},{64,192},{80,208},{96,224},{112... | collective-permute-start | bytes 36872 | tf_op jit(solution)/shard_map/cond/branch_1_fun/ppermute | solution.py:206
  68.3 1.9 %collective-permute-done.3 = f32[1,1,3072]{2,1,0:T(1,128)S(1)} collective-permute-done((f32[1,1,3072]{2,1,0:T(1,128)S(1)}, f32[1,1,3072]{2,1,0:T(1,128)S(1)}, u32[]{:S(2)}, u32[]{:S(2)}) %collective-permute-start.3) | collective-permute-done | bytes 12320 | tf_op jit(solution)/shard_map/cond/branch_1_fun/ppermute | solution.py:206
  70.2 3.8 %collective-permute-start.4 = (f32[1,1,3072]{2,1,0:T(1,128)S(1)}, f32[1,1,3072]{2,1,0:T(1,128)S(1)}, u32[]{:S(2)}, u32[]{:S(2)}) collective-permute-start(f32[1,1,3072]{2,1,0:T(1,128)S(1)} %add.15), channel_id=1, source_target_pairs={{0,256},{16,272},{32,288},{48,304},{64,320},{80,336},{96,352},{112... | collective-permute-start | bytes 36872 | tf_op jit(solution)/shard_map/cond/branch_1_fun/ppermute | solution.py:206
  74.0 1.9 %collective-permute-done.4 = f32[1,1,3072]{2,1,0:T(1,128)S(1)} collective-permute-done((f32[1,1,3072]{2,1,0:T(1,128)S(1)}, f32[1,1,3072]{2,1,0:T(1,128)S(1)}, u32[]{:S(2)}, u32[]{:S(2)}) %collective-permute-start.4) | collective-permute-done | bytes 12320 | tf_op jit(solution)/shard_map/cond/branch_1_fun/ppermute | solution.py:206
  75.9 7.0 %collective-permute-start.5 = (f32[1,1,3072]{2,1,0:T(1,128)S(1)}, f32[1,1,3072]{2,1,0:T(1,128)S(1)}, u32[]{:S(2)}, u32[]{:S(2)}) collective-permute-start(f32[1,1,3072]{2,1,0:T(1,128)S(1)} %add.16), channel_id=1, source_target_pairs={{0,512},{16,528},{32,544},{48,560},{64,576},{80,592},{96,608},{112... | collective-permute-start | bytes 36872 | tf_op jit(solution)/shard_map/cond/branch_1_fun/ppermute | solution.py:206
  83.1 1.5 %collective-permute-done.5 = f32[1,1,3072]{2,1,0:T(1,128)S(1)} collective-permute-done((f32[1,1,3072]{2,1,0:T(1,128)S(1)}, f32[1,1,3072]{2,1,0:T(1,128)S(1)}, u32[]{:S(2)}, u32[]{:S(2)}) %collective-permute-start.5) | collective-permute-done | bytes 12320 | tf_op jit(solution)/shard_map/cond/branch_1_fun/ppermute | solution.py:206
  84.6 5.6 %all-to-all-done.2.refs_2_ = bf16[16,80,768]{2,1,0:T(8,128)(2,1)S(1)} async-done(((bf16[16,80,768]{2,1,0:T(8,128)(2,1)}), bf16[16,80,768]{2,1,0:T(8,128)(2,1)S(1)}, u32[]{:S(2)}, u32[]{:S(2)}) %all-to-all-start.2) | async-done | bytes 1966112 | tf_op jit(solution)/shard_map/all_to_all | solution.py:194
  90.2 1.7 %shard_map.81 = bf16[128,3072]{1,0:T(8,128)(2,1)} custom-call(bf16[256,400]{1,0:T(8,128)(2,1)S(1)} %get-tuple-element.27.refs_0_, bf16[16,3072]{1,0:T(8,128)(2,1)S(1)} %copy-done.2, bf16[16,80,768]{2,1,0:T(8,128)(2,1)S(1)} %all-to-all-done.2.refs_2_), custom_call_target="tpu_custom_call" | custom-call | tf_op jit(solution)/shard_map/pallas_call | solution.py:211
  (21 shorter events, 0.8 us)
Async XLA Ops:
  0.6 0.7 copy-start.4
  2.1 24.4 %all-to-all-start = ((f32[16,1,128]{2,1,0:T(1,128)}), f32[16,1,128]{2,1,0:T(1,128)S(1)}, u32[]{:S(2)}, u32[]{:S(2)}) async-start(f32[16,1,128]{2,1,0:T(1,128)} %shard_map.77), calls=%async_computation | async-start | bytes 16384 | tf_op jit(solution)/shard_map/all_to_all | solution.py:164
  19.5 1.5 %copy-start = (bf16[1,1,320,3072]{3,2,1,0:T(8,128)(2,1)S(1)}, bf16[1,1,320,3072]{3,2,1,0:T(8,128)(2,1)}, u32[]{:S(2)}) copy-start(bf16[1,1,320,3072]{3,2,1,0:T(8,128)(2,1)} %param.12) | copy-start | bytes 5898244
  21.1 5.4 %copy-start.1 = (bf16[1,128,3072]{2,1,0:T(8,128)(2,1)S(1)}, bf16[1,128,3072]{2,1,0:T(8,128)(2,1)}, u32[]{:S(2)}) copy-start(bf16[1,128,3072]{2,1,0:T(8,128)(2,1)} %param.8) | copy-start | bytes 2359300
  21.1 5.4 %copy-start.3 = (f32[1,128,16]{1,2,0:T(8,128)S(1)}, f32[1,128,16]{1,2,0:T(8,128)}, u32[]{:S(2)}) copy-start(f32[1,128,16]{1,2,0:T(8,128)} %param.10) | copy-start | bytes 24580
  21.1 5.4 %copy-start.5 = (s32[1,128,2]{1,2,0:T(2,128)S(1)}, s32[1,128,2]{1,2,0:T(2,128)}, u32[]{:S(2)}) copy-start(s32[1,128,2]{1,2,0:T(2,128)} %param.9) | copy-start | bytes 3076
  40.5 49.7 %copy-start.2 = (bf16[16,3072]{1,0:T(8,128)(2,1)S(1)}, bf16[16,3072]{1,0:T(8,128)(2,1)}, u32[]{:S(2)}) copy-start(bf16[16,3072]{1,0:T(8,128)(2,1)} %refs_1_.1) | copy-start | bytes 294916
  40.5 49.7 %all-to-all-start.2 = ((bf16[16,80,768]{2,1,0:T(8,128)(2,1)}), bf16[16,80,768]{2,1,0:T(8,128)(2,1)S(1)}, u32[]{:S(2)}, u32[]{:S(2)}) async-start(bf16[16,80,768]{2,1,0:T(8,128)(2,1)} %shard_map.78), calls=%async_computation.2 | async-start | bytes 3932160 | tf_op jit(solution)/shard_map/all_to_all | solution.py:194
  45.5 4.7 %collective-permute-start = (f32[1,1,3072]{2,1,0:T(1,128)S(1)}, f32[1,1,3072]{2,1,0:T(1,128)S(1)}, u32[]{:S(2)}, u32[]{:S(2)}) collective-permute-start(f32[1,1,3072]{2,1,0:T(1,128)S(1)} %get-tuple-element.9), channel_id=1, source_target_pairs={{0,16},{16,0},{32,48},{48,32},{64,80},{80,64},{96,112},{112,96},{1... | collective-permute-start | bytes 36872 | tf_op jit(solution)/shard_map/cond/branch_1_fun/ppermute | solution.py:206
  50.2 5.6 %collective-permute-start.1 = (f32[1,1,3072]{2,1,0:T(1,128)S(1)}, f32[1,1,3072]{2,1,0:T(1,128)S(1)}, u32[]{:S(2)}, u32[]{:S(2)}) collective-permute-start(f32[1,1,3072]{2,1,0:T(1,128)S(1)} %add.12), channel_id=1, source_target_pairs={{0,32},{16,48},{32,0},{48,16},{64,96},{80,112},{96,64},{112,80},{1... | collective-permute-start | bytes 36872 | tf_op jit(solution)/shard_map/cond/branch_1_fun/ppermute | solution.py:206
  55.9 9.6 %collective-permute-start.2 = (f32[1,1,3072]{2,1,0:T(1,128)S(1)}, f32[1,1,3072]{2,1,0:T(1,128)S(1)}, u32[]{:S(2)}, u32[]{:S(2)}) collective-permute-start(f32[1,1,3072]{2,1,0:T(1,128)S(1)} %add.13), channel_id=1, source_target_pairs={{0,64},{16,80},{32,96},{48,112},{64,0},{80,16},{96,32},{112,48},{1... | collective-permute-start | bytes 36872 | tf_op jit(solution)/shard_map/cond/branch_1_fun/ppermute | solution.py:206
  65.5 4.7 %collective-permute-start.3 = (f32[1,1,3072]{2,1,0:T(1,128)S(1)}, f32[1,1,3072]{2,1,0:T(1,128)S(1)}, u32[]{:S(2)}, u32[]{:S(2)}) collective-permute-start(f32[1,1,3072]{2,1,0:T(1,128)S(1)} %add.14), channel_id=1, source_target_pairs={{0,128},{16,144},{32,160},{48,176},{64,192},{80,208},{96,224},{112... | collective-permute-start | bytes 36872 | tf_op jit(solution)/shard_map/cond/branch_1_fun/ppermute | solution.py:206
  70.2 5.6 %collective-permute-start.4 = (f32[1,1,3072]{2,1,0:T(1,128)S(1)}, f32[1,1,3072]{2,1,0:T(1,128)S(1)}, u32[]{:S(2)}, u32[]{:S(2)}) collective-permute-start(f32[1,1,3072]{2,1,0:T(1,128)S(1)} %add.15), channel_id=1, source_target_pairs={{0,256},{16,272},{32,288},{48,304},{64,320},{80,336},{96,352},{112... | collective-permute-start | bytes 36872 | tf_op jit(solution)/shard_map/cond/branch_1_fun/ppermute | solution.py:206
  75.9 8.6 %collective-permute-start.5 = (f32[1,1,3072]{2,1,0:T(1,128)S(1)}, f32[1,1,3072]{2,1,0:T(1,128)S(1)}, u32[]{:S(2)}, u32[]{:S(2)}) collective-permute-start(f32[1,1,3072]{2,1,0:T(1,128)S(1)} %add.16), channel_id=1, source_target_pairs={{0,512},{16,528},{32,544},{48,560},{64,576},{80,592},{96,608},{112... | collective-permute-start | bytes 36872 | tf_op jit(solution)/shard_map/cond/branch_1_fun/ppermute | solution.py:206
  84.6 7.3 %copy-start.6 = (f32[1,3072]{1,0:T(1,128)}, f32[1,3072]{1,0:T(1,128)S(1)}, u32[]{:S(2)}) copy-start(f32[1,3072]{1,0:T(1,128)S(1)} %get-tuple-element.20) | copy-start | bytes 36868

commit v10 on v9

--- a/solution.py
+++ b/solution.py
@@ -34,15 +34,26 @@
     out_ref[...] = laid[:, None, :]
 
 
-def pack_kernel(cap, rows_ref, out_ref):
-    part = out_ref.shape[2]
+def pack_kernel(cap, rows_ref, kept_ref, given_ref):
+    part = kept_ref.shape[2]
+    core = lax.axis_index("exp") % 2
     rows = rows_ref[...].astype(jnp.float32)
-    for w in range(out_ref.shape[0]):
-        window = rows[w * cap : (w + 1) * cap]
-        stacked = jnp.concatenate(
-            [window[:, q * part : (q + 1) * part] for q in range(QUARTERS)], axis=0
-        )
-        out_ref[w] = stacked.astype(jnp.bfloat16)
+    for pair in range(kept_ref.shape[0]):
+        stacks = []
+        for w in (2 * pair, 2 * pair + 1):
+            window = rows[w * cap : (w + 1) * cap]
+            stacked = jnp.concatenate(
+                [window[:, q * part : (q + 1) * part] for q in range(QUARTERS)], axis=0
+            )
+            stacks.append(stacked)
+        kept_ref[pair] = jnp.where(core == 0, stacks[0], stacks[1]).astype(jnp.bfloat16)
+        given_ref[pair] = jnp.where(core == 0, stacks[1], stacks[0]).astype(jnp.bfloat16)
+
+
+def deal_kernel(kept_ref, got_ref, out_ref):
+    for chip in range(kept_ref.shape[0]):
+        out_ref[2 * chip] = kept_ref[chip]
+        out_ref[2 * chip + 1] = got_ref[chip]
 
 
 def sum_kernel(parts_ref, out_ref):
@@ -86,9 +97,11 @@
     logit = probs * (router_grad - jnp.sum(probs * router_grad, axis=0, keepdims=True))
     logit = logit.astype(jnp.bfloat16)
     logit_ref[...] = logit
+    core = lax.axis_index("exp") % 2
     rows = []
     for k in range(2):
-        block = ids_ref[k : k + 1, :]
+        ids = ids_ref[k : k + 1, :]
+        block = ids // 2 * 2 + (ids % 2 + core) % 2
         rows.append((block * depth + slots[k]).astype(jnp.float32))
     place = jnp.concatenate(
         [picked[0] / total, picked[1] / total] + rows + [jnp.zeros((4, tokens), jnp.float32)],
@@ -163,13 +176,18 @@
     )(gate_dots[0])
     dots = lax.all_to_all(laid, "exp", 0, 0, tiled=True)
 
-    packed = pl.pallas_call(
-        lambda *refs: pack_kernel(cap, *refs),
-        out_shape=jax.ShapeDtypeStruct((windows, stack, part), jnp.bfloat16),
-        compiler_params=params,
-    )(expert_grads[0, 0])
-
-    dots, packed = lax.optimization_barrier((dots, packed))
+    half = jax.ShapeDtypeStruct((windows // 2, stack, part), jnp.bfloat16)
+
+    def share(rows):
+        kept, given = pl.pallas_call(
+            lambda *refs: pack_kernel(cap, *refs),
+            out_shape=(half, half),
+            compiler_params=params,
+        )(rows)
+        return kept, lax.ppermute(given, "exp", [(i, i ^ 1) for i in range(windows)])
+
+    kept, got = unit(share, expert_grads[0, 0])
+    dots, got = lax.optimization_barrier((dots, got))
     ids = jnp.swapaxes(expert_ids, 1, 2)[0]
     probs = jnp.swapaxes(router_probs, 1, 2)[0]
     logit, place, term = pl.pallas_call(
@@ -190,8 +208,14 @@
 
     own = add(lax.all_to_all(term, "exp", 0, 0, tiled=True), 1)
 
-    packed, own = lax.optimization_barrier((packed, own))
-    copies = lax.all_to_all(packed, "exp", 0, 0, tiled=True)
+    dealt = pl.pallas_call(
+        deal_kernel,
+        out_shape=jax.ShapeDtypeStruct((windows, stack, part), jnp.bfloat16),
+        compiler_params=params,
+    )(kept, got)
+    dealt, own = lax.optimization_barrier((dealt, own))
+    cores = [[i for i in range(windows) if i % 2 == core] for core in range(2)]
+    copies = lax.all_to_all(dealt, "exp", 0, 0, axis_index_groups=cores, tiled=True)
 
     def over_ctx(operand):
         own, place, logit = operand

time: 92.4 us -> 102 us (1.10)
  blocking collectives: 13.5 us -> 0 us
  waiting for transfers between devices: 22.6 us -> 32.7 us
  starting transfers between devices: 46.8 us -> 56.6 us
  Pallas kernels: 4.72 us -> 8.61 us
    all_to_all x1 -> x0, blocking collectives: 13.5 us -> none  [shards(): own = add(lax.all_to_all(term, 'exp', 0, 0, tiled=True), 1)]
    all_to_all x1 -> x2, waiting for transfers between devices: 5.62 us -> 17.9 us  [the longest x1 10.2 us: shards(): lax.all_to_all(dealt, 'exp', 0, 0, axis_index_groups=cores, tiled=True)]
    all_to_all x1 -> x2, starting transfers between devices: 3.76 us -> 11 us  [the longest x1 7.27 us: shards(): own = add(lax.all_to_all(term, 'exp', 0, 0, tiled=True), 1)]
    all_to_all x1, waiting for transfers between devices: 3.87 us -> 0.01 us  [shards(): dots = lax.all_to_all(laid, 'exp', 0, 0, tiled=True)]
    pallas_call x1 -> x2, Pallas kernels: 1.56 us -> 4.77 us  [the longest x1 2.62 us: shards(): pl.pallas_call(deal_kernel, out_shape=jax.ShapeDtypeStruct((windows, stac...]
    ppermute x0 -> x1, waiting for transfers between devices: none -> 2.45 us  [share(): lax.ppermute(given, 'exp', [(i, i ^ 1) for i in range(windows)])]
    ppermute x0 -> x1, starting transfers between devices: none -> 2.13 us  [share(): lax.ppermute(given, 'exp', [(i, i ^ 1) for i in range(windows)])]
    unnamed x14 -> x12, local copies, waits for them, and re-layouts: 2.24 us -> 0.71 us
  transfers between devices with their start and end apart: 8 -> 10, of which waited for: 8 -> 9; matrix products, arithmetic and copies ran while one was open for 1% -> 1% of each run, Pallas kernels for 2% -> 5%
where the time goes in v10:
time: 102 us; the launch traced here: 101 us
  starting transfers between devices  56.6 us (55%)
  waiting for transfers between devices  32.7 us (32%)
  Pallas kernels  8.61 us (8%)
  local copies, waits for them, and re-layouts  1.89 us (2%)
  between operations  1.37 us (1%)
    ppermute x6, starting transfers between devices, over_ctx(): own = own + lax.ppermute(own, 'ctx', moves)  26 us
    all_to_all x1, starting transfers between devices, shards(): dots = lax.all_to_all(laid, 'exp', 0, 0, tiled=True)  17.4 us
    ppermute x6, waiting for transfers between devices, over_ctx(): own = own + lax.ppermute(own, 'ctx', moves)  12.4 us
    all_to_all x1, waiting for transfers between devices, shards(): lax.all_to_all(dealt, 'exp', 0, 0, axis_index_groups=cores, tiled=True)  10.2 us
    all_to_all x1, waiting for transfers between devices, shards(): own = add(lax.all_to_all(term, 'exp', 0, 0, tiled=True), 1)  7.71 us
    all_to_all x1, starting transfers between devices, shards(): own = add(lax.all_to_all(term, 'exp', 0, 0, tiled=True), 1)  7.27 us
    all_to_all x1, starting transfers between devices, shards(): lax.all_to_all(dealt, 'exp', 0, 0, axis_index_groups=cores, tiled=True)  3.74 us
    pallas_call x1, Pallas kernels, shards(): pl.pallas_call(deal_kernel, out_shape=jax.ShapeDtypeStruct((windows, stac...  2.62 us
  transfers between devices with their start and end apart: 10, of which 9 were waited for; matrix products, arithmetic and copies ran while one was open for 1% of the time, Pallas kernels for 5%

profile of v10, /device:TPU:1, one launch (start us, length us, event | category | flops | bytes accessed | tf_op | source)
XLA Modules:
  0.0 101.3 jit_solution(16965874516381101615)
XLA Ops:
  2.1 17.4 %all-to-all-start = ((f32[16,1,128]{2,1,0:T(1,128)}), f32[16,1,128]{2,1,0:T(1,128)S(1)}, u32[]{:S(2)}, u32[]{:S(2)}) async-start(f32[16,1,128]{2,1,0:T(1,128)} %shard_map.79), calls=%async_computation | async-start | bytes 16384 | tf_op jit(solution)/shard_map/all_to_all | solution.py:177
  19.5 1.2 %slice.3 = s32[1,1,1]{1,2,0:T(1,128)} slice(s32[1,128,2]{1,2,0:T(2,128)} %param.11), slice={[0:1], [0:1], [0:1]} | slice | bytes 8 | tf_op jit(solution)/shard_map/slice | solution.py:165
  21.4 6.8 %conditional.2 = (bf16[8,80,768]{2,1,0:T(8,128)(2,1)S(1)}, bf16[8,80,768]{2,1,0:T(8,128)(2,1)}) conditional(s32[]{:T(128)} %bitcast.2, () %tuple.29, (bf16[1,1,320,3072]{3,2,1,0:T(8,128)(2,1)}) %tuple.34), branch_computations={%region_0.0_spmd, %region_1.0_spmd} | conditional | bytes 3932216 | solution.py:170
  21.4 2.2 %branch_1_fun.2 = (bf16[8,80,768]{2,1,0:T(8,128)(2,1)S(1)}, bf16[8,80,768]{2,1,0:T(8,128)(2,1)S(1)}) custom-call(bf16[320,3072]{1,0:T(8,128)(2,1)} %bitcast.17), custom_call_target="tpu_custom_call" | custom-call | tf_op jit(solution)/shard_map/cond/branch_1_fun/pallas_call | solution.py:182
  23.6 2.1 %collective-permute-start = (bf16[8,80,768]{2,1,0:T(8,128)(2,1)S(1)}, bf16[8,80,768]{2,1,0:T(8,128)(2,1)}, u32[]{:S(2)}, u32[]{:S(2)}) collective-permute-start(bf16[8,80,768]{2,1,0:T(8,128)(2,1)S(1)} %get-tuple-element.10), channel_id=1, source_target_pairs={{0,1},{1,0},{2,3},{3,2},{4,5},{5,4},{6,7},{7,6},{8,9},{9,8},{10,11... | collective-permute-start | bytes 2949128 | tf_op jit(solution)/shard_map/cond/branch_1_fun/ppermute | solution.py:187
  25.7 2.5 %collective-permute-done = bf16[8,80,768]{2,1,0:T(8,128)(2,1)} collective-permute-done((bf16[8,80,768]{2,1,0:T(8,128)(2,1)S(1)}, bf16[8,80,768]{2,1,0:T(8,128)(2,1)}, u32[]{:S(2)}, u32[]{:S(2)}) %collective-permute-start) | collective-permute-done | bytes 983072 | tf_op jit(solution)/shard_map/cond/branch_1_fun/ppermute | solution.py:187
  29.3 7.3 %all-to-all-start.1 = ((f32[16,1,3072]{2,1,0:T(1,128)}), f32[16,1,3072]{2,1,0:T(1,128)S(1)}, u32[]{:S(2)}, u32[]{:S(2)}) async-start(f32[16,1,3072]{2,1,0:T(1,128)} %get-tuple-element.33), calls=%async_computation.1 | async-start | bytes 393216 | tf_op jit(solution)/shard_map/all_to_all | solution.py:209
  36.6 2.6 %shard_map.81 = bf16[16,80,768]{2,1,0:T(8,128)(2,1)} custom-call(bf16[8,80,768]{2,1,0:T(8,128)(2,1)S(1)} %get-tuple-element.31.kept_ref, bf16[8,80,768]{2,1,0:T(8,128)(2,1)} %get-tuple-element.32.got_ref), custom_call_target="tpu_custom_call" | custom-call | tf_op jit(solution)/shard_map/pallas_call | solution.py:211
  39.2 7.7 %all-to-all-done.1.parts_ref = f32[16,1,3072]{2,1,0:T(1,128)S(1)} async-done(((f32[16,1,3072]{2,1,0:T(1,128)}), f32[16,1,3072]{2,1,0:T(1,128)S(1)}, u32[]{:S(2)}, u32[]{:S(2)}) %all-to-all-start.1) | async-done | bytes 196640 | tf_op jit(solution)/shard_map/all_to_all | solution.py:209
  47.0 3.7 %all-to-all-start.2 = ((bf16[16,80,768]{2,1,0:T(8,128)(2,1)}), bf16[16,80,768]{2,1,0:T(8,128)(2,1)S(1)}, u32[]{:S(2)}, u32[]{:S(2)}) async-start(bf16[16,80,768]{2,1,0:T(8,128)(2,1)} %shard_map.81), calls=%async_computation.2 | async-start | bytes 3932160 | tf_op jit(solution)/shard_map/all_to_all | solution.py:218
  50.7 38.7 %conditional.3 = (bf16[256,400]{1,0:T(8,128)(2,1)S(1)}, f32[1,3072]{1,0:T(1,128)S(1)}) conditional(s32[]{:T(128)} %bitcast.2, () %tuple.28, (f32[128,8]{1,0:T(8,128)S(1)}, bf16[16,128]{1,0:T(8,128)(2,1)S(1)}, f32[1,1,3072]{2,1,0:T(1,128)S(1)}) %tuple.32), branch_computations={%region_2.0_spmd, %region_3.0_spmd} | conditional | flops 18432 | bytes 516352 | solution.py:170
  50.7 1.9 %collective-permute-start.1 = (f32[1,1,3072]{2,1,0:T(1,128)S(1)}, f32[1,1,3072]{2,1,0:T(1,128)S(1)}, u32[]{:S(2)}, u32[]{:S(2)}) collective-permute-start(f32[1,1,3072]{2,1,0:T(1,128)S(1)} %get-tuple-element.13), channel_id=1, source_target_pairs={{0,16},{16,0},{32,48},{48,32},{64,80},{80,64},{96,112},{112,96},{1... | collective-permute-start | bytes 36872 | tf_op jit(solution)/shard_map/cond/branch_1_fun/ppermute | solution.py:230
  52.6 2.8 %collective-permute-done.1 = f32[1,1,3072]{2,1,0:T(1,128)S(1)} collective-permute-done((f32[1,1,3072]{2,1,0:T(1,128)S(1)}, f32[1,1,3072]{2,1,0:T(1,128)S(1)}, u32[]{:S(2)}, u32[]{:S(2)}) %collective-permute-start.1) | collective-permute-done | bytes 12320 | tf_op jit(solution)/shard_map/cond/branch_1_fun/ppermute | solution.py:230
  55.5 1.9 %collective-permute-start.2 = (f32[1,1,3072]{2,1,0:T(1,128)S(1)}, f32[1,1,3072]{2,1,0:T(1,128)S(1)}, u32[]{:S(2)}, u32[]{:S(2)}) collective-permute-start(f32[1,1,3072]{2,1,0:T(1,128)S(1)} %add.12), channel_id=1, source_target_pairs={{0,32},{16,48},{32,0},{48,16},{64,96},{80,112},{96,64},{112,80},{1... | collective-permute-start | bytes 36872 | tf_op jit(solution)/shard_map/cond/branch_1_fun/ppermute | solution.py:230
  57.4 3.7 %collective-permute-done.2 = f32[1,1,3072]{2,1,0:T(1,128)S(1)} collective-permute-done((f32[1,1,3072]{2,1,0:T(1,128)S(1)}, f32[1,1,3072]{2,1,0:T(1,128)S(1)}, u32[]{:S(2)}, u32[]{:S(2)}) %collective-permute-start.2) | collective-permute-done | bytes 12320 | tf_op jit(solution)/shard_map/cond/branch_1_fun/ppermute | solution.py:230
  61.1 8.1 %collective-permute-start.3 = (f32[1,1,3072]{2,1,0:T(1,128)S(1)}, f32[1,1,3072]{2,1,0:T(1,128)S(1)}, u32[]{:S(2)}, u32[]{:S(2)}) collective-permute-start(f32[1,1,3072]{2,1,0:T(1,128)S(1)} %add.13), channel_id=1, source_target_pairs={{0,64},{16,80},{32,96},{48,112},{64,0},{80,16},{96,32},{112,48},{1... | collective-permute-start | bytes 36872 | tf_op jit(solution)/shard_map/cond/branch_1_fun/ppermute | solution.py:230
  70.4 3.1 %collective-permute-start.4 = (f32[1,1,3072]{2,1,0:T(1,128)S(1)}, f32[1,1,3072]{2,1,0:T(1,128)S(1)}, u32[]{:S(2)}, u32[]{:S(2)}) collective-permute-start(f32[1,1,3072]{2,1,0:T(1,128)S(1)} %add.14), channel_id=1, source_target_pairs={{0,128},{16,144},{32,160},{48,176},{64,192},{80,208},{96,224},{112... | collective-permute-start | bytes 36872 | tf_op jit(solution)/shard_map/cond/branch_1_fun/ppermute | solution.py:230
  73.5 1.6 %collective-permute-done.4 = f32[1,1,3072]{2,1,0:T(1,128)S(1)} collective-permute-done((f32[1,1,3072]{2,1,0:T(1,128)S(1)}, f32[1,1,3072]{2,1,0:T(1,128)S(1)}, u32[]{:S(2)}, u32[]{:S(2)}) %collective-permute-start.4) | collective-permute-done | bytes 12320 | tf_op jit(solution)/shard_map/cond/branch_1_fun/ppermute | solution.py:230
  75.1 4.1 %collective-permute-start.5 = (f32[1,1,3072]{2,1,0:T(1,128)S(1)}, f32[1,1,3072]{2,1,0:T(1,128)S(1)}, u32[]{:S(2)}, u32[]{:S(2)}) collective-permute-start(f32[1,1,3072]{2,1,0:T(1,128)S(1)} %add.15), channel_id=1, source_target_pairs={{0,256},{16,272},{32,288},{48,304},{64,320},{80,336},{96,352},{112... | collective-permute-start | bytes 36872 | tf_op jit(solution)/shard_map/cond/branch_1_fun/ppermute | solution.py:230
  79.2 1.6 %collective-permute-done.5 = f32[1,1,3072]{2,1,0:T(1,128)S(1)} collective-permute-done((f32[1,1,3072]{2,1,0:T(1,128)S(1)}, f32[1,1,3072]{2,1,0:T(1,128)S(1)}, u32[]{:S(2)}, u32[]{:S(2)}) %collective-permute-start.5) | collective-permute-done | bytes 12320 | tf_op jit(solution)/shard_map/cond/branch_1_fun/ppermute | solution.py:230
  80.8 6.8 %collective-permute-start.6 = (f32[1,1,3072]{2,1,0:T(1,128)S(1)}, f32[1,1,3072]{2,1,0:T(1,128)S(1)}, u32[]{:S(2)}, u32[]{:S(2)}) collective-permute-start(f32[1,1,3072]{2,1,0:T(1,128)S(1)} %add.16), channel_id=1, source_target_pairs={{0,512},{16,528},{32,544},{48,560},{64,576},{80,592},{96,608},{112... | collective-permute-start | bytes 36872 | tf_op jit(solution)/shard_map/cond/branch_1_fun/ppermute | solution.py:230
  87.8 1.6 %collective-permute-done.6 = f32[1,1,3072]{2,1,0:T(1,128)S(1)} collective-permute-done((f32[1,1,3072]{2,1,0:T(1,128)S(1)}, f32[1,1,3072]{2,1,0:T(1,128)S(1)}, u32[]{:S(2)}, u32[]{:S(2)}) %collective-permute-start.6) | collective-permute-done | bytes 12320 | tf_op jit(solution)/shard_map/cond/branch_1_fun/ppermute | solution.py:230
  89.4 10.2 %all-to-all-done.2.refs_2_ = bf16[16,80,768]{2,1,0:T(8,128)(2,1)S(1)} async-done(((bf16[16,80,768]{2,1,0:T(8,128)(2,1)}), bf16[16,80,768]{2,1,0:T(8,128)(2,1)S(1)}, u32[]{:S(2)}, u32[]{:S(2)}) %all-to-all-start.2) | async-done | bytes 1966112 | tf_op jit(solution)/shard_map/all_to_all | solution.py:218
  99.6 1.7 %shard_map.83 = bf16[128,3072]{1,0:T(8,128)(2,1)} custom-call(bf16[256,400]{1,0:T(8,128)(2,1)S(1)} %get-tuple-element.35.refs_0_, bf16[16,3072]{1,0:T(8,128)(2,1)S(1)} %copy-done.1, bf16[16,80,768]{2,1,0:T(8,128)(2,1)S(1)} %all-to-all-done.2.refs_2_), custom_call_target="tpu_custom_call" | custom-call | tf_op jit(solution)/shard_map/pallas_call | solution.py:235
  (24 shorter events, 4.0 us)
Async XLA Ops:
  0.6 0.7 copy-start.3
  2.1 26.1 %all-to-all-start = ((f32[16,1,128]{2,1,0:T(1,128)}), f32[16,1,128]{2,1,0:T(1,128)S(1)}, u32[]{:S(2)}, u32[]{:S(2)}) async-start(f32[16,1,128]{2,1,0:T(1,128)} %shard_map.79), calls=%async_computation | async-start | bytes 16384 | tf_op jit(solution)/shard_map/all_to_all | solution.py:177
  21.4 6.8 %copy-start = (bf16[1,128,3072]{2,1,0:T(8,128)(2,1)S(1)}, bf16[1,128,3072]{2,1,0:T(8,128)(2,1)}, u32[]{:S(2)}) copy-start(bf16[1,128,3072]{2,1,0:T(8,128)(2,1)} %param.10) | copy-start | bytes 2359300
  21.4 6.8 %copy-start.2 = (f32[1,128,16]{1,2,0:T(8,128)S(1)}, f32[1,128,16]{1,2,0:T(8,128)}, u32[]{:S(2)}) copy-start(f32[1,128,16]{1,2,0:T(8,128)} %param.12) | copy-start | bytes 24580
  21.4 6.8 %copy-start.4 = (s32[1,128,2]{1,2,0:T(2,128)S(1)}, s32[1,128,2]{1,2,0:T(2,128)}, u32[]{:S(2)}) copy-start(s32[1,128,2]{1,2,0:T(2,128)} %param.11) | copy-start | bytes 3076
  23.6 4.6 %collective-permute-start = (bf16[8,80,768]{2,1,0:T(8,128)(2,1)S(1)}, bf16[8,80,768]{2,1,0:T(8,128)(2,1)}, u32[]{:S(2)}, u32[]{:S(2)}) collective-permute-start(bf16[8,80,768]{2,1,0:T(8,128)(2,1)S(1)} %get-tuple-element.10), channel_id=1, source_target_pairs={{0,1},{1,0},{2,3},{3,2},{4,5},{5,4},{6,7},{7,6},{8,9},{9,8},{10,11... | collective-permute-start | bytes 2949128 | tf_op jit(solution)/shard_map/cond/branch_1_fun/ppermute | solution.py:187
  29.3 17.6 %all-to-all-start.1 = ((f32[16,1,3072]{2,1,0:T(1,128)}), f32[16,1,3072]{2,1,0:T(1,128)S(1)}, u32[]{:S(2)}, u32[]{:S(2)}) async-start(f32[16,1,3072]{2,1,0:T(1,128)} %get-tuple-element.33), calls=%async_computation.1 | async-start | bytes 393216 | tf_op jit(solution)/shard_map/all_to_all | solution.py:209
  46.9 52.7 %copy-start.1 = (bf16[16,3072]{1,0:T(8,128)(2,1)S(1)}, bf16[16,3072]{1,0:T(8,128)(2,1)}, u32[]{:S(2)}) copy-start(bf16[16,3072]{1,0:T(8,128)(2,1)} %refs_1_.1) | copy-start | bytes 294916
  47.0 52.7 %all-to-all-start.2 = ((bf16[16,80,768]{2,1,0:T(8,128)(2,1)}), bf16[16,80,768]{2,1,0:T(8,128)(2,1)S(1)}, u32[]{:S(2)}, u32[]{:S(2)}) async-start(bf16[16,80,768]{2,1,0:T(8,128)(2,1)} %shard_map.81), calls=%async_computation.2 | async-start | bytes 3932160 | tf_op jit(solution)/shard_map/all_to_all | solution.py:218
  50.7 4.7 %collective-permute-start.1 = (f32[1,1,3072]{2,1,0:T(1,128)S(1)}, f32[1,1,3072]{2,1,0:T(1,128)S(1)}, u32[]{:S(2)}, u32[]{:S(2)}) collective-permute-start(f32[1,1,3072]{2,1,0:T(1,128)S(1)} %get-tuple-element.13), channel_id=1, source_target_pairs={{0,16},{16,0},{32,48},{48,32},{64,80},{80,64},{96,112},{112,96},{1... | collective-permute-start | bytes 36872 | tf_op jit(solution)/shard_map/cond/branch_1_fun/ppermute | solution.py:230
  55.5 5.6 %collective-permute-start.2 = (f32[1,1,3072]{2,1,0:T(1,128)S(1)}, f32[1,1,3072]{2,1,0:T(1,128)S(1)}, u32[]{:S(2)}, u32[]{:S(2)}) collective-permute-start(f32[1,1,3072]{2,1,0:T(1,128)S(1)} %add.12), channel_id=1, source_target_pairs={{0,32},{16,48},{32,0},{48,16},{64,96},{80,112},{96,64},{112,80},{1... | collective-permute-start | bytes 36872 | tf_op jit(solution)/shard_map/cond/branch_1_fun/ppermute | solution.py:230
  61.1 9.2 %collective-permute-start.3 = (f32[1,1,3072]{2,1,0:T(1,128)S(1)}, f32[1,1,3072]{2,1,0:T(1,128)S(1)}, u32[]{:S(2)}, u32[]{:S(2)}) collective-permute-start(f32[1,1,3072]{2,1,0:T(1,128)S(1)} %add.13), channel_id=1, source_target_pairs={{0,64},{16,80},{32,96},{48,112},{64,0},{80,16},{96,32},{112,48},{1... | collective-permute-start | bytes 36872 | tf_op jit(solution)/shard_map/cond/branch_1_fun/ppermute | solution.py:230
  70.4 4.7 %collective-permute-start.4 = (f32[1,1,3072]{2,1,0:T(1,128)S(1)}, f32[1,1,3072]{2,1,0:T(1,128)S(1)}, u32[]{:S(2)}, u32[]{:S(2)}) collective-permute-start(f32[1,1,3072]{2,1,0:T(1,128)S(1)} %add.14), channel_id=1, source_target_pairs={{0,128},{16,144},{32,160},{48,176},{64,192},{80,208},{96,224},{112... | collective-permute-start | bytes 36872 | tf_op jit(solution)/shard_map/cond/branch_1_fun/ppermute | solution.py:230
  75.1 5.6 %collective-permute-start.5 = (f32[1,1,3072]{2,1,0:T(1,128)S(1)}, f32[1,1,3072]{2,1,0:T(1,128)S(1)}, u32[]{:S(2)}, u32[]{:S(2)}) collective-permute-start(f32[1,1,3072]{2,1,0:T(1,128)S(1)} %add.15), channel_id=1, source_target_pairs={{0,256},{16,272},{32,288},{48,304},{64,320},{80,336},{96,352},{112... | collective-permute-start | bytes 36872 | tf_op jit(solution)/shard_map/cond/branch_1_fun/ppermute | solution.py:230
  80.8 8.6 %collective-permute-start.6 = (f32[1,1,3072]{2,1,0:T(1,128)S(1)}, f32[1,1,3072]{2,1,0:T(1,128)S(1)}, u32[]{:S(2)}, u32[]{:S(2)}) collective-permute-start(f32[1,1,3072]{2,1,0:T(1,128)S(1)} %add.16), channel_id=1, source_target_pairs={{0,512},{16,528},{32,544},{48,560},{64,576},{80,592},{96,608},{112... | collective-permute-start | bytes 36872 | tf_op jit(solution)/shard_map/cond/branch_1_fun/ppermute | solution.py:230
  89.4 11.9 %copy-start.5 = (f32[1,3072]{1,0:T(1,128)}, f32[1,3072]{1,0:T(1,128)S(1)}, u32[]{:S(2)}) copy-start(f32[1,3072]{1,0:T(1,128)S(1)} %get-tuple-element.26) | copy-start | bytes 36868

commit v11 on v10

--- a/solution.py
+++ b/solution.py
@@ -51,9 +51,10 @@
 
 
 def deal_kernel(kept_ref, got_ref, out_ref):
+    stack = kept_ref.shape[1]
     for chip in range(kept_ref.shape[0]):
-        out_ref[2 * chip] = kept_ref[chip]
-        out_ref[2 * chip + 1] = got_ref[chip]
+        out_ref[chip, :stack, :] = kept_ref[chip]
+        out_ref[chip, stack:, :] = got_ref[chip]
 
 
 def sum_kernel(parts_ref, out_ref):
@@ -199,6 +200,13 @@
         ),
         compiler_params=params,
     )(ids, probs, dots, layer_input[0])
+    dealt = pl.pallas_call(
+        deal_kernel,
+        out_shape=jax.ShapeDtypeStruct((windows // 2, 2 * stack, part), jnp.bfloat16),
+        compiler_params=params,
+    )(kept, got)
+    term, dealt = lax.optimization_barrier((term, dealt))
+
     def add(parts, count):
         return pl.pallas_call(
             sum_kernel,
@@ -208,14 +216,10 @@
 
     own = add(lax.all_to_all(term, "exp", 0, 0, tiled=True), 1)
 
-    dealt = pl.pallas_call(
-        deal_kernel,
-        out_shape=jax.ShapeDtypeStruct((windows, stack, part), jnp.bfloat16),
-        compiler_params=params,
-    )(kept, got)
     dealt, own = lax.optimization_barrier((dealt, own))
     cores = [[i for i in range(windows) if i % 2 == core] for core in range(2)]
     copies = lax.all_to_all(dealt, "exp", 0, 0, axis_index_groups=cores, tiled=True)
+    copies = copies.reshape(windows, stack, part)
 
     def over_ctx(operand):
         own, place, logit = operand

time: 102 us -> 104 us (1.020)
  blocking collectives: 0 us -> 17.4 us
  waiting for transfers between devices: 32.7 us -> 25 us
  starting transfers between devices: 56.6 us -> 49.3 us
    all_to_all x0 -> x1, blocking collectives: none -> 17.4 us  [shards(): own = add(lax.all_to_all(term, 'exp', 0, 0, tiled=True), 1)]
    all_to_all x1 -> x0, waiting for transfers between devices: 7.71 us -> none  [shards(): own = add(lax.all_to_all(term, 'exp', 0, 0, tiled=True), 1)]
    all_to_all x1 -> x0, starting transfers between devices: 7.27 us -> none  [shards(): own = add(lax.all_to_all(term, 'exp', 0, 0, tiled=True), 1)]
  transfers between devices with their start and end apart: 10 -> 9, of which waited for: 9 -> 8; matrix products, arithmetic and copies ran while one was open for 1% -> 1% of each run, Pallas kernels for 5% -> 2%
where the time goes in v11:
time: 104 us; the launch traced here: 103 us
  starting transfers between devices  49.3 us (47%)
  waiting for transfers between devices  25 us (24%)
  blocking collectives  17.4 us (17%)
  Pallas kernels  7.95 us (8%)
  local copies, waits for them, and re-layouts  1.89 us (2%)
  between operations  1.36 us (1%)
    ppermute x6, starting transfers between devices, over_ctx(): own = own + lax.ppermute(own, 'ctx', moves)  26 us
    all_to_all x1, starting transfers between devices, shards(): dots = lax.all_to_all(laid, 'exp', 0, 0, tiled=True)  17.4 us
    all_to_all x1, blocking collectives, shards(): own = add(lax.all_to_all(term, 'exp', 0, 0, tiled=True), 1)  17.4 us
    ppermute x6, waiting for transfers between devices, over_ctx(): own = own + lax.ppermute(own, 'ctx', moves)  12.4 us
    all_to_all x1, waiting for transfers between devices, shards(): lax.all_to_all(dealt, 'exp', 0, 0, axis_index_groups=cores, tiled=True)  10.2 us
    all_to_all x1, starting transfers between devices, shards(): lax.all_to_all(dealt, 'exp', 0, 0, axis_index_groups=cores, tiled=True)  3.74 us
    pallas_call x1, Pallas kernels, shards(): pl.pallas_call(deal_kernel, out_shape=jax.ShapeDtypeStruct((windows // 2,...  2.7 us
    ppermute x1, waiting for transfers between devices, share(): lax.ppermute(given, 'exp', [(i, i ^ 1) for i in range(windows)])  2.45 us
  transfers between devices with their start and end apart: 9, of which 8 were waited for; matrix products, arithmetic and copies ran while one was open for 1% of the time, Pallas kernels for 2%

profile of v11, /device:TPU:1, one launch (start us, length us, event | category | flops | bytes accessed | tf_op | source)
XLA Modules:
  0.0 103.1 jit_solution(7126710179408652859)
XLA Ops:
  2.1 17.4 %all-to-all-start = ((f32[16,1,128]{2,1,0:T(1,128)}), f32[16,1,128]{2,1,0:T(1,128)S(1)}, u32[]{:S(2)}, u32[]{:S(2)}) async-start(f32[16,1,128]{2,1,0:T(1,128)} %shard_map.79), calls=%async_computation | async-start | bytes 16384 | tf_op jit(solution)/shard_map/all_to_all | solution.py:178
  19.5 1.2 %slice.3 = s32[1,1,1]{1,2,0:T(1,128)} slice(s32[1,128,2]{1,2,0:T(2,128)} %param.11), slice={[0:1], [0:1], [0:1]} | slice | bytes 8 | tf_op jit(solution)/shard_map/slice | solution.py:166
  21.4 6.7 %conditional.2 = (bf16[8,80,768]{2,1,0:T(8,128)(2,1)S(1)}, bf16[8,80,768]{2,1,0:T(8,128)(2,1)}) conditional(s32[]{:T(128)} %bitcast.2, () %tuple.30, (bf16[1,1,320,3072]{3,2,1,0:T(8,128)(2,1)}) %tuple.36), branch_computations={%region_0.0_spmd, %region_1.0_spmd} | conditional | bytes 3932216 | solution.py:171
  21.4 2.1 %branch_1_fun.2 = (bf16[8,80,768]{2,1,0:T(8,128)(2,1)S(1)}, bf16[8,80,768]{2,1,0:T(8,128)(2,1)S(1)}) custom-call(bf16[320,3072]{1,0:T(8,128)(2,1)} %bitcast.19), custom_call_target="tpu_custom_call" | custom-call | tf_op jit(solution)/shard_map/cond/branch_1_fun/pallas_call | solution.py:183
  23.5 2.1 %collective-permute-start = (bf16[8,80,768]{2,1,0:T(8,128)(2,1)S(1)}, bf16[8,80,768]{2,1,0:T(8,128)(2,1)}, u32[]{:S(2)}, u32[]{:S(2)}) collective-permute-start(bf16[8,80,768]{2,1,0:T(8,128)(2,1)S(1)} %get-tuple-element.10), channel_id=1, source_target_pairs={{0,1},{1,0},{2,3},{3,2},{4,5},{5,4},{6,7},{7,6},{8,9},{9,8},{10,11... | collective-permute-start | bytes 2949128 | tf_op jit(solution)/shard_map/cond/branch_1_fun/ppermute | solution.py:188
  25.6 2.5 %collective-permute-done = bf16[8,80,768]{2,1,0:T(8,128)(2,1)} collective-permute-done((bf16[8,80,768]{2,1,0:T(8,128)(2,1)S(1)}, bf16[8,80,768]{2,1,0:T(8,128)(2,1)}, u32[]{:S(2)}, u32[]{:S(2)}) %collective-permute-start) | collective-permute-done | bytes 983072 | tf_op jit(solution)/shard_map/cond/branch_1_fun/ppermute | solution.py:188
  28.1 2.7 %shard_map.81 = bf16[8,160,768]{2,1,0:T(8,128)(2,1)} custom-call(bf16[8,80,768]{2,1,0:T(8,128)(2,1)S(1)} %get-tuple-element.34.kept_ref, bf16[8,80,768]{2,1,0:T(8,128)(2,1)} %get-tuple-element.35.got_ref), custom_call_target="tpu_custom_call" | custom-call | tf_op jit(solution)/shard_map/pallas_call | solution.py:203
  31.3 17.4 %all_to_all.15.parts_ref = f32[16,1,3072]{2,1,0:T(1,128)S(1)} all-to-all(f32[16,1,3072]{2,1,0:T(1,128)S(1)} %get-tuple-element.37), channel_id=1, replica_groups=mesh['ctx'=64,'exp'=16] {'exp'}, dimensions={0} | all-to-all | bytes 393216 | tf_op jit(solution)/shard_map/all_to_all | solution.py:217
  48.7 3.7 %all-to-all-start.2 = ((bf16[8,160,768]{2,1,0:T(8,128)(2,1)}), bf16[8,160,768]{2,1,0:T(8,128)(2,1)S(1)}, u32[]{:S(2)}, u32[]{:S(2)}) async-start(bf16[8,160,768]{2,1,0:T(8,128)(2,1)} %shard_map.81), calls=%async_computation.2 | async-start | bytes 3932160 | tf_op jit(solution)/shard_map/all_to_all | solution.py:221
  52.4 38.7 %conditional.3 = (bf16[256,400]{1,0:T(8,128)(2,1)S(1)}, f32[1,3072]{1,0:T(1,128)S(1)}) conditional(s32[]{:T(128)} %bitcast.2, () %tuple.29, (f32[128,8]{1,0:T(8,128)S(1)}, bf16[16,128]{1,0:T(8,128)(2,1)S(1)}, f32[1,1,3072]{2,1,0:T(1,128)S(1)}) %tuple.34), branch_computations={%region_2.0_spmd, %region_3.0_spmd} | conditional | flops 18432 | bytes 516352 | solution.py:171
  52.5 1.9 %collective-permute-start.1 = (f32[1,1,3072]{2,1,0:T(1,128)S(1)}, f32[1,1,3072]{2,1,0:T(1,128)S(1)}, u32[]{:S(2)}, u32[]{:S(2)}) collective-permute-start(f32[1,1,3072]{2,1,0:T(1,128)S(1)} %get-tuple-element.13), channel_id=1, source_target_pairs={{0,16},{16,0},{32,48},{48,32},{64,80},{80,64},{96,112},{112,96},{1... | collective-permute-start | bytes 36872 | tf_op jit(solution)/shard_map/cond/branch_1_fun/ppermute | solution.py:234
  54.4 2.8 %collective-permute-done.1 = f32[1,1,3072]{2,1,0:T(1,128)S(1)} collective-permute-done((f32[1,1,3072]{2,1,0:T(1,128)S(1)}, f32[1,1,3072]{2,1,0:T(1,128)S(1)}, u32[]{:S(2)}, u32[]{:S(2)}) %collective-permute-start.1) | collective-permute-done | bytes 12320 | tf_op jit(solution)/shard_map/cond/branch_1_fun/ppermute | solution.py:234
  57.2 1.9 %collective-permute-start.2 = (f32[1,1,3072]{2,1,0:T(1,128)S(1)}, f32[1,1,3072]{2,1,0:T(1,128)S(1)}, u32[]{:S(2)}, u32[]{:S(2)}) collective-permute-start(f32[1,1,3072]{2,1,0:T(1,128)S(1)} %add.12), channel_id=1, source_target_pairs={{0,32},{16,48},{32,0},{48,16},{64,96},{80,112},{96,64},{112,80},{1... | collective-permute-start | bytes 36872 | tf_op jit(solution)/shard_map/cond/branch_1_fun/ppermute | solution.py:234
  59.1 3.7 %collective-permute-done.2 = f32[1,1,3072]{2,1,0:T(1,128)S(1)} collective-permute-done((f32[1,1,3072]{2,1,0:T(1,128)S(1)}, f32[1,1,3072]{2,1,0:T(1,128)S(1)}, u32[]{:S(2)}, u32[]{:S(2)}) %collective-permute-start.2) | collective-permute-done | bytes 12320 | tf_op jit(solution)/shard_map/cond/branch_1_fun/ppermute | solution.py:234
  62.9 8.1 %collective-permute-start.3 = (f32[1,1,3072]{2,1,0:T(1,128)S(1)}, f32[1,1,3072]{2,1,0:T(1,128)S(1)}, u32[]{:S(2)}, u32[]{:S(2)}) collective-permute-start(f32[1,1,3072]{2,1,0:T(1,128)S(1)} %add.13), channel_id=1, source_target_pairs={{0,64},{16,80},{32,96},{48,112},{64,0},{80,16},{96,32},{112,48},{1... | collective-permute-start | bytes 36872 | tf_op jit(solution)/shard_map/cond/branch_1_fun/ppermute | solution.py:234
  71.0 1.1 %collective-permute-done.3 = f32[1,1,3072]{2,1,0:T(1,128)S(1)} collective-permute-done((f32[1,1,3072]{2,1,0:T(1,128)S(1)}, f32[1,1,3072]{2,1,0:T(1,128)S(1)}, u32[]{:S(2)}, u32[]{:S(2)}) %collective-permute-start.3) | collective-permute-done | bytes 12320 | tf_op jit(solution)/shard_map/cond/branch_1_fun/ppermute | solution.py:234
  72.1 3.1 %collective-permute-start.4 = (f32[1,1,3072]{2,1,0:T(1,128)S(1)}, f32[1,1,3072]{2,1,0:T(1,128)S(1)}, u32[]{:S(2)}, u32[]{:S(2)}) collective-permute-start(f32[1,1,3072]{2,1,0:T(1,128)S(1)} %add.14), channel_id=1, source_target_pairs={{0,128},{16,144},{32,160},{48,176},{64,192},{80,208},{96,224},{112... | collective-permute-start | bytes 36872 | tf_op jit(solution)/shard_map/cond/branch_1_fun/ppermute | solution.py:234
  75.2 1.6 %collective-permute-done.4 = f32[1,1,3072]{2,1,0:T(1,128)S(1)} collective-permute-done((f32[1,1,3072]{2,1,0:T(1,128)S(1)}, f32[1,1,3072]{2,1,0:T(1,128)S(1)}, u32[]{:S(2)}, u32[]{:S(2)}) %collective-permute-start.4) | collective-permute-done | bytes 12320 | tf_op jit(solution)/shard_map/cond/branch_1_fun/ppermute | solution.py:234
  76.8 4.1 %collective-permute-start.5 = (f32[1,1,3072]{2,1,0:T(1,128)S(1)}, f32[1,1,3072]{2,1,0:T(1,128)S(1)}, u32[]{:S(2)}, u32[]{:S(2)}) collective-permute-start(f32[1,1,3072]{2,1,0:T(1,128)S(1)} %add.15), channel_id=1, source_target_pairs={{0,256},{16,272},{32,288},{48,304},{64,320},{80,336},{96,352},{112... | collective-permute-start | bytes 36872 | tf_op jit(solution)/shard_map/cond/branch_1_fun/ppermute | solution.py:234
  80.9 1.6 %collective-permute-done.5 = f32[1,1,3072]{2,1,0:T(1,128)S(1)} collective-permute-done((f32[1,1,3072]{2,1,0:T(1,128)S(1)}, f32[1,1,3072]{2,1,0:T(1,128)S(1)}, u32[]{:S(2)}, u32[]{:S(2)}) %collective-permute-start.5) | collective-permute-done | bytes 12320 | tf_op jit(solution)/shard_map/cond/branch_1_fun/ppermute | solution.py:234
  82.5 6.8 %collective-permute-start.6 = (f32[1,1,3072]{2,1,0:T(1,128)S(1)}, f32[1,1,3072]{2,1,0:T(1,128)S(1)}, u32[]{:S(2)}, u32[]{:S(2)}) collective-permute-start(f32[1,1,3072]{2,1,0:T(1,128)S(1)} %add.16), channel_id=1, source_target_pairs={{0,512},{16,528},{32,544},{48,560},{64,576},{80,592},{96,608},{112... | collective-permute-start | bytes 36872 | tf_op jit(solution)/shard_map/cond/branch_1_fun/ppermute | solution.py:234
  89.5 1.6 %collective-permute-done.6 = f32[1,1,3072]{2,1,0:T(1,128)S(1)} collective-permute-done((f32[1,1,3072]{2,1,0:T(1,128)S(1)}, f32[1,1,3072]{2,1,0:T(1,128)S(1)}, u32[]{:S(2)}, u32[]{:S(2)}) %collective-permute-start.6) | collective-permute-done | bytes 12320 | tf_op jit(solution)/shard_map/cond/branch_1_fun/ppermute | solution.py:234
  91.2 10.2 %all-to-all-done.2 = bf16[8,160,768]{2,1,0:T(8,128)(2,1)S(1)} async-done(((bf16[8,160,768]{2,1,0:T(8,128)(2,1)}), bf16[8,160,768]{2,1,0:T(8,128)(2,1)S(1)}, u32[]{:S(2)}, u32[]{:S(2)}) %all-to-all-start.2) | async-done | bytes 1966112 | tf_op jit(solution)/shard_map/all_to_all | solution.py:221
  101.4 1.7 %shard_map.83 = bf16[128,3072]{1,0:T(8,128)(2,1)} custom-call(bf16[256,400]{1,0:T(8,128)(2,1)S(1)} %get-tuple-element.39.refs_0_, bf16[16,3072]{1,0:T(8,128)(2,1)S(1)} %copy-done.1, bf16[16,80,768]{2,1,0:T(8,128)(2,1)S(1)} %bitcast.14), custom_call_target="tpu_custom_call" | custom-call | tf_op jit(solution)/shard_map/pallas_call | solution.py:239
  (23 shorter events, 2.2 us)
Async XLA Ops:
  0.6 0.7 copy-start.3
  2.1 26.0 %all-to-all-start = ((f32[16,1,128]{2,1,0:T(1,128)}), f32[16,1,128]{2,1,0:T(1,128)S(1)}, u32[]{:S(2)}, u32[]{:S(2)}) async-start(f32[16,1,128]{2,1,0:T(1,128)} %shard_map.79), calls=%async_computation | async-start | bytes 16384 | tf_op jit(solution)/shard_map/all_to_all | solution.py:178
  23.5 4.6 %collective-permute-start = (bf16[8,80,768]{2,1,0:T(8,128)(2,1)S(1)}, bf16[8,80,768]{2,1,0:T(8,128)(2,1)}, u32[]{:S(2)}, u32[]{:S(2)}) collective-permute-start(bf16[8,80,768]{2,1,0:T(8,128)(2,1)S(1)} %get-tuple-element.10), channel_id=1, source_target_pairs={{0,1},{1,0},{2,3},{3,2},{4,5},{5,4},{6,7},{7,6},{8,9},{9,8},{10,11... | collective-permute-start | bytes 2949128 | tf_op jit(solution)/shard_map/cond/branch_1_fun/ppermute | solution.py:188
  28.1 2.7 %copy-start = (bf16[1,128,3072]{2,1,0:T(8,128)(2,1)S(1)}, bf16[1,128,3072]{2,1,0:T(8,128)(2,1)}, u32[]{:S(2)}) copy-start(bf16[1,128,3072]{2,1,0:T(8,128)(2,1)} %param.10) | copy-start | bytes 2359300
  28.1 2.7 %copy-start.2 = (f32[1,128,16]{1,2,0:T(8,128)S(1)}, f32[1,128,16]{1,2,0:T(8,128)}, u32[]{:S(2)}) copy-start(f32[1,128,16]{1,2,0:T(8,128)} %param.12) | copy-start | bytes 24580
  28.1 2.7 %copy-start.4 = (s32[1,128,2]{1,2,0:T(2,128)S(1)}, s32[1,128,2]{1,2,0:T(2,128)}, u32[]{:S(2)}) copy-start(s32[1,128,2]{1,2,0:T(2,128)} %param.11) | copy-start | bytes 3076
  48.7 52.7 %copy-start.1 = (bf16[16,3072]{1,0:T(8,128)(2,1)S(1)}, bf16[16,3072]{1,0:T(8,128)(2,1)}, u32[]{:S(2)}) copy-start(bf16[16,3072]{1,0:T(8,128)(2,1)} %refs_1_.1) | copy-start | bytes 294916
  48.7 52.7 %all-to-all-start.2 = ((bf16[8,160,768]{2,1,0:T(8,128)(2,1)}), bf16[8,160,768]{2,1,0:T(8,128)(2,1)S(1)}, u32[]{:S(2)}, u32[]{:S(2)}) async-start(bf16[8,160,768]{2,1,0:T(8,128)(2,1)} %shard_map.81), calls=%async_computation.2 | async-start | bytes 3932160 | tf_op jit(solution)/shard_map/all_to_all | solution.py:221
  52.5 4.7 %collective-permute-start.1 = (f32[1,1,3072]{2,1,0:T(1,128)S(1)}, f32[1,1,3072]{2,1,0:T(1,128)S(1)}, u32[]{:S(2)}, u32[]{:S(2)}) collective-permute-start(f32[1,1,3072]{2,1,0:T(1,128)S(1)} %get-tuple-element.13), channel_id=1, source_target_pairs={{0,16},{16,0},{32,48},{48,32},{64,80},{80,64},{96,112},{112,96},{1... | collective-permute-start | bytes 36872 | tf_op jit(solution)/shard_map/cond/branch_1_fun/ppermute | solution.py:234
  57.2 5.6 %collective-permute-start.2 = (f32[1,1,3072]{2,1,0:T(1,128)S(1)}, f32[1,1,3072]{2,1,0:T(1,128)S(1)}, u32[]{:S(2)}, u32[]{:S(2)}) collective-permute-start(f32[1,1,3072]{2,1,0:T(1,128)S(1)} %add.12), channel_id=1, source_target_pairs={{0,32},{16,48},{32,0},{48,16},{64,96},{80,112},{96,64},{112,80},{1... | collective-permute-start | bytes 36872 | tf_op jit(solution)/shard_map/cond/branch_1_fun/ppermute | solution.py:234
  62.9 9.2 %collective-permute-start.3 = (f32[1,1,3072]{2,1,0:T(1,128)S(1)}, f32[1,1,3072]{2,1,0:T(1,128)S(1)}, u32[]{:S(2)}, u32[]{:S(2)}) collective-permute-start(f32[1,1,3072]{2,1,0:T(1,128)S(1)} %add.13), channel_id=1, source_target_pairs={{0,64},{16,80},{32,96},{48,112},{64,0},{80,16},{96,32},{112,48},{1... | collective-permute-start | bytes 36872 | tf_op jit(solution)/shard_map/cond/branch_1_fun/ppermute | solution.py:234
  72.1 4.7 %collective-permute-start.4 = (f32[1,1,3072]{2,1,0:T(1,128)S(1)}, f32[1,1,3072]{2,1,0:T(1,128)S(1)}, u32[]{:S(2)}, u32[]{:S(2)}) collective-permute-start(f32[1,1,3072]{2,1,0:T(1,128)S(1)} %add.14), channel_id=1, source_target_pairs={{0,128},{16,144},{32,160},{48,176},{64,192},{80,208},{96,224},{112... | collective-permute-start | bytes 36872 | tf_op jit(solution)/shard_map/cond/branch_1_fun/ppermute | solution.py:234
  76.8 5.6 %collective-permute-start.5 = (f32[1,1,3072]{2,1,0:T(1,128)S(1)}, f32[1,1,3072]{2,1,0:T(1,128)S(1)}, u32[]{:S(2)}, u32[]{:S(2)}) collective-permute-start(f32[1,1,3072]{2,1,0:T(1,128)S(1)} %add.15), channel_id=1, source_target_pairs={{0,256},{16,272},{32,288},{48,304},{64,320},{80,336},{96,352},{112... | collective-permute-start | bytes 36872 | tf_op jit(solution)/shard_map/cond/branch_1_fun/ppermute | solution.py:234
  82.5 8.6 %collective-permute-start.6 = (f32[1,1,3072]{2,1,0:T(1,128)S(1)}, f32[1,1,3072]{2,1,0:T(1,128)S(1)}, u32[]{:S(2)}, u32[]{:S(2)}) collective-permute-start(f32[1,1,3072]{2,1,0:T(1,128)S(1)} %add.16), channel_id=1, source_target_pairs={{0,512},{16,528},{32,544},{48,560},{64,576},{80,592},{96,608},{112... | collective-permute-start | bytes 36872 | tf_op jit(solution)/shard_map/cond/branch_1_fun/ppermute | solution.py:234
  91.2 11.9 %copy-start.5 = (f32[1,3072]{1,0:T(1,128)}, f32[1,3072]{1,0:T(1,128)S(1)}, u32[]{:S(2)}) copy-start(f32[1,3072]{1,0:T(1,128)S(1)} %get-tuple-element.28) | copy-start | bytes 36868
